TPU v7x, 32 devices: a whole 2x2x4 slice. The times are simulated.
32 devices in a mesh: groups: 2 (over y), row: 4 (over x, core), col: 4 (over z).
Axes of the slice: x: 2, y: 2, z: 4, core: 2. Of those that a mesh axis runs over, the one named last changes fastest.
Arguments:
- latents: bfloat16 [2048, 3072], P(('groups', 'col'), 'row'), parts along dimension 0, may hold values from -400 to 400
- modulation: float32 [16, 2, 3072], P('groups', None, 'row'), parts along dimension 0, may hold values from -3 to 3
- sample_of: int32 [2048], P('groups'), parts along dimension 0, may hold values from 0 to 7, never falling along the last dimension, each value on 1 to 256 neighbouring positions
- timestep: int32 [16], P('groups'), parts along dimension 0, may hold values from 0 to 999
- reward: float32 [16], P('groups'), parts along dimension 0, may hold values from -4 to 4
- qkv_cotangent: bfloat16 [2048, 9216], P(('groups', 'row'), 'col'), parts along dimension 0, may hold values from -18 to 18
- mlp_cotangent: bfloat16 [2048, 12288], P(('groups', 'row'), 'col'), parts along dimension 0, may hold values from -18 to 18
- mlp_preact: bfloat16 [2048, 12288], P(('groups', 'row'), 'col'), parts along dimension 0, may hold values from -6 to 6
- w_qkv: bfloat16 [3072, 9216], P('row', 'col'), may hold values from -0.109375 to 0.109375
- w_mlp: bfloat16 [3072, 12288], P('row', 'col'), may hold values from -0.109375 to 0.109375
Outputs:
- latent_input_gradient: bfloat16 [2048, 3072], P(('groups', 'col'), 'row'), parts along dimension 0
- qkv_weight_grad: bfloat16 [6144, 9216], P(('groups', 'row'), 'col'), parts along dimension 0
- mlp_weight_grad: bfloat16 [6144, 12288], P(('groups', 'row'), 'col'), parts along dimension 0
There are 2 independent parts, one for each index of `groups`. A program takes and returns all parts, laid end to end along the dimension named above; an argument that names none is the same for every part. Nothing has to cross between parts.
Inputs may be any that keep to these rules, and one draw needn't show every extreme that they name: sample_of never falls along the tokens; each of the 8 samples has at least one token, and the longest has exactly 256.
All inputs are finite; a program needn't handle non-finite values.
Results may differ from a plain program's by a relative error of at most 0.012.
Values may be sent and summed in bfloat16 or wider, within the bound.
No kernel may reach another device: no remote copies, remote signals or barrier semaphores. Data moves between devices by JAX's collectives and lax.ppermute only.
A program may use at most 128 MiB of HBM per device.

v0:
```python
import math

import jax
import jax.numpy as jnp
from jax import lax
from jax.sharding import PartitionSpec as P

MODEL_WIDTH = 3072
TSTEPS = 1000


EPS = 1e-06
ROOT = math.sqrt(2.0 / math.pi)


def gelu_slope(value):
    inner = ROOT * (value + 0.044715 * value * value * value)
    tangent = jnp.tanh(inner)
    return 0.5 * (1.0 + tangent) + 0.5 * value * (1.0 - tangent * tangent) * ROOT * (
        1.0 + 3.0 * 0.044715 * value * value
    )


def over_tokens(left, right):
    return lax.dot_general(
        left, right, (((0,), (0,)), ((), ())), preferred_element_type=jnp.float32
    )


def against_weight(left, right):
    return lax.dot_general(
        left, right, (((1,), (1,)), ((), ())), preferred_element_type=jnp.float32
    )


def lookup(onehot, table):
    return lax.dot_general(
        onehot,
        table,
        (((0,), (0,)), ((), ())),
        precision=lax.Precision.HIGHEST,
        preferred_element_type=jnp.float32,
    )


def on_device(
    latents,
    modulation,
    sample_of,
    timestep,
    reward,
    qkv_cotangent,
    mlp_cotangent,
    mlp_preact,
    w_qkv,
    w_mlp,
):
    row_id = lax.axis_index("row")
    col_id = lax.axis_index("col")
    tok_col = latents.shape[0]
    tok_row = qkv_cotangent.shape[0]
    width_row = latents.shape[1]
    samples = reward.shape[0]
    sample_ids = jnp.arange(samples, dtype=jnp.int32)
    onehot = (sample_ids[:, None] == sample_of[None, :]).astype(jnp.float32)
    counts = jnp.sum(onehot, axis=1)
    levels = (jnp.arange(TSTEPS, dtype=jnp.float32) + 0.5) / TSTEPS
    table = 0.5 + 1.5 * levels * (2.0 - levels)
    level_hits = (timestep[:, None] == jnp.arange(TSTEPS, dtype=jnp.int32)[None, :]).astype(
        jnp.float32
    )
    step_weight = jnp.sum(level_hits * table[None, :], axis=1)
    omega_sample = reward * step_weight * lax.rsqrt(counts)
    omega_tokens = lookup(onehot, omega_sample[:, None])[:, 0]
    omega_rows = lax.dynamic_slice_in_dim(omega_tokens, row_id * tok_row, tok_row)[:, None]
    grad_q = (qkv_cotangent.astype(jnp.float32) * omega_rows).astype(jnp.bfloat16)
    grad_m = (
        mlp_cotangent.astype(jnp.float32) * gelu_slope(mlp_preact.astype(jnp.float32)) * omega_rows
    ).astype(jnp.bfloat16)
    mod_flat = modulation.reshape(samples, 2 * width_row)
    input_float_copy = latents.astype(jnp.float32)
    own_onehot = lax.dynamic_slice_in_dim(onehot, col_id * tok_col, tok_col, 1)
    own_mod = lookup(own_onehot, mod_flat)
    sample_offset = own_mod[:, :width_row]
    sample_scale_factor = 1.0 + own_mod[:, width_row:]
    total_sum, total_square = lax.psum(
        (jnp.sum(input_float_copy, axis=1), jnp.sum(input_float_copy * input_float_copy, axis=1)),
        "row",
    )
    feature_average = (total_sum / MODEL_WIDTH)[:, None]
    inverse_deviation = lax.rsqrt(
        (total_square / MODEL_WIDTH)[:, None] - feature_average * feature_average + EPS
    )
    centered_normalized = (input_float_copy - feature_average) * inverse_deviation
    norm_output = (centered_normalized * sample_scale_factor + sample_offset).astype(jnp.bfloat16)
    normed_all = lax.all_gather(norm_output, "col", axis=0, tiled=True)
    all_q, all_m = (
        lax.all_gather(grad_q, "row", axis=0, tiled=True),
        lax.all_gather(grad_m, "row", axis=0, tiled=True),
    )
    qkv_total = over_tokens(normed_all, all_q)
    mlp_total = over_tokens(normed_all, all_m)
    normed_grad = lax.psum_scatter(
        (against_weight(all_q, w_qkv) + against_weight(all_m, w_mlp)).astype(jnp.bfloat16),
        "col",
        scatter_dimension=0,
        tiled=True,
    ).astype(jnp.float32)
    incoming_gradient = normed_grad * sample_scale_factor
    first_moment_term, second_moment_term = lax.psum(
        (
            jnp.sum(incoming_gradient, axis=1),
            jnp.sum(incoming_gradient * centered_normalized, axis=1),
        ),
        "row",
    )
    latent_input_gradient = inverse_deviation * (
        incoming_gradient
        - (first_moment_term / MODEL_WIDTH)[:, None]
        - centered_normalized * (second_moment_term / MODEL_WIDTH)[:, None]
    )
    return (
        latent_input_gradient.astype(jnp.bfloat16),
        qkv_total.astype(jnp.bfloat16),
        mlp_total.astype(jnp.bfloat16),
    )


def solution(mesh):
    in_specs = (
        P(("groups", "col"), "row"),
        P("groups", None, "row"),
        P("groups"),
        P("groups"),
        P("groups"),
        P(("groups", "row"), "col"),
        P(("groups", "row"), "col"),
        P(("groups", "row"), "col"),
        P("row", "col"),
        P("row", "col"),
    )
    out_specs = (
        P(("groups", "col"), "row"),
        P(("groups", "row"), "col"),
        P(("groups", "row"), "col"),
    )
    return jax.shard_map(
        on_device, mesh=mesh, in_specs=in_specs, out_specs=out_specs, check_vma=False
    )
```

profile of v0, /device:TPU:0, one launch (start us, length us, event | category | flops | bytes accessed | tf_op | source)
XLA Modules:
  0.0 219.7 jit_solution(13876928323038361879)
XLA Ops:
  7.2 0.0 copy-start
  7.2 0.0 all-gather.4.cloned.1.call-start
  7.2 1.0 convert_reduce_fusion.1
  8.2 0.9 select_reduce_fusion
  9.1 0.8 fusion.22
  9.9 0.1 dynamic_slice.6
  10.0 2.5 %multiply_convert_fusion = bf16[256,2304]{1,0:T(8,128)(2,1)} fusion(bf16[256,2304]{1,0:T(8,128)(2,1)} %param.15, f32[256]{0:T(256)S(1)} %dynamic_slice.6), kind=kLoop, calls=%fused_computation.20 | loop fusion | flops 1769472 | bytes 2360320 | tf_op jit(solution)/shard_map/convert_element_type | solution.py:76
  12.6 0.0 all-gather.4.cloned.1.call-update
  12.6 0.0 all-gather.6.cloned.1.call-start
  12.6 4.6 %fusion.8 = bf16[256,3072]{1,0:T(8,128)(2,1)} fusion(bf16[256,3072]{1,0:T(8,128)(2,1)} %param.17, bf16[256,3072]{1,0:T(8,128)(2,1)} %param.16, f32[256]{0:T(256)S(1)} %dynamic_slice.6), kind=kLoop, calls=%fused_computation.17 | loop fusion | flops 17301504 | bytes 4719616 | tf_op jit(solution)/shard_map/convert_element_type | solution.py:79
  17.2 0.0 all-gather.6.cloned.1.call-update
  17.3 0.0 reduce-scatter.2.cloned.1.call-start
  17.3 35.6 %all-gather.4.cloned.1.call-done = bf16[1024,2304]{1,0:T(8,128)(2,1)} async-done(((bf16[256,2304]{1,0:T(8,128)(2,1)}), bf16[1024,2304]{1,0:T(8,128)(2,1)}) %all-gather.4.cloned.1.call-update) | async-done | bytes 4718608 | tf_op jit(solution)/shard_map/all_gather | solution.py:98
  52.9 0.0 copy-done
  52.9 7.8 %fusion.29 = f32[1024,768]{1,0:T(8,128)} fusion(bf16[1024,2304]{1,0:T(8,128)(2,1)} %all-gather.4.cloned.1.call-done, bf16[768,2304]{1,0:T(8,128)(2,1)S(1)} %copy-done), kind=kOutput, calls=%fused_computation.55 | convolution fusion | flops 3623878656 | bytes 11403264 | tf_op jit(solution)/shard_map/dot_general | solution.py:31
  60.7 0.0 copy-start.1
  60.7 40.7 %all-gather.6.cloned.1.call-done = bf16[1024,3072]{1,0:T(8,128)(2,1)} async-done(((bf16[256,3072]{1,0:T(8,128)(2,1)}), bf16[1024,3072]{1,0:T(8,128)(2,1)}) %all-gather.6.cloned.1.call-update) | async-done | bytes 6291472 | tf_op jit(solution)/shard_map/all_gather | solution.py:99
  101.4 10.0 %add_convert_fusion = bf16[1024,768]{1,0:T(8,128)(2,1)} fusion(f32[1024,768]{1,0:T(8,128)} %fusion.29, bf16[1024,3072]{1,0:T(8,128)(2,1)} %all-gather.6.cloned.1.call-done, bf16[768,3072]{1,0:T(8,128)(2,1)} %param.19), kind=kOutput, calls=%fused_computation.19 | convolution fusion | flops 4833411072 | bytes 15728640 | tf_op jit(solution)/shard_map/dot_general | solution.py:31
  111.4 0.0 reduce-scatter.2.cloned.1.call-update
  111.4 0.0 all-gather.8.cloned.1.call-start
  111.5 1.4 copy.13
  112.9 1.2 fusion.10
  114.1 6.5 %all-reduce.1 = (f32[256]{0:T(256)S(1)}, f32[256]{0:T(256)}) all-reduce(f32[256]{0:T(256)S(1)} %get-tuple-element.5, f32[256]{0:T(256)S(1)} %get-tuple-element.6), channel_id=1, replica_groups=mesh['groups'=2,'row'=4,'col'=4] {'row'}, use_global_device_ids=true, to_apply=%region_1.0 | all-reduce | flops 512 | bytes 4096 | tf_op jit(solution)/shard_map/psum | solution.py:86
  120.6 0.7 broadcast_multiply_fusion.2
  121.2 0.0 copy-done.1
  121.3 2.8 %fusion.24 = f32[256,1536]{1,0:T(8,128)} fusion(f32[8,1536]{1,0:T(8,128)} %bitcast.15, pred[8,1024]{1,0:T(8,128)(4,1)S(1)} %iota_compare_fusion.1, s32[]{:T(128)S(6)} %select_n.7), kind=kOutput, calls=%fused_computation.44 | convolution fusion | flops 37748736 | bytes 1624068 | tf_op jit(solution)/shard_map/dot_general | solution.py:37
  124.0 22.8 %reduce-scatter.2.cloned.1.call-done = bf16[256,768]{1,0:T(8,128)(2,1)} async-done(((bf16[1024,768]{1,0:T(8,128)(2,1)}), bf16[256,768]{1,0:T(8,128)(2,1)}) %reduce-scatter.2.cloned.1.call-update) | async-done | bytes 393232 | tf_op jit(solution)/shard_map/reduce_scatter | solution.py:103
  146.9 1.7 fusion.21
  148.5 7.1 %all-reduce = (f32[256]{0:T(256)}, f32[256]{0:T(256)}) all-reduce(f32[256]{0:T(256)S(1)} %get-tuple-element.4, f32[256]{0:T(256)S(1)} %get-tuple-element.3), channel_id=1, replica_groups=mesh['groups'=2,'row'=4,'col'=4] {'row'}, use_global_device_ids=true, to_apply=%region_10.0 | all-reduce | flops 512 | bytes 4096 | tf_op jit(solution)/shard_map/psum | solution.py:110
  155.7 0.7 broadcast_multiply_fusion
  156.4 2.8 %fusion.20 = (bf16[256,768]{1,0:T(8,128)(2,1)}, bf16[256,768]{1,0:T(8,128)(2,1)}) fusion(bf16[256,768]{1,0:T(8,128)(2,1)} %param.10, f32[256,1536]{1,0:T(8,128)} %fusion.24, f32[256]{0:T(256)S(1)} %get-tuple-element.13, f32[256]{0:T(256)S(1)} %get-tuple-element.14, f32[256]{0:T(256)S(1)} %get-tuple-element.15, f32[256]{0:T(256)S(1)} %get-tuple-element.16, ...), kind=kLoop, calls=%fused_computation.34 | loop fusion | flops 2752512 | bytes 3149824 | tf_op jit(solution)/shard_map/convert_element_type | solution.py:95
  159.2 0.0 all-gather.8.cloned.1.call-update
  159.3 35.8 %all-gather.8.cloned.1.call-done = bf16[1024,768]{1,0:T(8,128)(2,1)} async-done(((bf16[256,768]{1,0:T(8,128)(2,1)}), bf16[1024,768]{1,0:T(8,128)(2,1)}) %all-gather.8.cloned.1.call-update) | async-done | bytes 1572880 | tf_op jit(solution)/shard_map/all_gather | solution.py:96
  195.0 0.0 copy-start.2
  195.0 8.6 %convolution_convert_fusion.1 = bf16[768,2304]{1,0:T(8,128)(2,1)} fusion(bf16[1024,768]{1,0:T(8,128)(2,1)} %all-gather.8.cloned.1.call-done, bf16[1024,2304]{1,0:T(8,128)(2,1)} %all-gather.4.cloned.1.call-done), kind=kOutput, calls=%fused_computation.8 | convolution fusion | flops 3625648128 | bytes 9830400 | tf_op jit(solution)/shard_map/dot_general | solution.py:25
  203.6 0.0 copy-done.2
  203.6 9.5 %convolution_convert_fusion = bf16[768,3072]{1,0:T(8,128)(2,1)} fusion(bf16[1024,768]{1,0:T(8,128)(2,1)S(1)} %copy-done.2, bf16[1024,3072]{1,0:T(8,128)(2,1)} %all-gather.6.cloned.1.call-done), kind=kOutput, calls=%fused_computation.7 | convolution fusion | flops 4834197504 | bytes 12582912 | tf_op jit(solution)/shard_map/dot_general | solution.py:25
  (2 shorter events, 0.0 us)
Async XLA Ops:
  7.2 45.7 %copy-start = (bf16[768,2304]{1,0:T(8,128)(2,1)S(1)}, bf16[768,2304]{1,0:T(8,128)(2,1)}, u32[]{:S(2)}) copy-start(bf16[768,2304]{1,0:T(8,128)(2,1)} %param.18) | copy-start | bytes 10616836
  7.2 45.7 %all-gather.4.cloned.1.call-start = ((), (), s32[]{:S(2)}) async-start(), calls=%async_computation.1 | async-start | bytes 5898240 | tf_op jit(solution)/shard_map/all_gather | solution.py:98
  12.6 88.9 %all-gather.6.cloned.1.call-start = ((), (), s32[]{:S(2)}) async-start(), calls=%async_computation.2 | async-start | bytes 7864320 | tf_op jit(solution)/shard_map/all_gather | solution.py:99
  17.3 129.6 %reduce-scatter.2.cloned.1.call-start = ((), (), s32[]{:S(2)}) async-start(), calls=%async_computation.3 | async-start | bytes 1966080 | tf_op jit(solution)/shard_map/reduce_scatter | solution.py:103
  60.7 60.5 %copy-start.1 = (s32[1024]{0:T(1024)S(1)}, s32[1024]{0:T(1024)}, u32[]{:S(2)}) copy-start(s32[1024]{0:T(1024)} %param.12) | copy-start | bytes 12292
  111.4 83.6 %all-gather.8.cloned.1.call-start = ((), (), s32[]{:S(2)}) async-start(), calls=%async_computation.4 | async-start | bytes 1966080 | tf_op jit(solution)/shard_map/all_gather | solution.py:96
  195.0 8.6 %copy-start.2 = (bf16[1024,768]{1,0:T(8,128)(2,1)S(1)}, bf16[1024,768]{1,0:T(8,128)(2,1)}, u32[]{:S(2)}) copy-start(bf16[1024,768]{1,0:T(8,128)(2,1)} %all-gather.8.cloned.1.call-done) | copy-start | bytes 4718596
Sparse Core Ops, SparseCore 0:
  12.7 40.1 all-gather.3
  55.0 46.3 all-gather.5
  111.5 35.2 reduce-scatter.1
  159.4 35.6 all-gather.7
where the time goes:
time: 220 us
  waiting for transfers between devices  135 us (61%)
  matrix products  39.5 us (18%)
  other arithmetic  16.1 us (7%)
  between operations  13.8 us (6%)
  blocking collectives  13.6 us (6%)
    all_gather x1, waiting for transfers between devices, on_device(): lax.all_gather(grad_m, 'row', axis=0, tiled=True)  40.7 us
    all_gather x1, waiting for transfers between devices, on_device(): normed_all = lax.all_gather(norm_output, 'col', axis=0, tiled=True)  35.8 us
    all_gather x1, waiting for transfers between devices, on_device(): lax.all_gather(grad_q, 'row', axis=0, tiled=True)  35.6 us
    reduce_scatter x1, waiting for transfers between devices, on_device(): lax.psum_scatter((against_weight(all_q, w_qkv) + against_weight(all_m, w_...  22.8 us
    dot_general x2, matrix products, over_tokens(): lax.dot_general(left, right, (((0,), (0,)), ((), ())), preferred_element_...  18.1 us
    dot_general x2, matrix products, against_weight(): lax.dot_general(left, right, (((1,), (1,)), ((), ())), preferred_element_...  17.8 us
    psum x1, blocking collectives, on_device(): lax.psum((jnp.sum(incoming_gradient, axis=1), jnp.sum(incoming_gradient *...  7.14 us
    psum x1, blocking collectives, on_device(): lax.psum((jnp.sum(input_float_copy, axis=1), jnp.sum(input_float_copy * i...  6.48 us
  transfers between devices with their start and end apart: 4, of which 4 were waited for; matrix products, arithmetic and copies ran while one was open for 8% of the time, Pallas kernels for 0%

commit v1 on v0

--- a/solution.py
+++ b/solution.py
@@ -1,8 +1,11 @@
+import functools
 import math
 
 import jax
 import jax.numpy as jnp
 from jax import lax
+from jax.experimental import pallas as pl
+from jax.experimental.pallas import tpu as pltpu
 from jax.sharding import PartitionSpec as P
 
 MODEL_WIDTH = 3072
@@ -11,13 +14,20 @@
 
 EPS = 1e-06
 ROOT = math.sqrt(2.0 / math.pi)
+CUBE = 0.044715
+VMEM_BYTES = 48 * 2**20
+
+CORE = [(0, 1), (1, 0), (2, 3), (3, 2)]
+CHIP = [(0, 2), (2, 0), (1, 3), (3, 1)]
+BOTH = [(0, 3), (3, 0), (1, 2), (2, 1)]
+PIECES = (64, 64, 64, 64)
 
 
 def gelu_slope(value):
-    inner = ROOT * (value + 0.044715 * value * value * value)
+    inner = ROOT * (value + CUBE * value * value * value)
     tangent = jnp.tanh(inner)
     return 0.5 * (1.0 + tangent) + 0.5 * value * (1.0 - tangent * tangent) * ROOT * (
-        1.0 + 3.0 * 0.044715 * value * value
+        1.0 + 3.0 * CUBE * value * value
     )
 
 
@@ -41,6 +51,302 @@
         precision=lax.Precision.HIGHEST,
         preferred_element_type=jnp.float32,
     )
+
+
+def sample_weights(onehot, timestep, reward):
+    counts = jnp.sum(onehot, axis=1)
+    levels = (jnp.arange(TSTEPS, dtype=jnp.float32) + 0.5) / TSTEPS
+    table = 0.5 + 1.5 * levels * (2.0 - levels)
+    level_hits = (timestep[:, None] == jnp.arange(TSTEPS, dtype=jnp.int32)[None, :]).astype(
+        jnp.float32
+    )
+    step_weight = jnp.sum(level_hits * table[None, :], axis=1)
+    return reward * step_weight * lax.rsqrt(counts)
+
+
+def params(**more):
+    return pltpu.CompilerParams(vmem_limit_bytes=VMEM_BYTES, **more)
+
+
+def rows_of(refs):
+    return refs[0][...] if len(refs) == 1 else jnp.concatenate([ref[...] for ref in refs], axis=0)
+
+
+def back_kernel(counts, steps, cuts, scaled, *refs):
+    lefts, at = [], 0
+    for count in counts:
+        lefts.append(refs[at : at + count])
+        at += count
+    weights = refs[at : at + len(counts)]
+    at += len(counts)
+    if scaled:
+        omega = refs[at]
+        at += 1
+    outs, total = refs[at:-1], refs[-1]
+    step = pl.program_id(0)
+
+    @pl.when(step == 0)
+    def _():
+        total[...] = jnp.zeros_like(total)
+
+    low = 0
+    for left, weight, amount in zip(lefts, weights, steps):
+
+        @pl.when((step >= low) & (step < low + amount))
+        def _(left=left, weight=weight):
+            total[...] += against_weight(rows_of(left), weight[...])
+
+        low += amount
+
+    @pl.when(step == low - 1)
+    def _():
+        for out, spans in zip(outs, cuts):
+            place = 0
+            for start, size in spans:
+                value = total[start : start + size, :]
+                if scaled:
+                    value = value * omega[start : start + size, :]
+                out[place : place + size, :] = value.astype(out.dtype)
+                place += size
+
+
+def back(lefts, weights, cuts, dtype, tile, omega=None):
+    width = weights[0].shape[0]
+    rows = sum(left.shape[0] for left in lefts[0])
+    steps = [weight.shape[1] // tile for weight in weights]
+    lows = [sum(steps[:i]) for i in range(len(steps))]
+
+    def at(low, amount):
+        return lambda i: (0, jnp.clip(i - low, 0, amount - 1))
+
+    in_specs = []
+    for group, low, amount in zip(lefts, lows, steps):
+        in_specs += [pl.BlockSpec((left.shape[0], tile), at(low, amount)) for left in group]
+    in_specs += [pl.BlockSpec((width, tile), at(low, amount)) for low, amount in zip(lows, steps)]
+    operands = [left for group in lefts for left in group] + list(weights)
+    if omega is not None:
+        in_specs.append(pl.BlockSpec(omega.shape, lambda i: (0, 0)))
+        operands.append(omega)
+    sizes = [sum(size for _, size in spans) for spans in cuts]
+    depth = sum(weight.shape[1] for weight in weights)
+    return pl.pallas_call(
+        functools.partial(
+            back_kernel, [len(group) for group in lefts], steps, cuts, omega is not None
+        ),
+        grid=(sum(steps),),
+        in_specs=in_specs,
+        out_specs=[pl.BlockSpec((size, width), lambda i: (0, 0)) for size in sizes],
+        out_shape=[jax.ShapeDtypeStruct((size, width), dtype) for size in sizes],
+        scratch_shapes=[pltpu.VMEM((rows, width), jnp.float32)],
+        compiler_params=params(),
+        cost_estimate=pl.CostEstimate(
+            flops=2 * rows * width * depth,
+            bytes_accessed=2 * depth * (rows + width),
+            transcendentals=0,
+        ),
+    )(*operands)
+
+
+def piece_kernel(order, first, second, weight, held, local, omega, *rest):
+    outs, total, blocks = rest[:4], rest[4], rest[5]
+    step = pl.program_id(0)
+    size = first.shape[0]
+
+    @pl.when(step == 0)
+    def _():
+        total[...] = held[...]
+
+    total[...] += against_weight(rows_of([first, second]), weight[...])
+
+    @pl.when(step == pl.num_programs(0) - 1)
+    def _():
+        far = (total[...] * omega[...]).astype(jnp.bfloat16)
+        blocks[0] = local[:size, :]
+        blocks[1] = local[size:, :]
+        blocks[2] = far[:size, :]
+        blocks[3] = far[size:, :]
+        for place, out in enumerate(outs):
+            out[...] = blocks[order[place]]
+
+
+def piece(order, first, second, weight, held, local, omega, tile):
+    size, depth = first.shape
+    width = weight.shape[0]
+    whole = lambda i: (0, 0)
+    return pl.pallas_call(
+        piece_kernel,
+        grid=(depth // tile,),
+        in_specs=[
+            pl.BlockSpec(memory_space=pltpu.SMEM),
+            pl.BlockSpec((size, tile), lambda i: (0, i)),
+            pl.BlockSpec((size, tile), lambda i: (0, i)),
+            pl.BlockSpec((width, tile), lambda i: (0, i)),
+            pl.BlockSpec((2 * size, width), whole),
+            pl.BlockSpec((2 * size, width), whole),
+            pl.BlockSpec((2 * size, 1), whole),
+        ],
+        out_specs=[pl.BlockSpec((size, width), whole)] * 4,
+        out_shape=[jax.ShapeDtypeStruct((size, width), jnp.bfloat16)] * 4,
+        scratch_shapes=[
+            pltpu.VMEM((2 * size, width), jnp.float32),
+            pltpu.VMEM((4, size, width), jnp.bfloat16),
+        ],
+        compiler_params=params(),
+        cost_estimate=pl.CostEstimate(
+            flops=4 * size * width * depth,
+            bytes_accessed=2 * depth * (2 * size + width),
+            transcendentals=0,
+        ),
+    )(order, first, second, weight, held, local, omega)
+
+
+def weight_kernel(*refs):
+    normed, grads, out = refs[0], refs[1:-1], refs[-1]
+    out[...] = over_tokens(normed[...], rows_of(grads)).astype(out.dtype)
+
+
+def weight_grad(normed, grads, tile):
+    tokens, width = normed.shape
+    columns = grads[0].shape[1]
+    return pl.pallas_call(
+        weight_kernel,
+        grid=(columns // tile,),
+        in_specs=[pl.BlockSpec((tokens, width), lambda i: (0, 0))]
+        + [pl.BlockSpec((grad.shape[0], tile), lambda i: (0, i)) for grad in grads],
+        out_specs=pl.BlockSpec((width, tile), lambda i: (0, i)),
+        out_shape=jax.ShapeDtypeStruct((width, columns), jnp.bfloat16),
+        compiler_params=params(),
+        cost_estimate=pl.CostEstimate(
+            flops=2 * tokens * width * columns,
+            bytes_accessed=2 * (tokens * columns + width * columns + tokens * width),
+            transcendentals=0,
+        ),
+    )(normed, *grads)
+
+
+def row_sum(pair):
+    return (
+        pair
+        + lax.ppermute(pair, "row", CORE)
+        + lax.ppermute(pair, "row", CHIP)
+        + lax.ppermute(pair, "row", BOTH)
+    )
+
+
+def on_grid(
+    latents,
+    modulation,
+    sample_of,
+    timestep,
+    reward,
+    qkv_cotangent,
+    mlp_cotangent,
+    mlp_preact,
+    w_qkv,
+    w_mlp,
+):
+    row_id = lax.axis_index("row")
+    col_id = lax.axis_index("col")
+    tok_col, width_row = latents.shape
+    tok_row = qkv_cotangent.shape[0]
+    samples = reward.shape[0]
+    starts = [sum(PIECES[:k]) for k in range(len(PIECES))]
+
+    latents32 = latents.astype(jnp.float32)
+    moments = row_sum(
+        jnp.stack([jnp.sum(latents32, axis=1), jnp.sum(latents32 * latents32, axis=1)])
+    )
+
+    far_q = lax.ppermute(qkv_cotangent, "row", CHIP)
+    side_q = lax.ppermute(qkv_cotangent, "row", CORE)
+
+    sample_ids = jnp.arange(samples, dtype=jnp.int32)
+    onehot = (sample_ids[:, None] == sample_of[None, :]).astype(jnp.float32)
+    omega = lookup(onehot, sample_weights(onehot, timestep, reward)[:, None])
+    blocks = omega.reshape(4, tok_row, 1)
+    omega_near = jnp.concatenate(
+        [lax.dynamic_index_in_dim(blocks, row_id ^ j, keepdims=False) for j in (0, 1)], axis=0
+    )
+    omega_far = [lax.dynamic_index_in_dim(blocks, row_id ^ j, keepdims=False) for j in (2, 3)]
+
+    own_m = [
+        (
+            mlp_cotangent[start : start + size].astype(jnp.float32)
+            * gelu_slope(mlp_preact[start : start + size].astype(jnp.float32))
+        ).astype(jnp.bfloat16)
+        for start, size in zip(starts, PIECES)
+    ]
+    far_m = [lax.ppermute(part, "row", CHIP) for part in own_m]
+    side_m = [lax.ppermute(part, "row", CORE) for part in own_m]
+
+    mod_flat = modulation.reshape(samples, 2 * width_row)
+    own_onehot = lax.dynamic_slice_in_dim(onehot, col_id * tok_col, tok_col, 1)
+    own_mod = lookup(own_onehot, mod_flat)
+    offset = own_mod[:, :width_row]
+    scale = 1.0 + own_mod[:, width_row:]
+    mean = (moments[0] / MODEL_WIDTH)[:, None]
+    rstd = lax.rsqrt((moments[1] / MODEL_WIDTH)[:, None] - mean * mean + EPS)
+    own_omega = lax.dynamic_slice_in_dim(omega, col_id * tok_col, tok_col, 0)
+    normed = (
+        ((latents32 - mean) * rstd * scale + offset) * own_omega
+    ).astype(jnp.bfloat16)
+    pair = jnp.concatenate(
+        [normed, lax.ppermute(normed, "col", [(0, 2), (2, 0), (1, 3), (3, 1)])], axis=0
+    )
+    gathered = jnp.concatenate(
+        [pair, lax.ppermute(pair, "col", [(0, 1), (1, 0), (2, 3), (3, 2)])], axis=0
+    ).reshape(2, 2, tok_col, width_row)
+    normed_all = jnp.concatenate(
+        [
+            lax.dynamic_slice(
+                gathered, (which % 2, which // 2, 0, 0), (1, 1, tok_col, width_row)
+            ).reshape(tok_col, width_row)
+            for which in ((row_id ^ j) ^ col_id for j in range(4))
+        ],
+        axis=0,
+    )
+
+    near_cuts = [
+        [(start, size), (tok_row + start, size)] for start, size in zip(starts, PIECES)
+    ]
+    near = back(
+        [[qkv_cotangent, side_q], own_m + side_m],
+        [w_qkv, w_mlp],
+        near_cuts,
+        jnp.bfloat16,
+        768,
+        omega_near,
+    )
+    farside_q = lax.ppermute(far_q, "row", CORE)
+    far = back([[far_q, farside_q]], [w_qkv], near_cuts, jnp.float32, 768)
+    qkv_total = weight_grad(normed_all, [qkv_cotangent, side_q, far_q, farside_q], 768)
+
+    order = jnp.stack([row_id ^ ((col_id + step) % 4) for step in range(4)])
+    farside_m, incoming = [], []
+    for k, (start, size) in enumerate(zip(starts, PIECES)):
+        farside_m.append(lax.ppermute(far_m[k], "row", CORE))
+        piece_omega = jnp.concatenate([part[start : start + size] for part in omega_far], axis=0)
+        sends = piece(
+            order, far_m[k], farside_m[k], w_mlp, far[k], near[k], piece_omega, 768
+        )
+        total = sends[0].astype(jnp.float32)
+        for step in (1, 2, 3):
+            total = total + lax.ppermute(
+                sends[step], "col", [(i, (i + step) % 4) for i in range(4)]
+            ).astype(jnp.float32)
+        incoming.append(total * scale[start : start + size])
+
+    mlp_total = weight_grad(normed_all, own_m + side_m + far_m + farside_m, 768)
+
+    incoming = jnp.concatenate(incoming, axis=0)
+    xhat = (latents32 - mean) * rstd
+    terms = row_sum(
+        jnp.stack([jnp.sum(incoming, axis=1), jnp.sum(incoming * xhat, axis=1)])
+    ) / MODEL_WIDTH
+    latent_input_gradient = rstd * (
+        incoming - terms[0][:, None] - xhat * terms[1][:, None]
+    )
+    return latent_input_gradient.astype(jnp.bfloat16), qkv_total, mlp_total
 
 
 def on_device(
@@ -63,14 +369,7 @@
     samples = reward.shape[0]
     sample_ids = jnp.arange(samples, dtype=jnp.int32)
     onehot = (sample_ids[:, None] == sample_of[None, :]).astype(jnp.float32)
-    counts = jnp.sum(onehot, axis=1)
-    levels = (jnp.arange(TSTEPS, dtype=jnp.float32) + 0.5) / TSTEPS
-    table = 0.5 + 1.5 * levels * (2.0 - levels)
-    level_hits = (timestep[:, None] == jnp.arange(TSTEPS, dtype=jnp.int32)[None, :]).astype(
-        jnp.float32
-    )
-    step_weight = jnp.sum(level_hits * table[None, :], axis=1)
-    omega_sample = reward * step_weight * lax.rsqrt(counts)
+    omega_sample = sample_weights(onehot, timestep, reward)
     omega_tokens = lookup(onehot, omega_sample[:, None])[:, 0]
     omega_rows = lax.dynamic_slice_in_dim(omega_tokens, row_id * tok_row, tok_row)[:, None]
     grad_q = (qkv_cotangent.astype(jnp.float32) * omega_rows).astype(jnp.bfloat16)
@@ -144,6 +443,11 @@
         P(("groups", "row"), "col"),
         P(("groups", "row"), "col"),
     )
+    small = mesh.shape["row"] == 4 and mesh.shape["col"] == 4
     return jax.shard_map(
-        on_device, mesh=mesh, in_specs=in_specs, out_specs=out_specs, check_vma=False
-    )
+        on_grid if small else on_device,
+        mesh=mesh,
+        in_specs=in_specs,
+        out_specs=out_specs,
+        check_vma=False,
+    )

time: 220 us -> 148 us (0.67)
  waiting for transfers between devices: 135 us -> 46.1 us
  Pallas kernels: 0 us -> 49.1 us
  matrix products: 39.5 us -> 0.97 us
  starting transfers between devices: 0.16 us -> 32.3 us
  blocking collectives: 13.6 us -> 0 us
  between operations: 13.8 us -> 1.15 us
  other arithmetic: 16.1 us -> 13.8 us
    all_gather x3 -> x0, waiting for transfers between devices: 112 us -> none  [the longest x1 40.7 us: on_device(): lax.all_gather(grad_m, 'row', axis=0, tiled=True)]
    pallas_call x0 -> x8, Pallas kernels: none -> 49.1 us  [the longest x4 18.2 us: piece(): pl.pallas_call(piece_kernel, grid=(depth // tile,), in_specs=[pl.BlockSpe...]
    ppermute x0 -> x35, waiting for transfers between devices: none -> 46.1 us  [the longest x4 21.5 us: on_grid(): far_m = [lax.ppermute(part, 'row', CHIP) for part in own_m]]
    dot_general x4 -> x0, matrix products: 35.9 us -> none  [the longest x2 18.1 us: over_tokens(): lax.dot_general(left, right, (((0,), (0,)), ((), ())), preferred_element_...]
    ppermute x0 -> x35, starting transfers between devices: none -> 32.3 us  [the longest x12 16.1 us: on_grid(): lax.ppermute(sends[step], 'col', [(i, (i + step) % 4) for i in range(4)])]
    reduce_scatter x1 -> x0, waiting for transfers between devices: 22.8 us -> none  [on_device(): lax.psum_scatter((against_weight(all_q, w_qkv) + against_weight(all_m, w_...]
    psum x2 -> x0, blocking collectives: 13.6 us -> none  [the longest x1 7.14 us: on_device(): lax.psum((jnp.sum(incoming_gradient, axis=1), jnp.sum(incoming_gradient *...]
    convert_element_type x3, other arithmetic: 9.99 us -> 4.38 us  [the longest x1 2.21 us: on_grid(): own_m = [(mlp_cotangent[start:start + size].astype(jnp.float32) * gelu_sl...]
  transfers between devices with their start and end apart: 4 -> 35, of which waited for: 4 -> 6; matrix products, arithmetic and copies ran while one was open for 8% -> 10% of each run, Pallas kernels for 0% -> 33%
where the time goes in v1:
time: 148 us; the launch traced here: 147 us
  Pallas kernels  49.1 us (33%)
  waiting for transfers between devices  46.1 us (31%)
  starting transfers between devices  32.3 us (22%)
  other arithmetic  13.8 us (9%)
  local copies, waits for them, and re-layouts  3.61 us (2%)
    ppermute x4, waiting for transfers between devices, on_grid(): far_m = [lax.ppermute(part, 'row', CHIP) for part in own_m]  21.5 us
    pallas_call x4, Pallas kernels, piece(): pl.pallas_call(piece_kernel, grid=(depth // tile,), in_specs=[pl.BlockSpe...  18.2 us
    pallas_call x2, Pallas kernels, weight_grad(): pl.pallas_call(weight_kernel, grid=(columns // tile,), in_specs=[pl.Block...  16.1 us
    ppermute x12, starting transfers between devices, on_grid(): lax.ppermute(sends[step], 'col', [(i, (i + step) % 4) for i in range(4)])  16.1 us
    pallas_call x2, Pallas kernels, back(): pl.pallas_call(functools.partial(back_kernel, [len(group) for group in le...  14.8 us
    ppermute x1, waiting for transfers between devices, on_grid(): lax.ppermute(normed, 'col', [(0, 2), (2, 0), (1, 3), (3, 1)])  14.8 us
    ppermute x12, waiting for transfers between devices, on_grid(): lax.ppermute(sends[step], 'col', [(i, (i + step) % 4) for i in range(4)])  9.78 us
    ppermute x4, starting transfers between devices, on_grid(): far_m = [lax.ppermute(part, 'row', CHIP) for part in own_m]  4.03 us
  transfers between devices with their start and end apart: 35, of which 6 were waited for; matrix products, arithmetic and copies ran while one was open for 10% of the time, Pallas kernels for 33%

profile of v1, /device:TPU:0, one launch (start us, length us, event | category | flops | bytes accessed | tf_op | source)
XLA Modules:
  0.0 147.1 jit_solution(13518929608270436399)
XLA Ops:
  0.7 1.3 convert_reduce_fusion
  1.9 2.4 %collective-permute-start.2 = (f32[2,256]{1,0:T(2,128)S(1)}, f32[2,256]{1,0:T(2,128)S(1)}, u32[]{:S(2)}, u32[]{:S(2)}) collective-permute-start(f32[2,256]{1,0:T(2,128)S(1)} %pad_maximum_fusion.4), channel_id=1, source_target_pairs={{0,12},{12,0},{4,8},{8,4},{1,13},{13,1},{5,9},{9,5},{2,14},{14,2},... | collective-permute-start | bytes 6152 | tf_op jit(solution)/shard_map/ppermute | solution.py:232
  4.4 0.6 collective-permute-start.1
  5.1 1.7 %collective-permute-start.5 = (bf16[256,2304]{1,0:T(8,128)(2,1)}, bf16[256,2304]{1,0:T(8,128)(2,1)}, u32[]{:S(2)}, u32[]{:S(2)}) collective-permute-start(bf16[256,2304]{1,0:T(8,128)(2,1)} %refs_1_.1), channel_id=1, source_target_pairs={{0,8},{8,0},{4,12},{12,4},{1,9},{9,1},{5,13},{13,5},{2,10},{10,2},... | collective-permute-start | bytes 3538952 | tf_op jit(solution)/shard_map/ppermute | solution.py:260
  6.8 0.7 iota_compare_fusion.1
  7.5 0.8 convert_reduce_fusion.1
  8.3 0.8 copy.41
  9.1 0.8 select_reduce_fusion
  10.0 0.8 fusion.51
  11.2 1.2 fusion.11
  12.3 2.6 %collective-permute-start.33 = (bf16[256,768]{1,0:T(8,128)(2,1)S(1)}, bf16[256,768]{1,0:T(8,128)(2,1)S(1)}, u32[]{:S(2)}, u32[]{:S(2)}) collective-permute-start(bf16[256,768]{1,0:T(8,128)(2,1)S(1)} %get-tuple-element.63), channel_id=1, source_target_pairs={{0,2},{2,0},{1,3},{3,1},{4,6},{6,4},{5,7},{7,5},{8,10},{10,8},{9,1... | collective-permute-start | bytes 1179656 | tf_op jit(solution)/shard_map/ppermute | solution.py:294
  14.9 2.2 %fusion.37 = (bf16[64,3072]{1,0:T(8,128)(2,1)S(1)}, bf16[64,3072]{1,0:T(8,128)(2,1)S(1)}, bf16[64,3072]{1,0:T(8,128)(2,1)S(1)}, bf16[64,3072]{1,0:T(8,128)(2,1)S(1)}) fusion(bf16[256,3072]{1,0:T(8,128)(2,1)S(1)} %copy-done.10, bf16[256,3072]{1,0:T(8,128)(2,1)S(1)} %copy-done.11), kind=kLoop, calls=%fused_computation.70 | loop fusion | flops 16515072 | bytes 4718592 | tf_op jit(solution)/shard_map/convert_element_type | solution.py:276
  17.7 0.7 fusion.58
  18.4 14.8 %collective-permute-done.33 = bf16[256,768]{1,0:T(8,128)(2,1)S(1)} collective-permute-done((bf16[256,768]{1,0:T(8,128)(2,1)S(1)}, bf16[256,768]{1,0:T(8,128)(2,1)S(1)}, u32[]{:S(2)}, u32[]{:S(2)}) %collective-permute-start.33) | collective-permute-done | bytes 393248 | tf_op jit(solution)/shard_map/ppermute | solution.py:294
  33.3 0.9 pad_maximum_fusion.3
  34.2 7.9 %collective-permute-done.3.first.refs_9_ = bf16[64,3072]{1,0:T(8,128)(2,1)S(1)} collective-permute-done((bf16[64,3072]{1,0:T(8,128)(2,1)S(1)}, bf16[64,3072]{1,0:T(8,128)(2,1)S(1)}, u32[]{:S(2)}, u32[]{:S(2)}) %collective-permute-start.3) | collective-permute-done | bytes 393248 | tf_op jit(solution)/shard_map/ppermute | solution.py:279
  42.6 1.6 %collective-permute-start.34 = (bf16[512,768]{1,0:T(8,128)(2,1)}, bf16[512,768]{1,0:T(8,128)(2,1)}, u32[]{:S(2)}, u32[]{:S(2)}) collective-permute-start(bf16[512,768]{1,0:T(8,128)(2,1)} %pad_maximum_fusion.3), channel_id=1, source_target_pairs={{0,1},{1,0},{2,3},{3,2},{4,5},{5,4},{6,7},{7,6},{8,9},{9,8},{10,11... | collective-permute-start | bytes 2359304 | tf_op jit(solution)/shard_map/ppermute | solution.py:297
  44.8 0.7 pad_maximum_fusion.9
  45.7 0.7 pad_maximum_fusion.8
  46.7 1.4 collective-permute-start.25
  48.1 0.6 collective-permute-start.20
  48.7 1.4 collective-permute-start.15
  50.1 1.3 copy-done.1
  51.4 9.9 %shard_map.122 = (bf16[128,768]{1,0:T(8,128)(2,1)S(1)}, bf16[128,768]{1,0:T(8,128)(2,1)S(1)}, bf16[128,768]{1,0:T(8,128)(2,1)S(1)}, bf16[128,768]{1,0:T(8,128)(2,1)S(1)}) custom-call(bf16[256,2304]{1,0:T(8,128)(2,1)S(1)} %copy-done.1, bf16[256,2304]{1,0:T(8,128)(2,1)} %collective-permute-done.7.refs_1_.refs_2_, ...), custom_call_target="tpu_custom_call" | custom-call | flops 4227858432 | bytes 13762560 | tf_op jit(solution)/shard_map/pallas_call | solution.py:132
  61.4 5.6 %collective-permute-done.20.first.refs_11_ = bf16[64,3072]{1,0:T(8,128)(2,1)S(1)} collective-permute-done((bf16[64,3072]{1,0:T(8,128)(2,1)S(1)}, bf16[64,3072]{1,0:T(8,128)(2,1)S(1)}, u32[]{:S(2)}, u32[]{:S(2)}) %collective-permute-start.20) | collective-permute-done | bytes 393248 | tf_op jit(solution)/shard_map/ppermute | solution.py:279
  67.0 8.0 %collective-permute-done.15.first.refs_10_ = bf16[64,3072]{1,0:T(8,128)(2,1)S(1)} collective-permute-done((bf16[64,3072]{1,0:T(8,128)(2,1)S(1)}, bf16[64,3072]{1,0:T(8,128)(2,1)S(1)}, u32[]{:S(2)}, u32[]{:S(2)}) %collective-permute-start.15) | collective-permute-done | bytes 393248 | tf_op jit(solution)/shard_map/ppermute | solution.py:279
  75.6 1.2 pad_maximum_fusion
  76.9 1.3 pad_maximum_fusion.1.refs_0_
  78.2 4.9 %shard_map.121 = (f32[128,768]{1,0:T(8,128)S(1)}, f32[128,768]{1,0:T(8,128)S(1)}, f32[128,768]{1,0:T(8,128)S(1)}, f32[128,768]{1,0:T(8,128)S(1)}) custom-call(bf16[256,2304]{1,0:T(8,128)(2,1)} %collective-permute-done.5.refs_0_.refs_3_, bf16[256,2304]{1,0:T(8,128)(2,1)} %collective-permute-done.6.refs_1_.refs_4_, bf16[768,2304]{1,0:T(8,128)(2,1)} %refs_10_.1), custom_call_target="tpu_custom_call" | custom-call | flops 1811939328 | bytes 5898240 | tf_op jit(solution)/shard_map/pallas_call | solution.py:132
  83.2 4.5 %shard_map.123 = (bf16[64,768]{1,0:T(8,128)(2,1)S(1)}, bf16[64,768]{1,0:T(8,128)(2,1)S(1)}, bf16[64,768]{1,0:T(8,128)(2,1)S(1)}, bf16[64,768]{1,0:T(8,128)(2,1)S(1)}) custom-call(s32[4]{0:T(128)S(1)} %pad_add_fusion.order, bf16[64,3072]{1,0:T(8,128)(2,1)S(1)} %collective-permute-done.3.first.refs_9_, ...), custom_call_target="tpu_custom_call" | custom-call | flops 603979776 | bytes 5505024 | tf_op jit(solution)/shard_map/pallas_call | solution.py:176
  87.7 2.5 %collective-permute-start.14 = (bf16[64,768]{1,0:T(8,128)(2,1)S(1)}, bf16[64,768]{1,0:T(8,128)(2,1)S(1)}, u32[]{:S(2)}, u32[]{:S(2)}) collective-permute-start(bf16[64,768]{1,0:T(8,128)(2,1)S(1)} %get-tuple-element.32), channel_id=1, source_target_pairs={{0,3},{1,0},{2,1},{3,2},{4,7},{5,4},{6,5},{7,6},{8,11},{9,8},{10,9... | collective-permute-start | bytes 294920 | tf_op jit(solution)/shard_map/ppermute | solution.py:334
  90.4 1.9 %collective-permute-start.12 = (bf16[64,768]{1,0:T(8,128)(2,1)S(1)}, bf16[64,768]{1,0:T(8,128)(2,1)S(1)}, u32[]{:S(2)}, u32[]{:S(2)}) collective-permute-start(bf16[64,768]{1,0:T(8,128)(2,1)S(1)} %get-tuple-element.30), channel_id=1, source_target_pairs={{0,1},{1,2},{2,3},{3,0},{4,5},{5,6},{6,7},{7,4},{8,9},{9,10},{10,1... | collective-permute-start | bytes 294920 | tf_op jit(solution)/shard_map/ppermute | solution.py:334
  92.4 4.5 %shard_map.126 = (bf16[64,768]{1,0:T(8,128)(2,1)S(1)}, bf16[64,768]{1,0:T(8,128)(2,1)S(1)}, bf16[64,768]{1,0:T(8,128)(2,1)S(1)}, bf16[64,768]{1,0:T(8,128)(2,1)S(1)}) custom-call(s32[4]{0:T(128)S(1)} %pad_add_fusion.order, bf16[64,3072]{1,0:T(8,128)(2,1)S(1)} %collective-permute-done.25.first.refs_12_, ...), custom_call_target="tpu_custom_call" | custom-call | flops 603979776 | bytes 5505024 | tf_op jit(solution)/shard_map/pallas_call | solution.py:176
  96.9 1.9 %collective-permute-start.29 = (bf16[64,768]{1,0:T(8,128)(2,1)S(1)}, bf16[64,768]{1,0:T(8,128)(2,1)S(1)}, u32[]{:S(2)}, u32[]{:S(2)}) collective-permute-start(bf16[64,768]{1,0:T(8,128)(2,1)S(1)} %get-tuple-element.50), channel_id=1, source_target_pairs={{0,3},{1,0},{2,1},{3,2},{4,7},{5,4},{6,5},{7,6},{8,11},{9,8},{10,9... | collective-permute-start | bytes 294920 | tf_op jit(solution)/shard_map/ppermute | solution.py:334
  98.9 4.5 %shard_map.124 = (bf16[64,768]{1,0:T(8,128)(2,1)S(1)}, bf16[64,768]{1,0:T(8,128)(2,1)S(1)}, bf16[64,768]{1,0:T(8,128)(2,1)S(1)}, bf16[64,768]{1,0:T(8,128)(2,1)S(1)}) custom-call(s32[4]{0:T(128)S(1)} %pad_add_fusion.order, bf16[64,3072]{1,0:T(8,128)(2,1)S(1)} %collective-permute-done.15.first.refs_10_, ...), custom_call_target="tpu_custom_call" | custom-call | flops 603979776 | bytes 5505024 | tf_op jit(solution)/shard_map/pallas_call | solution.py:176
  104.0 1.1 collective-permute-start.18
  105.1 1.3 collective-permute-start.17
  106.4 8.8 %shard_map.128 = bf16[768,3072]{1,0:T(8,128)(2,1)} custom-call(bf16[1024,768]{1,0:T(8,128)(2,1)} %pad_maximum_fusion.1.refs_0_, bf16[64,3072]{1,0:T(8,128)(2,1)S(1)} %get-tuple-element.57.refs_2_.refs_1_, bf16[64,3072]{1,0:T(8,128)(2,1)S(1)} %get-tuple-element.56.refs_3_.refs_2_, bf16[64,3072]{1,0:T(8,128)(2,1)S(1)} %get-tuple-element.55.refs_4_.refs_3_, ...), custom_call_target="tpu_custom_call" | custom-call | flops 4831838208 | bytes 12582912 | tf_op jit(solution)/shard_map/pallas_call | solution.py:211
  115.2 4.6 %shard_map.125 = (bf16[64,768]{1,0:T(8,128)(2,1)S(1)}, bf16[64,768]{1,0:T(8,128)(2,1)S(1)}, bf16[64,768]{1,0:T(8,128)(2,1)S(1)}, bf16[64,768]{1,0:T(8,128)(2,1)S(1)}) custom-call(s32[4]{0:T(128)S(1)} %pad_add_fusion.order, bf16[64,3072]{1,0:T(8,128)(2,1)S(1)} %collective-permute-done.20.first.refs_11_, ...), custom_call_target="tpu_custom_call" | custom-call | flops 603979776 | bytes 5505024 | tf_op jit(solution)/shard_map/pallas_call | solution.py:176
  119.8 2.1 %collective-permute-start.28 = (bf16[64,768]{1,0:T(8,128)(2,1)S(1)}, bf16[64,768]{1,0:T(8,128)(2,1)S(1)}, u32[]{:S(2)}, u32[]{:S(2)}) collective-permute-start(bf16[64,768]{1,0:T(8,128)(2,1)S(1)} %get-tuple-element.49), channel_id=1, source_target_pairs={{0,2},{1,3},{2,0},{3,1},{4,6},{5,7},{6,4},{7,5},{8,10},{9,11},{10,... | collective-permute-start | bytes 294920 | tf_op jit(solution)/shard_map/ppermute | solution.py:334
  121.9 1.0 collective-permute-start.27
  122.9 2.8 %collective-permute-start.24 = (bf16[64,768]{1,0:T(8,128)(2,1)S(1)}, bf16[64,768]{1,0:T(8,128)(2,1)S(1)}, u32[]{:S(2)}, u32[]{:S(2)}) collective-permute-start(bf16[64,768]{1,0:T(8,128)(2,1)S(1)} %get-tuple-element.44), channel_id=1, source_target_pairs={{0,3},{1,0},{2,1},{3,2},{4,7},{5,4},{6,5},{7,6},{8,11},{9,8},{10,9... | collective-permute-start | bytes 294920 | tf_op jit(solution)/shard_map/ppermute | solution.py:334
  125.7 0.6 collective-permute-start.22
  126.4 7.5 %collective-permute-done.28 = bf16[64,768]{1,0:T(8,128)(2,1)S(1)} collective-permute-done((bf16[64,768]{1,0:T(8,128)(2,1)S(1)}, bf16[64,768]{1,0:T(8,128)(2,1)S(1)}, u32[]{:S(2)}, u32[]{:S(2)}) %collective-permute-start.28) | collective-permute-done | bytes 98336 | tf_op jit(solution)/shard_map/ppermute | solution.py:334
  133.9 2.3 %collective-permute-done.23 = bf16[64,768]{1,0:T(8,128)(2,1)S(1)} collective-permute-done((bf16[64,768]{1,0:T(8,128)(2,1)S(1)}, bf16[64,768]{1,0:T(8,128)(2,1)S(1)}, u32[]{:S(2)}, u32[]{:S(2)}) %collective-permute-start.23) | collective-permute-done | bytes 98336 | tf_op jit(solution)/shard_map/ppermute | solution.py:334
  136.8 1.5 collective-permute-start.31
  138.6 7.4 %shard_map.127 = bf16[768,2304]{1,0:T(8,128)(2,1)} custom-call(bf16[1024,768]{1,0:T(8,128)(2,1)} %pad_maximum_fusion.1.refs_0_, bf16[256,2304]{1,0:T(8,128)(2,1)S(1)} %copy-done.2, bf16[256,2304]{1,0:T(8,128)(2,1)} %collective-permute-done.7.refs_1_.refs_2_, bf16[256,2304]{1,0:T(8,128)(2,1)} %collective-permute-done.5.refs_0_.refs_3_, ...), custom_call_target="tpu_custom_call" | custom-call | flops 3623878656 | bytes 9830400 | tf_op jit(solution)/shard_map/pallas_call | solution.py:211
  146.0 1.0 fusion.8
  (101 shorter events, 5.0 us)
Async XLA Ops:
  0.6 10.5 %copy-start.3 = (bf16[256,768]{1,0:T(8,128)(2,1)S(1)}, bf16[256,768]{1,0:T(8,128)(2,1)}, u32[]{:S(2)}) copy-start(bf16[256,768]{1,0:T(8,128)(2,1)} %param.10) | copy-start | bytes 1179652
  0.6 10.2 %copy-start.12 = (s32[1024]{0:T(1024)S(1)}, s32[1024]{0:T(1024)}, u32[]{:S(2)}) copy-start(s32[1024]{0:T(1024)} %param.12) | copy-start | bytes 12292
  0.7 10.2 %copy-start.15 = (f32[8]{0:T(128)S(1)}, f32[8]{0:T(128)}, u32[]{:S(2)}) copy-start(f32[8]{0:T(128)} %param.14) | copy-start | bytes 100
  1.9 9.1 %collective-permute-start.2 = (f32[2,256]{1,0:T(2,128)S(1)}, f32[2,256]{1,0:T(2,128)S(1)}, u32[]{:S(2)}, u32[]{:S(2)}) collective-permute-start(f32[2,256]{1,0:T(2,128)S(1)} %pad_maximum_fusion.4), channel_id=1, source_target_pairs={{0,12},{12,0},{4,8},{8,4},{1,13},{13,1},{5,9},{9,5},{2,14},{14,2},... | collective-permute-start | bytes 6152 | tf_op jit(solution)/shard_map/ppermute | solution.py:232
  4.4 6.7 %collective-permute-start.1 = (f32[2,256]{1,0:T(2,128)S(1)}, f32[2,256]{1,0:T(2,128)S(1)}, u32[]{:S(2)}, u32[]{:S(2)}) collective-permute-start(f32[2,256]{1,0:T(2,128)S(1)} %pad_maximum_fusion.4), channel_id=1, source_target_pairs={{0,8},{8,0},{4,12},{12,4},{1,9},{9,1},{5,13},{13,5},{2,10},{10,2},... | collective-permute-start | bytes 6152 | tf_op jit(solution)/shard_map/ppermute | solution.py:231
  5.0 6.0 %collective-permute-start = (f32[2,256]{1,0:T(2,128)S(1)}, f32[2,256]{1,0:T(2,128)S(1)}, u32[]{:S(2)}, u32[]{:S(2)}) collective-permute-start(f32[2,256]{1,0:T(2,128)S(1)} %pad_maximum_fusion.4), channel_id=1, source_target_pairs={{0,4},{4,0},{8,12},{12,8},{1,5},{5,1},{9,13},{13,9},{2,6},{6,2},{1... | collective-permute-start | bytes 6152 | tf_op jit(solution)/shard_map/ppermute | solution.py:230
  5.1 39.7 %collective-permute-start.5 = (bf16[256,2304]{1,0:T(8,128)(2,1)}, bf16[256,2304]{1,0:T(8,128)(2,1)}, u32[]{:S(2)}, u32[]{:S(2)}) collective-permute-start(bf16[256,2304]{1,0:T(8,128)(2,1)} %refs_1_.1), channel_id=1, source_target_pairs={{0,8},{8,0},{4,12},{12,4},{1,9},{9,1},{5,13},{13,5},{2,10},{10,2},... | collective-permute-start | bytes 3538952 | tf_op jit(solution)/shard_map/ppermute | solution.py:260
  6.8 41.9 %collective-permute-start.7 = (bf16[256,2304]{1,0:T(8,128)(2,1)}, bf16[256,2304]{1,0:T(8,128)(2,1)}, u32[]{:S(2)}, u32[]{:S(2)}) collective-permute-start(bf16[256,2304]{1,0:T(8,128)(2,1)} %refs_1_.1), channel_id=1, source_target_pairs={{0,4},{4,0},{8,12},{12,8},{1,5},{5,1},{9,13},{13,9},{2,6},{6,2},{1... | collective-permute-start | bytes 3538952 | tf_op jit(solution)/shard_map/ppermute | solution.py:261
  11.1 3.8 %copy-start.10 = (bf16[256,3072]{1,0:T(8,128)(2,1)S(1)}, bf16[256,3072]{1,0:T(8,128)(2,1)}, u32[]{:S(2)}) copy-start(bf16[256,3072]{1,0:T(8,128)(2,1)} %param.17) | copy-start | bytes 4718596
  12.3 21.0 %copy-start.5 = (bf16[256,768]{1,0:T(8,128)(2,1)}, bf16[256,768]{1,0:T(8,128)(2,1)S(1)}, u32[]{:S(2)}) copy-start(bf16[256,768]{1,0:T(8,128)(2,1)S(1)} %get-tuple-element.63) | copy-start | bytes 1179652
  12.3 20.9 %collective-permute-start.33 = (bf16[256,768]{1,0:T(8,128)(2,1)S(1)}, bf16[256,768]{1,0:T(8,128)(2,1)S(1)}, u32[]{:S(2)}, u32[]{:S(2)}) collective-permute-start(bf16[256,768]{1,0:T(8,128)(2,1)S(1)} %get-tuple-element.63), channel_id=1, source_target_pairs={{0,2},{2,0},{1,3},{3,1},{4,6},{6,4},{5,7},{7,5},{8,10},{10,8},{9,1... | collective-permute-start | bytes 1179656 | tf_op jit(solution)/shard_map/ppermute | solution.py:294
  17.1 24.9 %collective-permute-start.3 = (bf16[64,3072]{1,0:T(8,128)(2,1)S(1)}, bf16[64,3072]{1,0:T(8,128)(2,1)S(1)}, u32[]{:S(2)}, u32[]{:S(2)}) collective-permute-start(bf16[64,3072]{1,0:T(8,128)(2,1)S(1)} %get-tuple-element.57.refs_2_.refs_1_), channel_id=1, source_target_pairs={{0,8},{8,0},{4,12},{12,4},{1,9},{9,1},{5,13},{13,5},{2,10},{10,2},... | collective-permute-start | bytes 1179656 | tf_op jit(solution)/shard_map/ppermute | solution.py:279
  17.7 24.3 %collective-permute-start.8 = (bf16[64,3072]{1,0:T(8,128)(2,1)S(1)}, bf16[64,3072]{1,0:T(8,128)(2,1)S(1)}, u32[]{:S(2)}, u32[]{:S(2)}) collective-permute-start(bf16[64,3072]{1,0:T(8,128)(2,1)S(1)} %get-tuple-element.57.refs_2_.refs_1_), channel_id=1, source_target_pairs={{0,4},{4,0},{8,12},{12,8},{1,5},{5,1},{9,13},{13,9},{2,6},{6,2},{1... | collective-permute-start | bytes 1179656 | tf_op jit(solution)/shard_map/ppermute | solution.py:280
  33.2 11.2 %copy-start.8 = (bf16[256,768]{1,0:T(8,128)(2,1)}, bf16[256,768]{1,0:T(8,128)(2,1)S(1)}, u32[]{:S(2)}) copy-start(bf16[256,768]{1,0:T(8,128)(2,1)S(1)} %collective-permute-done.33) | copy-start | bytes 1179652
  33.2 9.4 %collective-permute-start.9 = (bf16[64,3072]{1,0:T(8,128)(2,1)S(1)}, bf16[64,3072]{1,0:T(8,128)(2,1)S(1)}, u32[]{:S(2)}, u32[]{:S(2)}) collective-permute-start(bf16[64,3072]{1,0:T(8,128)(2,1)S(1)} %get-tuple-element.56.refs_3_.refs_2_), channel_id=1, source_target_pairs={{0,4},{4,0},{8,12},{12,8},{1,5},{5,1},{9,13},{13,9},{2,6},{6,2},{1... | collective-permute-start | bytes 1179656 | tf_op jit(solution)/shard_map/ppermute | solution.py:280
  33.2 10.9 %copy-start.13 = (f32[64,1]{0,1:T(1,128)S(1)}, f32[64,1]{0,1:T(1,128)}, u32[]{:S(2)}) copy-start(f32[64,1]{0,1:T(1,128)} %get-tuple-element.74) | copy-start | bytes 772
  33.2 10.9 %copy-start.14 = (f32[64,1]{0,1:T(1,128)S(1)}, f32[64,1]{0,1:T(1,128)}, u32[]{:S(2)}) copy-start(f32[64,1]{0,1:T(1,128)} %get-tuple-element.75) | copy-start | bytes 772
  42.1 4.6 %collective-permute-start.10 = (bf16[64,3072]{1,0:T(8,128)(2,1)S(1)}, bf16[64,3072]{1,0:T(8,128)(2,1)}, u32[]{:S(2)}, u32[]{:S(2)}) collective-permute-start(bf16[64,3072]{1,0:T(8,128)(2,1)S(1)} %get-tuple-element.55.refs_4_.refs_3_), channel_id=1, source_target_pairs={{0,4},{4,0},{8,12},{12,8},{1,5},{5,1},{9,13},{13,9},{2,6},{6,2},{1... | collective-permute-start | bytes 1179656 | tf_op jit(solution)/shard_map/ppermute | solution.py:280
  42.1 6.0 %collective-permute-start.11 = (bf16[64,3072]{1,0:T(8,128)(2,1)S(1)}, bf16[64,3072]{1,0:T(8,128)(2,1)}, u32[]{:S(2)}, u32[]{:S(2)}) collective-permute-start(bf16[64,3072]{1,0:T(8,128)(2,1)S(1)} %get-tuple-element.58.refs_5_.refs_4_), channel_id=1, source_target_pairs={{0,4},{4,0},{8,12},{12,8},{1,5},{5,1},{9,13},{13,9},{2,6},{6,2},{1... | collective-permute-start | bytes 1179656 | tf_op jit(solution)/shard_map/ppermute | solution.py:280
  42.6 32.5 %collective-permute-start.34 = (bf16[512,768]{1,0:T(8,128)(2,1)}, bf16[512,768]{1,0:T(8,128)(2,1)}, u32[]{:S(2)}, u32[]{:S(2)}) collective-permute-start(bf16[512,768]{1,0:T(8,128)(2,1)} %pad_maximum_fusion.3), channel_id=1, source_target_pairs={{0,1},{1,0},{2,3},{3,2},{4,5},{5,4},{6,7},{7,6},{8,9},{9,8},{10,11... | collective-permute-start | bytes 2359304 | tf_op jit(solution)/shard_map/ppermute | solution.py:297
  44.7 33.5 %collective-permute-start.6 = (bf16[256,2304]{1,0:T(8,128)(2,1)}, bf16[256,2304]{1,0:T(8,128)(2,1)}, u32[]{:S(2)}, u32[]{:S(2)}) collective-permute-start(bf16[256,2304]{1,0:T(8,128)(2,1)} %collective-permute-done.5.refs_0_.refs_3_), channel_id=1, source_target_pairs={{0,4},{4,0},{8,12},{12,8},{1,5},{5,1},{9,13},{13,9},{2,6},{6,2},{1... | collective-permute-start | bytes 3538952 | tf_op jit(solution)/shard_map/ppermute | solution.py:320
  46.7 14.6 %collective-permute-start.25 = (bf16[64,3072]{1,0:T(8,128)(2,1)S(1)}, bf16[64,3072]{1,0:T(8,128)(2,1)S(1)}, u32[]{:S(2)}, u32[]{:S(2)}) collective-permute-start(bf16[64,3072]{1,0:T(8,128)(2,1)S(1)} %get-tuple-element.58.refs_5_.refs_4_), channel_id=1, source_target_pairs={{0,8},{8,0},{4,12},{12,4},{1,9},{9,1},{5,13},{13,5},{2,10},{10,2},... | collective-permute-start | bytes 1179656 | tf_op jit(solution)/shard_map/ppermute | solution.py:279
  48.1 18.9 %collective-permute-start.20 = (bf16[64,3072]{1,0:T(8,128)(2,1)S(1)}, bf16[64,3072]{1,0:T(8,128)(2,1)S(1)}, u32[]{:S(2)}, u32[]{:S(2)}) collective-permute-start(bf16[64,3072]{1,0:T(8,128)(2,1)S(1)} %get-tuple-element.55.refs_4_.refs_3_), channel_id=1, source_target_pairs={{0,8},{8,0},{4,12},{12,4},{1,9},{9,1},{5,13},{13,5},{2,10},{10,2},... | collective-permute-start | bytes 1179656 | tf_op jit(solution)/shard_map/ppermute | solution.py:279
  48.7 26.3 %collective-permute-start.15 = (bf16[64,3072]{1,0:T(8,128)(2,1)S(1)}, bf16[64,3072]{1,0:T(8,128)(2,1)S(1)}, u32[]{:S(2)}, u32[]{:S(2)}) collective-permute-start(bf16[64,3072]{1,0:T(8,128)(2,1)S(1)} %get-tuple-element.56.refs_3_.refs_2_), channel_id=1, source_target_pairs={{0,8},{8,0},{4,12},{12,4},{1,9},{9,1},{5,13},{13,5},{2,10},{10,2},... | collective-permute-start | bytes 1179656 | tf_op jit(solution)/shard_map/ppermute | solution.py:279
  51.4 24.2 %copy-start.6 = (bf16[256,768]{1,0:T(8,128)(2,1)S(1)}, bf16[256,768]{1,0:T(8,128)(2,1)}, u32[]{:S(2)}) copy-start(bf16[256,768]{1,0:T(8,128)(2,1)} %copy-done.5) | copy-start | bytes 1179652
  51.4 24.2 %copy-start.9 = (bf16[256,768]{1,0:T(8,128)(2,1)S(1)}, bf16[256,768]{1,0:T(8,128)(2,1)}, u32[]{:S(2)}) copy-start(bf16[256,768]{1,0:T(8,128)(2,1)} %copy-done.8) | copy-start | bytes 1179652
  61.3 21.9 %collective-permute-start.4 = (bf16[64,3072]{1,0:T(8,128)(2,1)S(1)}, bf16[64,3072]{1,0:T(8,128)(2,1)S(1)}, u32[]{:S(2)}, u32[]{:S(2)}) collective-permute-start(bf16[64,3072]{1,0:T(8,128)(2,1)S(1)} %collective-permute-done.3.first.refs_9_), channel_id=1, source_target_pairs={{0,4},{4,0},{8,12},{12,8},{1,5},{5,1},{9,13},{13,9},{2,6},{6,2},{1... | collective-permute-start | bytes 1179656 | tf_op jit(solution)/shard_map/ppermute | solution.py:327
  67.0 23.4 %collective-permute-start.26 = (bf16[64,3072]{1,0:T(8,128)(2,1)S(1)}, bf16[64,3072]{1,0:T(8,128)(2,1)S(1)}, u32[]{:S(2)}, u32[]{:S(2)}) collective-permute-start(bf16[64,3072]{1,0:T(8,128)(2,1)S(1)} %collective-permute-done.25.first.refs_12_), channel_id=1, source_target_pairs={{0,4},{4,0},{8,12},{12,8},{1,5},{5,1},{9,13},{13,9},{2,6},{6,2},{1... | collective-permute-start | bytes 1179656 | tf_op jit(solution)/shard_map/ppermute | solution.py:327
  75.0 28.3 %collective-permute-start.21 = (bf16[64,3072]{1,0:T(8,128)(2,1)S(1)}, bf16[64,3072]{1,0:T(8,128)(2,1)S(1)}, u32[]{:S(2)}, u32[]{:S(2)}) collective-permute-start(bf16[64,3072]{1,0:T(8,128)(2,1)S(1)} %collective-permute-done.20.first.refs_11_), channel_id=1, source_target_pairs={{0,4},{4,0},{8,12},{12,8},{1,5},{5,1},{9,13},{13,9},{2,6},{6,2},{1... | collective-permute-start | bytes 1179656 | tf_op jit(solution)/shard_map/ppermute | solution.py:327
  75.1 21.9 %collective-permute-start.16 = (bf16[64,3072]{1,0:T(8,128)(2,1)S(1)}, bf16[64,3072]{1,0:T(8,128)(2,1)S(1)}, u32[]{:S(2)}, u32[]{:S(2)}) collective-permute-start(bf16[64,3072]{1,0:T(8,128)(2,1)S(1)} %collective-permute-done.15.first.refs_10_), channel_id=1, source_target_pairs={{0,4},{4,0},{8,12},{12,8},{1,5},{5,1},{9,13},{13,9},{2,6},{6,2},{1... | collective-permute-start | bytes 1179656 | tf_op jit(solution)/shard_map/ppermute | solution.py:327
  87.7 16.2 %collective-permute-start.14 = (bf16[64,768]{1,0:T(8,128)(2,1)S(1)}, bf16[64,768]{1,0:T(8,128)(2,1)S(1)}, u32[]{:S(2)}, u32[]{:S(2)}) collective-permute-start(bf16[64,768]{1,0:T(8,128)(2,1)S(1)} %get-tuple-element.32), channel_id=1, source_target_pairs={{0,3},{1,0},{2,1},{3,2},{4,7},{5,4},{6,5},{7,6},{8,11},{9,8},{10,9... | collective-permute-start | bytes 294920 | tf_op jit(solution)/shard_map/ppermute | solution.py:334
  90.2 14.8 %collective-permute-start.13 = (bf16[64,768]{1,0:T(8,128)(2,1)S(1)}, bf16[64,768]{1,0:T(8,128)(2,1)S(1)}, u32[]{:S(2)}, u32[]{:S(2)}) collective-permute-start(bf16[64,768]{1,0:T(8,128)(2,1)S(1)} %get-tuple-element.31), channel_id=1, source_target_pairs={{0,2},{1,3},{2,0},{3,1},{4,6},{5,7},{6,4},{7,5},{8,10},{9,11},{10,... | collective-permute-start | bytes 294920 | tf_op jit(solution)/shard_map/ppermute | solution.py:334
  90.4 6.5 %copy-start = (bf16[64,3072]{1,0:T(8,128)(2,1)}, bf16[64,3072]{1,0:T(8,128)(2,1)S(1)}, u32[]{:S(2)}) copy-start(bf16[64,3072]{1,0:T(8,128)(2,1)S(1)} %collective-permute-done.26.second.refs_16_) | copy-start | bytes 1179652
  90.4 29.3 %collective-permute-start.12 = (bf16[64,768]{1,0:T(8,128)(2,1)S(1)}, bf16[64,768]{1,0:T(8,128)(2,1)S(1)}, u32[]{:S(2)}, u32[]{:S(2)}) collective-permute-start(bf16[64,768]{1,0:T(8,128)(2,1)S(1)} %get-tuple-element.30), channel_id=1, source_target_pairs={{0,1},{1,2},{2,3},{3,0},{4,5},{5,6},{6,7},{7,4},{8,9},{9,10},{10,1... | collective-permute-start | bytes 294920 | tf_op jit(solution)/shard_map/ppermute | solution.py:334
  96.9 24.9 %collective-permute-start.29 = (bf16[64,768]{1,0:T(8,128)(2,1)S(1)}, bf16[64,768]{1,0:T(8,128)(2,1)S(1)}, u32[]{:S(2)}, u32[]{:S(2)}) collective-permute-start(bf16[64,768]{1,0:T(8,128)(2,1)S(1)} %get-tuple-element.50), channel_id=1, source_target_pairs={{0,3},{1,0},{2,1},{3,2},{4,7},{5,4},{6,5},{7,6},{8,11},{9,8},{10,9... | collective-permute-start | bytes 294920 | tf_op jit(solution)/shard_map/ppermute | solution.py:334
  103.4 19.5 %collective-permute-start.19 = (bf16[64,768]{1,0:T(8,128)(2,1)S(1)}, bf16[64,768]{1,0:T(8,128)(2,1)S(1)}, u32[]{:S(2)}, u32[]{:S(2)}) collective-permute-start(bf16[64,768]{1,0:T(8,128)(2,1)S(1)} %get-tuple-element.38), channel_id=1, source_target_pairs={{0,3},{1,0},{2,1},{3,2},{4,7},{5,4},{6,5},{7,6},{8,11},{9,8},{10,9... | collective-permute-start | bytes 294920 | tf_op jit(solution)/shard_map/ppermute | solution.py:334
  104.0 21.7 %collective-permute-start.18 = (bf16[64,768]{1,0:T(8,128)(2,1)S(1)}, bf16[64,768]{1,0:T(8,128)(2,1)S(1)}, u32[]{:S(2)}, u32[]{:S(2)}) collective-permute-start(bf16[64,768]{1,0:T(8,128)(2,1)S(1)} %get-tuple-element.37), channel_id=1, source_target_pairs={{0,2},{1,3},{2,0},{3,1},{4,6},{5,7},{6,4},{7,5},{8,10},{9,11},{10,... | collective-permute-start | bytes 294920 | tf_op jit(solution)/shard_map/ppermute | solution.py:334
  105.1 20.6 %collective-permute-start.17 = (bf16[64,768]{1,0:T(8,128)(2,1)S(1)}, bf16[64,768]{1,0:T(8,128)(2,1)S(1)}, u32[]{:S(2)}, u32[]{:S(2)}) collective-permute-start(bf16[64,768]{1,0:T(8,128)(2,1)S(1)} %get-tuple-element.36), channel_id=1, source_target_pairs={{0,1},{1,2},{2,3},{3,0},{4,5},{5,6},{6,7},{7,4},{8,9},{9,10},{10,1... | collective-permute-start | bytes 294920 | tf_op jit(solution)/shard_map/ppermute | solution.py:334
  115.2 11.1 %copy-start.7 = (f32[256,768]{1,0:T(8,128)S(1)}, f32[256,768]{1,0:T(8,128)}, u32[]{:S(2)}) copy-start(f32[256,768]{1,0:T(8,128)} %get-tuple-element.64) | copy-start | bytes 2359300
  119.8 14.1 %collective-permute-start.28 = (bf16[64,768]{1,0:T(8,128)(2,1)S(1)}, bf16[64,768]{1,0:T(8,128)(2,1)S(1)}, u32[]{:S(2)}, u32[]{:S(2)}) collective-permute-start(bf16[64,768]{1,0:T(8,128)(2,1)S(1)} %get-tuple-element.49), channel_id=1, source_target_pairs={{0,2},{1,3},{2,0},{3,1},{4,6},{5,7},{6,4},{7,5},{8,10},{9,11},{10,... | collective-permute-start | bytes 294920 | tf_op jit(solution)/shard_map/ppermute | solution.py:334
  121.9 12.0 %collective-permute-start.27 = (bf16[64,768]{1,0:T(8,128)(2,1)S(1)}, bf16[64,768]{1,0:T(8,128)(2,1)S(1)}, u32[]{:S(2)}, u32[]{:S(2)}) collective-permute-start(bf16[64,768]{1,0:T(8,128)(2,1)S(1)} %get-tuple-element.48), channel_id=1, source_target_pairs={{0,1},{1,2},{2,3},{3,0},{4,5},{5,6},{6,7},{7,4},{8,9},{9,10},{10,1... | collective-permute-start | bytes 294920 | tf_op jit(solution)/shard_map/ppermute | solution.py:334
  122.9 10.9 %collective-permute-start.24 = (bf16[64,768]{1,0:T(8,128)(2,1)S(1)}, bf16[64,768]{1,0:T(8,128)(2,1)S(1)}, u32[]{:S(2)}, u32[]{:S(2)}) collective-permute-start(bf16[64,768]{1,0:T(8,128)(2,1)S(1)} %get-tuple-element.44), channel_id=1, source_target_pairs={{0,3},{1,0},{2,1},{3,2},{4,7},{5,4},{6,5},{7,6},{8,11},{9,8},{10,9... | collective-permute-start | bytes 294920 | tf_op jit(solution)/shard_map/ppermute | solution.py:334
  125.7 10.5 %collective-permute-start.23 = (bf16[64,768]{1,0:T(8,128)(2,1)S(1)}, bf16[64,768]{1,0:T(8,128)(2,1)S(1)}, u32[]{:S(2)}, u32[]{:S(2)}) collective-permute-start(bf16[64,768]{1,0:T(8,128)(2,1)S(1)} %get-tuple-element.43), channel_id=1, source_target_pairs={{0,2},{1,3},{2,0},{3,1},{4,6},{5,7},{6,4},{7,5},{8,10},{9,11},{10,... | collective-permute-start | bytes 294920 | tf_op jit(solution)/shard_map/ppermute | solution.py:334
  125.7 10.5 %collective-permute-start.22 = (bf16[64,768]{1,0:T(8,128)(2,1)S(1)}, bf16[64,768]{1,0:T(8,128)(2,1)S(1)}, u32[]{:S(2)}, u32[]{:S(2)}) collective-permute-start(bf16[64,768]{1,0:T(8,128)(2,1)S(1)} %get-tuple-element.42), channel_id=1, source_target_pairs={{0,1},{1,2},{2,3},{3,0},{4,5},{5,6},{6,7},{7,4},{8,9},{9,10},{10,1... | collective-permute-start | bytes 294920 | tf_op jit(solution)/shard_map/ppermute | solution.py:334
  126.3 10.0 %copy-start.4 = (bf16[256,768]{1,0:T(8,128)(2,1)S(1)}, bf16[256,768]{1,0:T(8,128)(2,1)}, u32[]{:S(2)}) copy-start(bf16[256,768]{1,0:T(8,128)(2,1)} %param.10) | copy-start | bytes 1179652
  136.7 9.3 %collective-permute-start.32 = (f32[2,256]{1,0:T(2,128)S(1)}, f32[2,256]{1,0:T(2,128)S(1)}, u32[]{:S(2)}, u32[]{:S(2)}) collective-permute-start(f32[2,256]{1,0:T(2,128)S(1)} %pad_maximum_fusion.6), channel_id=1, source_target_pairs={{0,12},{12,0},{4,8},{8,4},{1,13},{13,1},{5,9},{9,5},{2,14},{14,2},... | collective-permute-start | bytes 6152 | tf_op jit(solution)/shard_map/ppermute | solution.py:232
  136.8 9.2 %collective-permute-start.31 = (f32[2,256]{1,0:T(2,128)S(1)}, f32[2,256]{1,0:T(2,128)S(1)}, u32[]{:S(2)}, u32[]{:S(2)}) collective-permute-start(f32[2,256]{1,0:T(2,128)S(1)} %pad_maximum_fusion.6), channel_id=1, source_target_pairs={{0,8},{8,0},{4,12},{12,4},{1,9},{9,1},{5,13},{13,5},{2,10},{10,2},... | collective-permute-start | bytes 6152 | tf_op jit(solution)/shard_map/ppermute | solution.py:231
  138.2 7.8 %collective-permute-start.30 = (f32[2,256]{1,0:T(2,128)S(1)}, f32[2,256]{1,0:T(2,128)S(1)}, u32[]{:S(2)}, u32[]{:S(2)}) collective-permute-start(f32[2,256]{1,0:T(2,128)S(1)} %pad_maximum_fusion.6), channel_id=1, source_target_pairs={{0,4},{4,0},{8,12},{12,8},{1,5},{5,1},{9,13},{13,9},{2,6},{6,2},{1... | collective-permute-start | bytes 6152 | tf_op jit(solution)/shard_map/ppermute | solution.py:230
  (3 other events, 7.5 us)

commit v2 on v0

--- a/solution.py
+++ b/solution.py
@@ -1,8 +1,11 @@
+import functools
 import math
 
 import jax
 import jax.numpy as jnp
 from jax import lax
+from jax.experimental import pallas as pl
+from jax.experimental.pallas import tpu as pltpu
 from jax.sharding import PartitionSpec as P
 
 MODEL_WIDTH = 3072
@@ -11,13 +14,25 @@
 
 EPS = 1e-06
 ROOT = math.sqrt(2.0 / math.pi)
+CUBE = 0.044715
+VMEM_BYTES = 48 * 2**20
+QUICK = pl.CostEstimate(flops=1, bytes_accessed=1, transcendentals=0)
+AHEAD = 2
+
+CORE = [(0, 1), (1, 0), (2, 3), (3, 2)]
+CHIP = [(0, 2), (2, 0), (1, 3), (3, 1)]
+BOTH = [(0, 3), (3, 0), (1, 2), (2, 1)]
+NEXT, SKIP = CORE, CHIP
+PIECES = (32, 144, 80)
+STARTS = tuple(sum(PIECES[:k]) for k in range(len(PIECES)))
+TURNS = ((0, 1), (2,))
 
 
 def gelu_slope(value):
-    inner = ROOT * (value + 0.044715 * value * value * value)
+    inner = ROOT * (value + CUBE * value * value * value)
     tangent = jnp.tanh(inner)
     return 0.5 * (1.0 + tangent) + 0.5 * value * (1.0 - tangent * tangent) * ROOT * (
-        1.0 + 3.0 * 0.044715 * value * value
+        1.0 + 3.0 * CUBE * value * value
     )
 
 
@@ -41,6 +56,289 @@
         precision=lax.Precision.HIGHEST,
         preferred_element_type=jnp.float32,
     )
+
+
+def sample_weights(onehot, timestep, reward):
+    counts = jnp.sum(onehot, axis=1)
+    level = (timestep.astype(jnp.float32) + 0.5) / TSTEPS
+    return reward * (0.5 + 1.5 * level * (2.0 - level)) * lax.rsqrt(counts)
+
+
+def params(**more):
+    return pltpu.CompilerParams(vmem_limit_bytes=VMEM_BYTES, **more)
+
+
+def back_kernel(layout, tile, ordered, seeds, holds, *refs):
+    refs = list(refs)
+    order = refs.pop(0) if ordered else None
+    lefts = [[(place, refs.pop(0)) for place in places] for places in layout]
+    weights = [refs.pop(0) for _ in layout]
+    seed = refs.pop(0) if seeds else None
+    del refs[:holds]
+    left_sem, weight_sem, seed_sem = refs[-3:]
+    left_buf, weight_buf, total = refs[-6:-3]
+    outs = refs[:-6]
+
+    first, place = [], 0
+    for index, (start, size) in enumerate(seeds):
+        first.append(
+            pltpu.make_async_copy(
+                seed.at[pl.ds(start, size)], total.at[pl.ds(place, size)], seed_sem.at[index]
+            )
+        )
+        place += size
+    for copy in first:
+        copy.start()
+    tiles, column, number = [], 0, 0
+    for group, weight in zip(lefts, weights):
+        for low in range(0, weight.shape[1], tile):
+            span = pl.ds(column, tile)
+            copies = [
+                pltpu.make_async_copy(
+                    weight.at[:, pl.ds(low, tile)], weight_buf.at[:, span], weight_sem.at[column // tile]
+                )
+            ]
+            for place, left in group:
+                copies.append(
+                    pltpu.make_async_copy(
+                        left.at[:, pl.ds(low, tile)],
+                        left_buf.at[pl.ds(place, left.shape[0]), span],
+                        left_sem.at[number],
+                    )
+                )
+                number += 1
+            tiles.append((span, copies))
+            column += tile
+    start_tiles = lambda low, high: [copy.start() for _, copies in tiles[low:high] for copy in copies]
+    start_tiles(0, AHEAD)
+    for copy in first:
+        copy.wait()
+    for index, (span, copies) in enumerate(tiles):
+        start_tiles(index + AHEAD, index + AHEAD + 1)
+        for copy in copies:
+            copy.wait()
+        product = against_weight(left_buf[:, span], weight_buf[:, span])
+        if index or seeds:
+            total[...] += product
+        else:
+            total[...] = product
+    place = 0
+    for index, out in enumerate(outs):
+        size = out.shape[0]
+        if ordered:
+            place = pl.multiple_of(order[index] * size, size)
+        out[...] = total[pl.ds(place, size), :].astype(out.dtype)
+        place += size
+
+
+def back(groups, weights, sizes, dtype, tile=768, order=None, seed=None, seeds=(), hold=()):
+    width = weights[0].shape[0]
+    rows = sum(sizes)
+    depth = sum(weight.shape[1] for weight in weights)
+    layout = [[place for place, _ in group] for group in groups]
+    copies = sum(len(group) * (weight.shape[1] // tile) for group, weight in zip(groups, weights))
+    operands = [left for group in groups for _, left in group] + list(weights)
+    operands += ([] if seed is None else [seed]) + list(hold)
+    in_specs = [pl.BlockSpec(memory_space=pl.ANY)] * len(operands)
+    for index in range(len(weights)):
+        in_specs[sum(map(len, groups)) + index] = pl.BlockSpec(memory_space=pltpu.HBM)
+    if order is not None:
+        operands.insert(0, order)
+        in_specs.insert(0, pl.BlockSpec(memory_space=pltpu.SMEM))
+    return pl.pallas_call(
+        functools.partial(
+            back_kernel, layout, tile, order is not None, seeds, len(hold)
+        ),
+        in_specs=in_specs,
+        out_specs=[pl.BlockSpec(memory_space=pltpu.VMEM)] * len(sizes),
+        out_shape=[jax.ShapeDtypeStruct((size, width), dtype) for size in sizes],
+        scratch_shapes=[
+            pltpu.VMEM((rows, depth), jnp.bfloat16),
+            pltpu.VMEM((width, depth), jnp.bfloat16),
+            pltpu.VMEM((rows, width), jnp.float32),
+            pltpu.SemaphoreType.DMA((copies,)),
+            pltpu.SemaphoreType.DMA((depth // tile,)),
+            pltpu.SemaphoreType.DMA((max(1, len(seeds)),)),
+        ],
+        compiler_params=params(),
+        cost_estimate=QUICK,
+    )(*operands)
+
+
+def weight_kernel(count, holds, places, *refs):
+    parts, grads, (out, normed) = refs[:4], refs[4 : 4 + count], refs[-2:]
+
+    @pl.when(pl.program_id(0) == 0)
+    def _():
+        for index, part in enumerate(parts):
+            size = part.shape[0]
+            normed[pl.ds(pl.multiple_of(places[index] * size, size), size), :] = part[...]
+
+    joined = jnp.concatenate([grad[...] for grad in grads], axis=0)
+    out[...] = over_tokens(normed[...], joined).astype(out.dtype)
+
+
+def weight_grad(places, parts, grads, tile=768, low=0, high=None, held=None, hold=()):
+    width = parts[0].shape[1]
+    tokens = sum(part.shape[0] for part in parts)
+    columns = grads[0].shape[1]
+    high = columns // tile if high is None else high
+    extra = list(hold) + ([] if held is None else [held])
+    operands = [places] + list(parts) + list(grads) + extra
+    return pl.pallas_call(
+        functools.partial(weight_kernel, len(grads), len(extra)),
+        grid=(high - low,),
+        in_specs=[pl.BlockSpec(memory_space=pltpu.SMEM)]
+        + [pl.BlockSpec(part.shape, lambda i: (0, 0)) for part in parts]
+        + [pl.BlockSpec((grad.shape[0], tile), lambda i: (0, i + low)) for grad in grads]
+        + [pl.BlockSpec(memory_space=pl.ANY)] * len(extra),
+        out_specs=pl.BlockSpec((width, tile), lambda i: (0, i + low)),
+        out_shape=jax.ShapeDtypeStruct((width, columns), jnp.bfloat16),
+        scratch_shapes=[pltpu.VMEM((tokens, width), jnp.bfloat16)],
+        input_output_aliases={} if held is None else {len(operands) - 1: 0},
+        compiler_params=params(),
+        cost_estimate=QUICK,
+    )(*operands)
+
+
+def after(value, *others):
+    return lax.optimization_barrier((value, others))[0]
+
+
+def row_sum(pair):
+    return (
+        pair
+        + lax.ppermute(pair, "row", CORE)
+        + lax.ppermute(pair, "row", CHIP)
+        + lax.ppermute(pair, "row", BOTH)
+    )
+
+
+def on_grid(
+    latents,
+    modulation,
+    sample_of,
+    timestep,
+    reward,
+    qkv_cotangent,
+    mlp_cotangent,
+    mlp_preact,
+    w_qkv,
+    w_mlp,
+):
+    row_id = lax.axis_index("row")
+    col_id = lax.axis_index("col")
+    tok_col, width_row = latents.shape
+    tok_row = qkv_cotangent.shape[0]
+    samples = reward.shape[0]
+    own_first = (row_id ^ col_id) % 2
+    order = jnp.stack([own_first, 1 - own_first])
+
+    latents32 = latents.astype(jnp.float32)
+    moments = row_sum(
+        jnp.stack([jnp.sum(latents32, axis=1), jnp.sum(latents32 * latents32, axis=1)])
+    )
+
+    far_q = lax.ppermute(qkv_cotangent, "row", CHIP)
+    side_q = lax.ppermute(qkv_cotangent, "row", CORE)
+
+    sample_ids = jnp.arange(samples, dtype=jnp.int32)
+    onehot = (sample_ids[:, None] == sample_of[None, :]).astype(jnp.float32)
+    omega_sample = sample_weights(onehot, timestep, reward)
+    own_onehot = lax.dynamic_slice_in_dim(onehot, col_id * tok_col, tok_col, 1)
+    own_mod = lookup(own_onehot, modulation.reshape(samples, 2 * width_row))
+    own_omega = lookup(own_onehot, omega_sample[:, None])
+    offset = own_mod[:, :width_row]
+    scale = 1.0 + own_mod[:, width_row:]
+    mean = (moments[0] / MODEL_WIDTH)[:, None]
+    rstd = lax.rsqrt((moments[1] / MODEL_WIDTH)[:, None] - mean * mean + EPS)
+    xhat = (latents32 - mean) * rstd
+    normed = ((xhat * scale + offset) * own_omega).astype(jnp.bfloat16)
+    scale_omega = scale * own_omega
+    across = lax.ppermute(normed, "col", SKIP)
+    normed_next = lax.ppermute(normed, "col", NEXT)
+
+    mlp_preact = after(mlp_preact, normed)
+    own_m = [
+        (
+            mlp_cotangent[start : start + size].astype(jnp.float32)
+            * gelu_slope(mlp_preact[start : start + size].astype(jnp.float32))
+        ).astype(jnp.bfloat16)
+        for start, size in zip(STARTS, PIECES)
+    ]
+    side_m = [lax.ppermute(part, "row", CORE) for part in own_m]
+    far_m = [lax.ppermute(part, "row", CHIP) for part in own_m]
+
+    near_keep, near_send = back(
+        [
+            [(0, qkv_cotangent), (tok_row, side_q)],
+            [(start, part) for start, part in zip(STARTS, own_m)]
+            + [(tok_row + start, part) for start, part in zip(STARTS, side_m)],
+        ],
+        [w_qkv, w_mlp],
+        [tok_row, tok_row],
+        jnp.bfloat16,
+        order=order,
+        hold=[normed],
+    )
+    near_next = lax.ppermute(near_send, "col", NEXT)
+    across_next = lax.ppermute(after(across, near_send), "col", NEXT)
+
+    places = jnp.stack([row_id ^ col_id ^ j for j in (0, 2, 1, 3)])
+    parts = [normed, across, normed_next, across_next]
+
+    farside_q = lax.ppermute(after(far_q, near_send, across, normed_next, far_m[0]), "row", CORE)
+    far = back(
+        [[(0, far_q), (tok_row, farside_q)]],
+        [w_qkv],
+        [2 * tok_row],
+        jnp.float32,
+    )[0]
+    near_half = near_keep.astype(jnp.float32) + after(near_next, far).astype(jnp.float32)
+    takes_near = row_id // 2 == col_id // 2
+
+    qkv_total = weight_grad(
+        places, parts, [qkv_cotangent, side_q, far_q, farside_q], hold=[far]
+    )
+    farside_m, hold, halves = [], [qkv_total], []
+    for turn in TURNS:
+        for k in turn:
+            farside_m.append(lax.ppermute(after(far_m[k], hold), "row", CORE))
+        start, size = STARTS[turn[0]], sum(PIECES[k] for k in turn)
+        keep, send = back(
+            [
+                [(STARTS[k] - start, far_m[k]) for k in turn]
+                + [(size + STARTS[k] - start, farside_m[k]) for k in turn]
+            ],
+            [w_mlp],
+            [size, size],
+            jnp.bfloat16,
+            order=order,
+            seed=far,
+            seeds=((start, size), (tok_row + start, size)),
+            hold=hold,
+        )
+        hold = [keep]
+        halves.append((start, size, keep, lax.ppermute(send, "col", NEXT)))
+
+    all_m = own_m + side_m + far_m + farside_m
+    mlp_total = weight_grad(places, parts, all_m, hold=hold)
+
+    incoming = []
+    for start, size, keep, send in halves:
+        far_half = keep.astype(jnp.float32) + send.astype(jnp.float32)
+        near_piece = near_half[start : start + size]
+        own = jnp.where(takes_near, near_piece, far_half)
+        other = jnp.where(takes_near, far_half, near_piece).astype(jnp.bfloat16)
+        arrived = after(lax.ppermute(other, "col", SKIP), mlp_total)
+        incoming.append(own + arrived.astype(jnp.float32))
+    incoming = jnp.concatenate(incoming, axis=0) * scale_omega
+    own_terms = jnp.stack([jnp.sum(incoming, axis=1), jnp.sum(incoming * xhat, axis=1)])
+    terms = row_sum(own_terms) / MODEL_WIDTH
+    latent_input_gradient = rstd * (
+        incoming - terms[0][:, None] - xhat * terms[1][:, None]
+    )
+    return latent_input_gradient.astype(jnp.bfloat16), qkv_total, mlp_total
 
 
 def on_device(
@@ -63,14 +361,7 @@
     samples = reward.shape[0]
     sample_ids = jnp.arange(samples, dtype=jnp.int32)
     onehot = (sample_ids[:, None] == sample_of[None, :]).astype(jnp.float32)
-    counts = jnp.sum(onehot, axis=1)
-    levels = (jnp.arange(TSTEPS, dtype=jnp.float32) + 0.5) / TSTEPS
-    table = 0.5 + 1.5 * levels * (2.0 - levels)
-    level_hits = (timestep[:, None] == jnp.arange(TSTEPS, dtype=jnp.int32)[None, :]).astype(
-        jnp.float32
-    )
-    step_weight = jnp.sum(level_hits * table[None, :], axis=1)
-    omega_sample = reward * step_weight * lax.rsqrt(counts)
+    omega_sample = sample_weights(onehot, timestep, reward)
     omega_tokens = lookup(onehot, omega_sample[:, None])[:, 0]
     omega_rows = lax.dynamic_slice_in_dim(omega_tokens, row_id * tok_row, tok_row)[:, None]
     grad_q = (qkv_cotangent.astype(jnp.float32) * omega_rows).astype(jnp.bfloat16)
@@ -144,6 +435,11 @@
         P(("groups", "row"), "col"),
         P(("groups", "row"), "col"),
     )
+    small = mesh.shape["row"] == 4 and mesh.shape["col"] == 4
     return jax.shard_map(
-        on_device, mesh=mesh, in_specs=in_specs, out_specs=out_specs, check_vma=False
-    )
+        on_grid if small else on_device,
+        mesh=mesh,
+        in_specs=in_specs,
+        out_specs=out_specs,
+        check_vma=False,
+    )

time: 220 us -> 115 us (0.52)
  waiting for transfers between devices: 135 us -> 23.9 us
  Pallas kernels: 0 us -> 42.4 us
  matrix products: 39.5 us -> 0.96 us
  starting transfers between devices: 0.16 us -> 21.9 us
  blocking collectives: 13.6 us -> 0 us
  between operations: 13.8 us -> 1.03 us
  local copies, waits for them, and re-layouts: 1.52 us -> 13 us
  other arithmetic: 16.1 us -> 11.1 us
    all_gather x3 -> x0, waiting for transfers between devices: 112 us -> none  [the longest x1 40.7 us: on_device(): lax.all_gather(grad_m, 'row', axis=0, tiled=True)]
    pallas_call x0 -> x6, Pallas kernels: none -> 42.4 us  [the longest x4 26.3 us: back(): pl.pallas_call(functools.partial(back_kernel, layout, tile, order is not...]
    dot_general x4 -> x0, matrix products: 35.9 us -> none  [the longest x2 18.1 us: over_tokens(): lax.dot_general(left, right, (((0,), (0,)), ((), ())), preferred_element_...]
    ppermute x0 -> x26, waiting for transfers between devices: none -> 23.9 us  [the longest x2 6.31 us: on_grid(): arrived = after(lax.ppermute(other, 'col', SKIP), mlp_total)]
    reduce_scatter x1 -> x0, waiting for transfers between devices: 22.8 us -> none  [on_device(): lax.psum_scatter((against_weight(all_q, w_qkv) + against_weight(all_m, w_...]
    ppermute x0 -> x26, starting transfers between devices: none -> 21.9 us  [the longest x2 3.59 us: on_grid(): arrived = after(lax.ppermute(other, 'col', SKIP), mlp_total)]
    psum x2 -> x0, blocking collectives: 13.6 us -> none  [the longest x1 7.14 us: on_device(): lax.psum((jnp.sum(incoming_gradient, axis=1), jnp.sum(incoming_gradient *...]
    unnamed x7 -> x63, local copies, waits for them, and re-layouts: 1.44 us -> 13 us
  transfers between devices with their start and end apart: 4 -> 26, of which waited for: 4 -> 10; matrix products, arithmetic and copies ran while one was open for 8% -> 9% of each run, Pallas kernels for 0% -> 37%
where the time goes in v2:
time: 115 us; the launch traced here: 114 us
  Pallas kernels  42.4 us (37%)
  waiting for transfers between devices  23.9 us (21%)
  starting transfers between devices  21.9 us (19%)
  local copies, waits for them, and re-layouts  13 us (11%)
  other arithmetic  11.1 us (10%)
    pallas_call x4, Pallas kernels, back(): pl.pallas_call(functools.partial(back_kernel, layout, tile, order is not...  26.3 us
    pallas_call x2, Pallas kernels, weight_grad(): pl.pallas_call(functools.partial(weight_kernel, len(grads), len(extra)),...  16.1 us
    unnamed x63, local copies, waits for them, and re-layouts  13 us
    ppermute x2, waiting for transfers between devices, on_grid(): arrived = after(lax.ppermute(other, 'col', SKIP), mlp_total)  6.31 us
    ppermute x1, waiting for transfers between devices, on_grid(): across_next = lax.ppermute(after(across, near_send), 'col', NEXT)  4.19 us
    ppermute x2, waiting for transfers between devices, on_grid(): halves.append((start, size, keep, lax.ppermute(send, 'col', NEXT)))  3.88 us
    ppermute x2, starting transfers between devices, on_grid(): arrived = after(lax.ppermute(other, 'col', SKIP), mlp_total)  3.59 us
    ppermute x2, starting transfers between devices, row_sum(): lax.ppermute(pair, 'row', BOTH)  3.57 us
  transfers between devices with their start and end apart: 26, of which 10 were waited for; matrix products, arithmetic and copies ran while one was open for 9% of the time, Pallas kernels for 37%

profile of v2, /device:TPU:0, one launch (start us, length us, event | category | flops | bytes accessed | tf_op | source)
XLA Modules:
  0.0 114.3 jit_solution(10400361644704581862)
XLA Ops:
  0.7 1.3 %convert_reduce_fusion = (f32[256]{0:T(256)S(1)}, f32[256]{0:T(256)S(1)}) fusion(bf16[256,768]{1,0:T(8,128)(2,1)} %param.10), kind=kLoop, calls=%fused_computation.25 | loop fusion | flops 785920 | bytes 395264 | tf_op jit(solution)/shard_map/reduce_sum | solution.py:239
  1.9 2.4 %collective-permute-start.2 = (f32[2,256]{1,0:T(2,128)S(1)}, f32[2,256]{1,0:T(2,128)S(1)}, u32[]{:S(2)}, u32[]{:S(2)}) collective-permute-start(f32[2,256]{1,0:T(2,128)S(1)} %pad_maximum_fusion), channel_id=1, source_target_pairs={{0,12},{12,0},{4,8},{8,4},{1,13},{13,1},{5,9},{9,5},{2,14},{14,2},... | collective-permute-start | bytes 6152 | tf_op jit(solution)/shard_map/ppermute | solution.py:213
  5.5 1.4 %collective-permute-start.8 = (bf16[256,2304]{1,0:T(8,128)(2,1)}, bf16[256,2304]{1,0:T(8,128)(2,1)S(1)}, u32[]{:S(2)}, u32[]{:S(2)}) collective-permute-start(bf16[256,2304]{1,0:T(8,128)(2,1)} %refs_4_.1), channel_id=1, source_target_pairs={{0,8},{8,0},{4,12},{12,4},{1,9},{9,1},{5,13},{13,5},{2,10},{10,2},... | collective-permute-start | bytes 3538952 | tf_op jit(solution)/shard_map/ppermute | solution.py:242
  7.6 0.8 convert_reduce_fusion.1
  8.4 0.8 copy.13
  9.2 0.8 fusion.41
  12.0 1.2 %fusion.7.refs_4_.refs_5_ = bf16[144,3072]{1,0:T(8,128)(2,1)S(1)} fusion(bf16[256,3072]{1,0:T(8,128)(2,1)S(1)} %copy-done.25, bf16[256,3072]{1,0:T(8,128)(2,1)S(1)} %copy-done.26), kind=kLoop, calls=%fused_computation.21 | loop fusion | flops 9289728 | bytes 2654208 | tf_op jit(solution)/shard_map/convert_element_type | solution.py:266
  13.8 1.0 fusion.37.refs_3_.refs_4_
  14.9 2.0 %collective-permute-done.4.refs_6_.refs_7_ = bf16[32,3072]{1,0:T(8,128)(2,1)S(1)} collective-permute-done((bf16[32,3072]{1,0:T(8,128)(2,1)}, bf16[32,3072]{1,0:T(8,128)(2,1)S(1)}, u32[]{:S(2)}, u32[]{:S(2)}) %collective-permute-start.4) | collective-permute-done | bytes 196640 | tf_op jit(solution)/shard_map/ppermute | solution.py:269
  17.6 2.6 %collective-permute-start.9 = (bf16[256,768]{1,0:T(8,128)(2,1)S(1)}, bf16[256,768]{1,0:T(8,128)(2,1)}, u32[]{:S(2)}, u32[]{:S(2)}) collective-permute-start(bf16[256,768]{1,0:T(8,128)(2,1)S(1)} %fusion.25.refs_11_.refs_0_), channel_id=1, source_target_pairs={{0,2},{2,0},{1,3},{3,1},{4,6},{6,4},{5,7},{7,5},{8,10},{10,8},{9,1... | collective-permute-start | bytes 1179656 | tf_op jit(solution)/shard_map/ppermute | solution.py:258
  20.2 1.6 %collective-permute-start.10 = (bf16[256,768]{1,0:T(8,128)(2,1)S(1)}, bf16[256,768]{1,0:T(8,128)(2,1)}, u32[]{:S(2)}, u32[]{:S(2)}) collective-permute-start(bf16[256,768]{1,0:T(8,128)(2,1)S(1)} %fusion.25.refs_11_.refs_0_), channel_id=1, source_target_pairs={{0,1},{1,0},{2,3},{3,2},{4,5},{5,4},{6,7},{7,6},{8,9},{9,8},{10,11... | collective-permute-start | bytes 1179656 | tf_op jit(solution)/shard_map/ppermute | solution.py:259
  21.8 0.9 copy-done.7
  23.4 1.3 %copy-done.4 = bf16[256,2304]{1,0:T(8,128)(2,1)S(1)} copy-done((bf16[256,2304]{1,0:T(8,128)(2,1)S(1)}, bf16[256,2304]{1,0:T(8,128)(2,1)}, u32[]{:S(2)}) %copy-start.4) | copy-done | bytes 1179672
  24.7 1.2 %copy-done.8 = bf16[144,3072]{1,0:T(8,128)(2,1)S(1)} copy-done((bf16[144,3072]{1,0:T(8,128)(2,1)S(1)}, bf16[144,3072]{1,0:T(8,128)(2,1)}, u32[]{:S(2)}) %copy-start.8) | copy-done | bytes 884760
  25.9 0.9 copy-done.18
  26.8 10.6 %shard_map.121 = (bf16[256,768]{1,0:T(8,128)(2,1)S(1)}, bf16[256,768]{1,0:T(8,128)(2,1)}) custom-call(s32[2]{0:T(128)S(1)} %pad_add_fusion.refs_0_, bf16[256,2304]{1,0:T(8,128)(2,1)S(1)} %copy-done.4, bf16[256,2304]{1,0:T(8,128)(2,1)} %collective-permute-done.3.refs_2_.refs_5_, bf16[32,3072]{1,0:T(8,128)(2,1)} %fusion.37.refs_3_.refs_4_, ...), custom_call_target="tpu_custom_call" | custom-call | flops 1 | bytes 1 | tf_op jit(solution)/shard_map/pallas_call | solution.py:148
  37.4 0.8 copy-done.12
  38.2 0.8 copy-done.20
  39.1 1.5 %collective-permute-start.13 = (bf16[144,3072]{1,0:T(8,128)(2,1)S(1)}, bf16[144,3072]{1,0:T(8,128)(2,1)}, u32[]{:S(2)}, u32[]{:S(2)}) collective-permute-start(bf16[144,3072]{1,0:T(8,128)(2,1)S(1)} %fusion.7.refs_4_.refs_5_), channel_id=1, source_target_pairs={{0,8},{8,0},{4,12},{12,4},{1,9},{9,1},{5,13},{13,5},{2,10},{10,2},... | collective-permute-start | bytes 2654216 | tf_op jit(solution)/shard_map/ppermute | solution.py:270
  40.6 0.9 collective-permute-start.14
  42.1 4.5 %shard_map.122.refs_8_.refs_6_.refs_4_ = f32[512,768]{1,0:T(8,128)S(1)} custom-call(bf16[256,2304]{1,0:T(8,128)(2,1)S(1)} %collective-permute-done.8.refs_0_.refs_6_, bf16[256,2304]{1,0:T(8,128)(2,1)} %collective-permute-done.12.refs_1_.refs_7_, bf16[768,2304]{1,0:T(8,128)(2,1)} %refs_2_.1), custom_call_target="tpu_custom_call" | custom-call | flops 1 | bytes 1 | tf_op jit(solution)/shard_map/pallas_call | solution.py:148
  46.6 1.1 copy-done
  47.8 4.2 %collective-permute-done.14.refs_3_ = bf16[256,768]{1,0:T(8,128)(2,1)S(1)} collective-permute-done((bf16[256,768]{1,0:T(8,128)(2,1)}, bf16[256,768]{1,0:T(8,128)(2,1)S(1)}, u32[]{:S(2)}, u32[]{:S(2)}) %collective-permute-start.14) | collective-permute-done | bytes 393248 | tf_op jit(solution)/shard_map/ppermute | solution.py:285
  52.0 0.7 copy-done.14
  52.7 1.3 %copy-done.3 = bf16[256,2304]{1,0:T(8,128)(2,1)S(1)} copy-done((bf16[256,2304]{1,0:T(8,128)(2,1)S(1)}, bf16[256,2304]{1,0:T(8,128)(2,1)}, u32[]{:S(2)}) %copy-start.3) | copy-done | bytes 1179672
  54.0 1.0 copy-done.15
  55.0 7.1 %shard_map.123.refs_7_ = bf16[768,2304]{1,0:T(8,128)(2,1)} custom-call(s32[4]{0:T(128)S(1)} %pad_add_fusion.1.places, bf16[256,768]{1,0:T(8,128)(2,1)S(1)} %fusion.25.refs_11_.refs_0_, bf16[256,768]{1,0:T(8,128)(2,1)} %collective-permute-done.9.refs_1_, bf16[256,768]{1,0:T(8,128)(2,1)} %collective-permute-done.10.refs_2_, bf16[256,768]{1,0:T(8,128)(2,1)S(1)} %copy-done.15, ...), custom_call_target="tpu_custom_call" | custom-call | flops 1 | bytes 1 | tf_op jit(solution)/shard_map/pallas_call | solution.py:188
  62.8 0.8 collective-permute-start.7
  63.6 1.6 %collective-permute-done.15.refs_3_.refs_13_ = bf16[32,3072]{1,0:T(8,128)(2,1)S(1)} collective-permute-done((bf16[32,3072]{1,0:T(8,128)(2,1)}, bf16[32,3072]{1,0:T(8,128)(2,1)S(1)}, u32[]{:S(2)}, u32[]{:S(2)}) %collective-permute-start.15) | collective-permute-done | bytes 196640 | tf_op jit(solution)/shard_map/ppermute | solution.py:306
  65.3 6.0 %shard_map.124 = (bf16[176,768]{1,0:T(8,128)(2,1)S(1)}, bf16[176,768]{1,0:T(8,128)(2,1)}) custom-call(s32[2]{0:T(128)S(1)} %pad_add_fusion.refs_0_, bf16[32,3072]{1,0:T(8,128)(2,1)} %collective-permute-done.11.refs_1_.refs_10_, bf16[144,3072]{1,0:T(8,128)(2,1)} %collective-permute-done.13.refs_2_.refs_11_, ...), custom_call_target="tpu_custom_call" | custom-call | flops 1 | bytes 1 | tf_op jit(solution)/shard_map/pallas_call | solution.py:148
  71.3 0.7 copy-done.10
  72.1 1.2 %collective-permute-start.17 = (bf16[176,768]{1,0:T(8,128)(2,1)}, bf16[176,768]{1,0:T(8,128)(2,1)}, u32[]{:S(2)}, u32[]{:S(2)}) collective-permute-start(bf16[176,768]{1,0:T(8,128)(2,1)} %get-tuple-element.27), channel_id=1, source_target_pairs={{0,1},{1,0},{2,3},{3,2},{4,5},{5,4},{6,7},{7,6},{8,9},{9,8},{10,11... | collective-permute-start | bytes 811016 | tf_op jit(solution)/shard_map/ppermute | solution.py:322
  73.2 1.0 collective-permute-done.7
  74.3 1.5 %collective-permute-done.19.refs_1_.refs_12_ = bf16[80,3072]{1,0:T(8,128)(2,1)} collective-permute-done((bf16[80,3072]{1,0:T(8,128)(2,1)S(1)}, bf16[80,3072]{1,0:T(8,128)(2,1)}, u32[]{:S(2)}, u32[]{:S(2)}) %collective-permute-start.19) | collective-permute-done | bytes 491552 | tf_op jit(solution)/shard_map/ppermute | solution.py:270
  75.8 1.2 %convert_add_fusion.3 = f32[256,768]{1,0:T(8,128)S(1)} fusion(bf16[256,768]{1,0:T(8,128)(2,1)} %collective-permute-done.7, bf16[256,768]{1,0:T(8,128)(2,1)} %copy-done.20), kind=kLoop, calls=%fused_computation.56 | loop fusion | flops 589824 | bytes 1572864 | tf_op jit(solution)/shard_map/add | solution.py:297
  77.0 3.9 %collective-permute-done.17 = bf16[176,768]{1,0:T(8,128)(2,1)} collective-permute-done((bf16[176,768]{1,0:T(8,128)(2,1)}, bf16[176,768]{1,0:T(8,128)(2,1)}, u32[]{:S(2)}, u32[]{:S(2)}) %collective-permute-start.17) | collective-permute-done | bytes 270368 | tf_op jit(solution)/shard_map/ppermute | solution.py:322
  80.9 1.1 select_convert_fusion
  82.1 2.7 %collective-permute-start.18 = (bf16[176,768]{1,0:T(8,128)(2,1)S(1)}, bf16[176,768]{1,0:T(8,128)(2,1)S(1)}, u32[]{:S(2)}, u32[]{:S(2)}) collective-permute-start(bf16[176,768]{1,0:T(8,128)(2,1)S(1)} %select_convert_fusion), channel_id=1, source_target_pairs={{0,2},{2,0},{1,3},{3,1},{4,6},{6,4},{5,7},{7,5},{8,10},{10,8},{9,1... | collective-permute-start | bytes 811016 | tf_op jit(solution)/shard_map/ppermute | solution.py:333
  84.7 5.2 %shard_map.125 = (bf16[80,768]{1,0:T(8,128)(2,1)S(1)}, bf16[80,768]{1,0:T(8,128)(2,1)S(1)}) custom-call(s32[2]{0:T(128)S(1)} %pad_add_fusion.refs_0_, bf16[80,3072]{1,0:T(8,128)(2,1)} %collective-permute-done.19.refs_1_.refs_12_, bf16[80,3072]{1,0:T(8,128)(2,1)S(1)} %collective-permute-done.20.refs_2_.refs_15_, bf16[768,3072]{1,0:T(8,128)(2,1)} %refs_3_.1, ...), custom_call_target="tpu_custom_call" | custom-call | flops 1 | bytes 1 | tf_op jit(solution)/shard_map/pallas_call | solution.py:148
  89.9 0.7 collective-permute-start.21
  90.6 9.0 %shard_map.126 = bf16[768,3072]{1,0:T(8,128)(2,1)} custom-call(s32[4]{0:T(128)S(1)} %pad_add_fusion.1.places, bf16[256,768]{1,0:T(8,128)(2,1)S(1)} %fusion.25.refs_11_.refs_0_, bf16[256,768]{1,0:T(8,128)(2,1)} %collective-permute-done.9.refs_1_, bf16[256,768]{1,0:T(8,128)(2,1)} %collective-permute-done.10.refs_2_, bf16[256,768]{1,0:T(8,128)(2,1)S(1)} %copy-done.16, ...), custom_call_target="tpu_custom_call" | custom-call | flops 1 | bytes 1 | tf_op jit(solution)/shard_map/pallas_call | solution.py:188
  99.7 0.9 collective-permute-start.22
  100.6 1.1 convert_add_fusion.4
  101.7 6.3 %collective-permute-done.22 = bf16[80,768]{1,0:T(8,128)(2,1)S(1)} collective-permute-done((bf16[80,768]{1,0:T(8,128)(2,1)S(1)}, bf16[80,768]{1,0:T(8,128)(2,1)S(1)}, u32[]{:S(2)}, u32[]{:S(2)}) %collective-permute-start.22) | collective-permute-done | bytes 122912 | tf_op jit(solution)/shard_map/ppermute | solution.py:333
  108.6 1.1 collective-permute-start.25
  110.5 1.1 %collective-permute-done.25 = f32[2,256]{1,0:T(2,128)S(1)} collective-permute-done((f32[2,256]{1,0:T(2,128)S(1)}, f32[2,256]{1,0:T(2,128)S(1)}, u32[]{:S(2)}, u32[]{:S(2)}) %collective-permute-start.25) | collective-permute-done | bytes 2080 | tf_op jit(solution)/shard_map/ppermute | solution.py:213
  111.7 1.6 %collective-permute-done.24 = f32[2,256]{1,0:T(2,128)S(1)} collective-permute-done((f32[2,256]{1,0:T(2,128)S(1)}, f32[2,256]{1,0:T(2,128)S(1)}, u32[]{:S(2)}, u32[]{:S(2)}) %collective-permute-start.24) | collective-permute-done | bytes 2080 | tf_op jit(solution)/shard_map/ppermute | solution.py:212
  113.3 1.0 fusion.29
  (98 shorter events, 8.7 us)
Async XLA Ops:
  0.6 9.7 %copy-start.23 = (bf16[256,768]{1,0:T(8,128)(2,1)S(1)}, bf16[256,768]{1,0:T(8,128)(2,1)}, u32[]{:S(2)}) copy-start(bf16[256,768]{1,0:T(8,128)(2,1)} %param.10) | copy-start | bytes 1179652
  0.6 9.4 %copy-start.29 = (f32[8]{0:T(128)S(1)}, f32[8]{0:T(128)}, u32[]{:S(2)}) copy-start(f32[8]{0:T(128)} %param.14) | copy-start | bytes 100
  0.7 9.4 %copy-start.30 = (s32[8]{0:T(128)S(1)}, s32[8]{0:T(128)}, u32[]{:S(2)}) copy-start(s32[8]{0:T(128)} %param.13) | copy-start | bytes 100
  1.9 8.3 %collective-permute-start.2 = (f32[2,256]{1,0:T(2,128)S(1)}, f32[2,256]{1,0:T(2,128)S(1)}, u32[]{:S(2)}, u32[]{:S(2)}) collective-permute-start(f32[2,256]{1,0:T(2,128)S(1)} %pad_maximum_fusion), channel_id=1, source_target_pairs={{0,12},{12,0},{4,8},{8,4},{1,13},{13,1},{5,9},{9,5},{2,14},{14,2},... | collective-permute-start | bytes 6152 | tf_op jit(solution)/shard_map/ppermute | solution.py:213
  4.4 5.9 %collective-permute-start.1 = (f32[2,256]{1,0:T(2,128)S(1)}, f32[2,256]{1,0:T(2,128)S(1)}, u32[]{:S(2)}, u32[]{:S(2)}) collective-permute-start(f32[2,256]{1,0:T(2,128)S(1)} %pad_maximum_fusion), channel_id=1, source_target_pairs={{0,8},{8,0},{4,12},{12,4},{1,9},{9,1},{5,13},{13,5},{2,10},{10,2},... | collective-permute-start | bytes 6152 | tf_op jit(solution)/shard_map/ppermute | solution.py:212
  5.0 5.2 %collective-permute-start = (f32[2,256]{1,0:T(2,128)S(1)}, f32[2,256]{1,0:T(2,128)S(1)}, u32[]{:S(2)}, u32[]{:S(2)}) collective-permute-start(f32[2,256]{1,0:T(2,128)S(1)} %pad_maximum_fusion), channel_id=1, source_target_pairs={{0,4},{4,0},{8,12},{12,8},{1,5},{5,1},{9,13},{13,9},{2,6},{6,2},{1... | collective-permute-start | bytes 6152 | tf_op jit(solution)/shard_map/ppermute | solution.py:211
  5.1 18.3 %collective-permute-start.3 = (bf16[256,2304]{1,0:T(8,128)(2,1)}, bf16[256,2304]{1,0:T(8,128)(2,1)}, u32[]{:S(2)}, u32[]{:S(2)}) collective-permute-start(bf16[256,2304]{1,0:T(8,128)(2,1)} %refs_4_.1), channel_id=1, source_target_pairs={{0,4},{4,0},{8,12},{12,8},{1,5},{5,1},{9,13},{13,9},{2,6},{6,2},{1... | collective-permute-start | bytes 3538952 | tf_op jit(solution)/shard_map/ppermute | solution.py:243
  5.5 33.5 %collective-permute-start.8 = (bf16[256,2304]{1,0:T(8,128)(2,1)}, bf16[256,2304]{1,0:T(8,128)(2,1)S(1)}, u32[]{:S(2)}, u32[]{:S(2)}) collective-permute-start(bf16[256,2304]{1,0:T(8,128)(2,1)} %refs_4_.1), channel_id=1, source_target_pairs={{0,8},{8,0},{4,12},{12,4},{1,9},{9,1},{5,13},{13,5},{2,10},{10,2},... | collective-permute-start | bytes 3538952 | tf_op jit(solution)/shard_map/ppermute | solution.py:242
  9.2 2.1 %copy-start.25 = (bf16[256,3072]{1,0:T(8,128)(2,1)S(1)}, bf16[256,3072]{1,0:T(8,128)(2,1)}, u32[]{:S(2)}) copy-start(bf16[256,3072]{1,0:T(8,128)(2,1)} %param.17) | copy-start | bytes 4718596
  9.2 2.1 %copy-start.26 = (bf16[256,3072]{1,0:T(8,128)(2,1)S(1)}, bf16[256,3072]{1,0:T(8,128)(2,1)}, u32[]{:S(2)}) copy-start(bf16[256,3072]{1,0:T(8,128)(2,1)} %param.16) | copy-start | bytes 4718596
  10.1 1.2 %copy-start.21 = (f32[256,1536]{1,0:T(8,128)}, f32[256,1536]{1,0:T(8,128)S(1)}, u32[]{:S(2)}) copy-start(f32[256,1536]{1,0:T(8,128)S(1)} %fusion.41) | copy-start | bytes 4718596
  13.2 8.5 %collective-permute-start.5 = (bf16[144,3072]{1,0:T(8,128)(2,1)S(1)}, bf16[144,3072]{1,0:T(8,128)(2,1)S(1)}, u32[]{:S(2)}, u32[]{:S(2)}) collective-permute-start(bf16[144,3072]{1,0:T(8,128)(2,1)S(1)} %fusion.7.refs_4_.refs_5_), channel_id=1, source_target_pairs={{0,4},{4,0},{8,12},{12,8},{1,5},{5,1},{9,13},{13,9},{2,6},{6,2},{1... | collective-permute-start | bytes 2654216 | tf_op jit(solution)/shard_map/ppermute | solution.py:269
  13.4 6.7 %collective-permute-start.6 = (bf16[80,3072]{1,0:T(8,128)(2,1)S(1)}, bf16[80,3072]{1,0:T(8,128)(2,1)S(1)}, u32[]{:S(2)}, u32[]{:S(2)}) collective-permute-start(bf16[80,3072]{1,0:T(8,128)(2,1)S(1)} %fusion.16.refs_5_.refs_6_), channel_id=1, source_target_pairs={{0,4},{4,0},{8,12},{12,8},{1,5},{5,1},{9,13},{13,9},{2,6},{6,2},{1... | collective-permute-start | bytes 1474568 | tf_op jit(solution)/shard_map/ppermute | solution.py:269
  14.8 2.1 %collective-permute-start.4 = (bf16[32,3072]{1,0:T(8,128)(2,1)}, bf16[32,3072]{1,0:T(8,128)(2,1)S(1)}, u32[]{:S(2)}, u32[]{:S(2)}) collective-permute-start(bf16[32,3072]{1,0:T(8,128)(2,1)} %fusion.37.refs_3_.refs_4_), channel_id=1, source_target_pairs={{0,4},{4,0},{8,12},{12,8},{1,5},{5,1},{9,13},{13,9},{2,6},{6,2},{1... | collective-permute-start | bytes 589832 | tf_op jit(solution)/shard_map/ppermute | solution.py:269
  17.6 21.4 %collective-permute-start.9 = (bf16[256,768]{1,0:T(8,128)(2,1)S(1)}, bf16[256,768]{1,0:T(8,128)(2,1)}, u32[]{:S(2)}, u32[]{:S(2)}) collective-permute-start(bf16[256,768]{1,0:T(8,128)(2,1)S(1)} %fusion.25.refs_11_.refs_0_), channel_id=1, source_target_pairs={{0,2},{2,0},{1,3},{3,1},{4,6},{6,4},{5,7},{7,5},{8,10},{10,8},{9,1... | collective-permute-start | bytes 1179656 | tf_op jit(solution)/shard_map/ppermute | solution.py:258
  20.2 18.8 %collective-permute-start.10 = (bf16[256,768]{1,0:T(8,128)(2,1)S(1)}, bf16[256,768]{1,0:T(8,128)(2,1)}, u32[]{:S(2)}, u32[]{:S(2)}) collective-permute-start(bf16[256,768]{1,0:T(8,128)(2,1)S(1)} %fusion.25.refs_11_.refs_0_), channel_id=1, source_target_pairs={{0,1},{1,0},{2,3},{3,2},{4,5},{5,4},{6,7},{7,6},{8,9},{9,8},{10,11... | collective-permute-start | bytes 1179656 | tf_op jit(solution)/shard_map/ppermute | solution.py:259
  22.7 16.3 %collective-permute-start.11 = (bf16[32,3072]{1,0:T(8,128)(2,1)}, bf16[32,3072]{1,0:T(8,128)(2,1)}, u32[]{:S(2)}, u32[]{:S(2)}) collective-permute-start(bf16[32,3072]{1,0:T(8,128)(2,1)} %fusion.37.refs_3_.refs_4_), channel_id=1, source_target_pairs={{0,8},{8,0},{4,12},{12,4},{1,9},{9,1},{5,13},{13,5},{2,10},{10,2},... | collective-permute-start | bytes 589832 | tf_op jit(solution)/shard_map/ppermute | solution.py:270
  23.4 1.3 %copy-start.4 = (bf16[256,2304]{1,0:T(8,128)(2,1)S(1)}, bf16[256,2304]{1,0:T(8,128)(2,1)}, u32[]{:S(2)}) copy-start(bf16[256,2304]{1,0:T(8,128)(2,1)} %refs_4_.1) | copy-start | bytes 3538948
  24.7 1.2 %copy-start.8 = (bf16[144,3072]{1,0:T(8,128)(2,1)S(1)}, bf16[144,3072]{1,0:T(8,128)(2,1)}, u32[]{:S(2)}) copy-start(bf16[144,3072]{1,0:T(8,128)(2,1)} %copy-done.7) | copy-start | bytes 2654212
  39.0 7.6 %copy-start.2 = (bf16[256,2304]{1,0:T(8,128)(2,1)}, bf16[256,2304]{1,0:T(8,128)(2,1)S(1)}, u32[]{:S(2)}) copy-start(bf16[256,2304]{1,0:T(8,128)(2,1)S(1)} %collective-permute-done.8.refs_0_.refs_6_) | copy-start | bytes 3538948
  39.0 3.0 %collective-permute-start.12 = (bf16[256,2304]{1,0:T(8,128)(2,1)S(1)}, bf16[256,2304]{1,0:T(8,128)(2,1)}, u32[]{:S(2)}, u32[]{:S(2)}) collective-permute-start(bf16[256,2304]{1,0:T(8,128)(2,1)S(1)} %collective-permute-done.8.refs_0_.refs_6_), channel_id=1, source_target_pairs={{0,4},{4,0},{8,12},{12,8},{1,5},{5,1},{9,13},{13,9},{2,6},{6,2},{1... | collective-permute-start | bytes 3538952 | tf_op jit(solution)/shard_map/ppermute | solution.py:290
  39.1 22.9 %collective-permute-start.13 = (bf16[144,3072]{1,0:T(8,128)(2,1)S(1)}, bf16[144,3072]{1,0:T(8,128)(2,1)}, u32[]{:S(2)}, u32[]{:S(2)}) collective-permute-start(bf16[144,3072]{1,0:T(8,128)(2,1)S(1)} %fusion.7.refs_4_.refs_5_), channel_id=1, source_target_pairs={{0,8},{8,0},{4,12},{12,4},{1,9},{9,1},{5,13},{13,5},{2,10},{10,2},... | collective-permute-start | bytes 2654216 | tf_op jit(solution)/shard_map/ppermute | solution.py:270
  40.6 11.4 %collective-permute-start.14 = (bf16[256,768]{1,0:T(8,128)(2,1)}, bf16[256,768]{1,0:T(8,128)(2,1)S(1)}, u32[]{:S(2)}, u32[]{:S(2)}) collective-permute-start(bf16[256,768]{1,0:T(8,128)(2,1)} %collective-permute-done.9.refs_1_), channel_id=1, source_target_pairs={{0,1},{1,0},{2,3},{3,2},{4,5},{5,4},{6,7},{7,6},{8,9},{9,8},{10,11... | collective-permute-start | bytes 1179656 | tf_op jit(solution)/shard_map/ppermute | solution.py:285
  41.6 11.1 %copy-start.5 = (bf16[256,2304]{1,0:T(8,128)(2,1)S(1)}, bf16[256,2304]{1,0:T(8,128)(2,1)}, u32[]{:S(2)}) copy-start(bf16[256,2304]{1,0:T(8,128)(2,1)} %refs_4_.1) | copy-start | bytes 3538948
  46.6 1.1 %copy-start = (f32[512,768]{1,0:T(8,128)}, f32[512,768]{1,0:T(8,128)S(1)}, u32[]{:S(2)}) copy-start(f32[512,768]{1,0:T(8,128)S(1)} %shard_map.122.refs_8_.refs_6_.refs_4_) | copy-start | bytes 4718596
  52.7 1.3 %copy-start.3 = (bf16[256,2304]{1,0:T(8,128)(2,1)S(1)}, bf16[256,2304]{1,0:T(8,128)(2,1)}, u32[]{:S(2)}) copy-start(bf16[256,2304]{1,0:T(8,128)(2,1)} %copy-done.2) | copy-start | bytes 3538948
  55.0 10.3 %copy-start.1 = (f32[512,768]{1,0:T(8,128)S(1)}, f32[512,768]{1,0:T(8,128)}, u32[]{:S(2)}) copy-start(f32[512,768]{1,0:T(8,128)} %copy-done) | copy-start | bytes 4718596
  62.1 3.2 %collective-permute-start.16 = (bf16[144,3072]{1,0:T(8,128)(2,1)}, bf16[144,3072]{1,0:T(8,128)(2,1)S(1)}, u32[]{:S(2)}, u32[]{:S(2)}) collective-permute-start(bf16[144,3072]{1,0:T(8,128)(2,1)} %collective-permute-done.13.refs_2_.refs_11_), channel_id=1, source_target_pairs={{0,4},{4,0},{8,12},{12,8},{1,5},{5,1},{9,13},{13,9},{2,6},{6,2},{1... | collective-permute-start | bytes 2654216 | tf_op jit(solution)/shard_map/ppermute | solution.py:306
  62.1 13.7 %collective-permute-start.19 = (bf16[80,3072]{1,0:T(8,128)(2,1)S(1)}, bf16[80,3072]{1,0:T(8,128)(2,1)}, u32[]{:S(2)}, u32[]{:S(2)}) collective-permute-start(bf16[80,3072]{1,0:T(8,128)(2,1)S(1)} %fusion.16.refs_5_.refs_6_), channel_id=1, source_target_pairs={{0,8},{8,0},{4,12},{12,4},{1,9},{9,1},{5,13},{13,5},{2,10},{10,2},... | collective-permute-start | bytes 1474568 | tf_op jit(solution)/shard_map/ppermute | solution.py:270
  62.8 11.5 %collective-permute-start.7 = (bf16[256,768]{1,0:T(8,128)(2,1)}, bf16[256,768]{1,0:T(8,128)(2,1)}, u32[]{:S(2)}, u32[]{:S(2)}) collective-permute-start(bf16[256,768]{1,0:T(8,128)(2,1)} %get-tuple-element.20), channel_id=1, source_target_pairs={{0,1},{1,0},{2,3},{3,2},{4,5},{5,4},{6,7},{7,6},{8,9},{9,8},{10,11... | collective-permute-start | bytes 1179656 | tf_op jit(solution)/shard_map/ppermute | solution.py:284
  63.6 1.7 %collective-permute-start.15 = (bf16[32,3072]{1,0:T(8,128)(2,1)}, bf16[32,3072]{1,0:T(8,128)(2,1)S(1)}, u32[]{:S(2)}, u32[]{:S(2)}) collective-permute-start(bf16[32,3072]{1,0:T(8,128)(2,1)} %collective-permute-done.11.refs_1_.refs_10_), channel_id=1, source_target_pairs={{0,4},{4,0},{8,12},{12,8},{1,5},{5,1},{9,13},{13,9},{2,6},{6,2},{1... | collective-permute-start | bytes 589832 | tf_op jit(solution)/shard_map/ppermute | solution.py:306
  65.3 6.1 %copy-start.6 = (bf16[144,3072]{1,0:T(8,128)(2,1)}, bf16[144,3072]{1,0:T(8,128)(2,1)S(1)}, u32[]{:S(2)}) copy-start(bf16[144,3072]{1,0:T(8,128)(2,1)S(1)} %collective-permute-done.16.refs_4_.refs_14_) | copy-start | bytes 2654212
  72.1 8.8 %collective-permute-start.17 = (bf16[176,768]{1,0:T(8,128)(2,1)}, bf16[176,768]{1,0:T(8,128)(2,1)}, u32[]{:S(2)}, u32[]{:S(2)}) collective-permute-start(bf16[176,768]{1,0:T(8,128)(2,1)} %get-tuple-element.27), channel_id=1, source_target_pairs={{0,1},{1,0},{2,3},{3,2},{4,5},{5,4},{6,7},{7,6},{8,9},{9,8},{10,11... | collective-permute-start | bytes 811016 | tf_op jit(solution)/shard_map/ppermute | solution.py:322
  73.2 11.5 %copy-start.11 = (bf16[176,768]{1,0:T(8,128)(2,1)S(1)}, bf16[176,768]{1,0:T(8,128)(2,1)}, u32[]{:S(2)}) copy-start(bf16[176,768]{1,0:T(8,128)(2,1)} %copy-done.10) | copy-start | bytes 811012
  75.8 8.9 %collective-permute-start.20 = (bf16[80,3072]{1,0:T(8,128)(2,1)}, bf16[80,3072]{1,0:T(8,128)(2,1)S(1)}, u32[]{:S(2)}, u32[]{:S(2)}) collective-permute-start(bf16[80,3072]{1,0:T(8,128)(2,1)} %collective-permute-done.19.refs_1_.refs_12_), channel_id=1, source_target_pairs={{0,4},{4,0},{8,12},{12,8},{1,5},{5,1},{9,13},{13,9},{2,6},{6,2},{1... | collective-permute-start | bytes 1474568 | tf_op jit(solution)/shard_map/ppermute | solution.py:306
  82.0 8.6 %copy-start.9 = (bf16[144,3072]{1,0:T(8,128)(2,1)S(1)}, bf16[144,3072]{1,0:T(8,128)(2,1)}, u32[]{:S(2)}) copy-start(bf16[144,3072]{1,0:T(8,128)(2,1)} %copy-done.7) | copy-start | bytes 2654212
  82.0 8.6 %copy-start.13 = (bf16[80,3072]{1,0:T(8,128)(2,1)S(1)}, bf16[80,3072]{1,0:T(8,128)(2,1)}, u32[]{:S(2)}) copy-start(bf16[80,3072]{1,0:T(8,128)(2,1)} %copy-done.12) | copy-start | bytes 1474564
  82.0 8.6 %copy-start.16 = (bf16[256,768]{1,0:T(8,128)(2,1)S(1)}, bf16[256,768]{1,0:T(8,128)(2,1)}, u32[]{:S(2)}) copy-start(bf16[256,768]{1,0:T(8,128)(2,1)} %copy-done.14) | copy-start | bytes 1179652
  82.0 8.6 %copy-start.19 = (bf16[32,3072]{1,0:T(8,128)(2,1)S(1)}, bf16[32,3072]{1,0:T(8,128)(2,1)}, u32[]{:S(2)}) copy-start(bf16[32,3072]{1,0:T(8,128)(2,1)} %copy-done.17) | copy-start | bytes 589828
  82.1 17.6 %collective-permute-start.18 = (bf16[176,768]{1,0:T(8,128)(2,1)S(1)}, bf16[176,768]{1,0:T(8,128)(2,1)S(1)}, u32[]{:S(2)}, u32[]{:S(2)}) collective-permute-start(bf16[176,768]{1,0:T(8,128)(2,1)S(1)} %select_convert_fusion), channel_id=1, source_target_pairs={{0,2},{2,0},{1,3},{3,1},{4,6},{6,4},{5,7},{7,5},{8,10},{10,8},{9,1... | collective-permute-start | bytes 811016 | tf_op jit(solution)/shard_map/ppermute | solution.py:333
  89.9 9.8 %collective-permute-start.21 = (bf16[80,768]{1,0:T(8,128)(2,1)S(1)}, bf16[80,768]{1,0:T(8,128)(2,1)S(1)}, u32[]{:S(2)}, u32[]{:S(2)}) collective-permute-start(bf16[80,768]{1,0:T(8,128)(2,1)S(1)} %get-tuple-element.31), channel_id=1, source_target_pairs={{0,1},{1,0},{2,3},{3,2},{4,5},{5,4},{6,7},{7,6},{8,9},{9,8},{10,11... | collective-permute-start | bytes 368648 | tf_op jit(solution)/shard_map/ppermute | solution.py:322
  99.6 8.5 %copy-start.22 = (f32[256,1536]{1,0:T(8,128)S(1)}, f32[256,1536]{1,0:T(8,128)}, u32[]{:S(2)}) copy-start(f32[256,1536]{1,0:T(8,128)} %copy-done.21) | copy-start | bytes 4718596
  99.6 8.5 %copy-start.24 = (bf16[256,768]{1,0:T(8,128)(2,1)S(1)}, bf16[256,768]{1,0:T(8,128)(2,1)}, u32[]{:S(2)}) copy-start(bf16[256,768]{1,0:T(8,128)(2,1)} %param.10) | copy-start | bytes 1179652
  99.6 8.5 %copy-start.28 = (f32[1,256]{1,0:T(1,128)S(1)}, f32[1,256]{1,0:T(1,128)}, u32[]{:S(2)}) copy-start(f32[1,256]{1,0:T(1,128)} %copy-done.27) | copy-start | bytes 3076
  99.7 8.3 %collective-permute-start.22 = (bf16[80,768]{1,0:T(8,128)(2,1)S(1)}, bf16[80,768]{1,0:T(8,128)(2,1)S(1)}, u32[]{:S(2)}, u32[]{:S(2)}) collective-permute-start(bf16[80,768]{1,0:T(8,128)(2,1)S(1)} %select_convert_fusion.1), channel_id=1, source_target_pairs={{0,2},{2,0},{1,3},{3,1},{4,6},{6,4},{5,7},{7,5},{8,10},{10,8},{9,1... | collective-permute-start | bytes 368648 | tf_op jit(solution)/shard_map/ppermute | solution.py:333
  108.6 3.1 %collective-permute-start.25 = (f32[2,256]{1,0:T(2,128)S(1)}, f32[2,256]{1,0:T(2,128)S(1)}, u32[]{:S(2)}, u32[]{:S(2)}) collective-permute-start(f32[2,256]{1,0:T(2,128)S(1)} %pad_maximum_fusion.1), channel_id=1, source_target_pairs={{0,12},{12,0},{4,8},{8,4},{1,13},{13,1},{5,9},{9,5},{2,14},{14,2},... | collective-permute-start | bytes 6152 | tf_op jit(solution)/shard_map/ppermute | solution.py:213
  109.7 3.6 %collective-permute-start.24 = (f32[2,256]{1,0:T(2,128)S(1)}, f32[2,256]{1,0:T(2,128)S(1)}, u32[]{:S(2)}, u32[]{:S(2)}) collective-permute-start(f32[2,256]{1,0:T(2,128)S(1)} %pad_maximum_fusion.1), channel_id=1, source_target_pairs={{0,8},{8,0},{4,12},{12,4},{1,9},{9,1},{5,13},{13,5},{2,10},{10,2},... | collective-permute-start | bytes 6152 | tf_op jit(solution)/shard_map/ppermute | solution.py:212
  110.3 3.1 %collective-permute-start.23 = (f32[2,256]{1,0:T(2,128)S(1)}, f32[2,256]{1,0:T(2,128)S(1)}, u32[]{:S(2)}, u32[]{:S(2)}) collective-permute-start(f32[2,256]{1,0:T(2,128)S(1)} %pad_maximum_fusion.1), channel_id=1, source_target_pairs={{0,4},{4,0},{8,12},{12,8},{1,5},{5,1},{9,13},{13,9},{2,6},{6,2},{1... | collective-permute-start | bytes 6152 | tf_op jit(solution)/shard_map/ppermute | solution.py:211
  (9 other events, 7.6 us)

commit v3 on v2

--- a/solution.py
+++ b/solution.py
@@ -15,17 +15,18 @@
 EPS = 1e-06
 ROOT = math.sqrt(2.0 / math.pi)
 CUBE = 0.044715
-VMEM_BYTES = 48 * 2**20
+VMEM_BYTES = 36 * 2**20
 QUICK = pl.CostEstimate(flops=1, bytes_accessed=1, transcendentals=0)
+MARK = jax.ShapeDtypeStruct((8, 128), jnp.float32)
 AHEAD = 2
 
 CORE = [(0, 1), (1, 0), (2, 3), (3, 2)]
 CHIP = [(0, 2), (2, 0), (1, 3), (3, 1)]
-BOTH = [(0, 3), (3, 0), (1, 2), (2, 1)]
 NEXT, SKIP = CORE, CHIP
-PIECES = (32, 144, 80)
+PIECES = (160, 96)
 STARTS = tuple(sum(PIECES[:k]) for k in range(len(PIECES)))
-TURNS = ((0, 1), (2,))
+TURNS = ((0,), (1,))
+PART = 128
 
 
 def gelu_slope(value):
@@ -77,7 +78,8 @@
     del refs[:holds]
     left_sem, weight_sem, seed_sem = refs[-3:]
     left_buf, weight_buf, total = refs[-6:-3]
-    outs = refs[:-6]
+    mark, outs = refs[-7], refs[:-7]
+    mark[...] = jnp.zeros_like(mark)
 
     first, place = [], 0
     for index, (start, size) in enumerate(seeds):
@@ -131,17 +133,20 @@
         place += size
 
 
-def back(groups, weights, sizes, dtype, tile=768, order=None, seed=None, seeds=(), hold=()):
+def back(groups, weights, sizes, dtype, tile=768, order=None, seed=None, seeds=(), hold=(), pin=True):
     width = weights[0].shape[0]
     rows = sum(sizes)
     depth = sum(weight.shape[1] for weight in weights)
     layout = [[place for place, _ in group] for group in groups]
     copies = sum(len(group) * (weight.shape[1] // tile) for group, weight in zip(groups, weights))
-    operands = [left for group in groups for _, left in group] + list(weights)
-    operands += ([] if seed is None else [seed]) + list(hold)
+    operands = [left for group in groups for _, left in group]
+    if pin:
+        operands = [pltpu.with_memory_space_constraint(left, pltpu.HBM) for left in operands]
+    operands += [pltpu.with_memory_space_constraint(weight, pltpu.HBM) for weight in weights]
+    if seed is not None:
+        operands.append(pltpu.with_memory_space_constraint(seed, pltpu.HBM))
+    operands += list(hold)
     in_specs = [pl.BlockSpec(memory_space=pl.ANY)] * len(operands)
-    for index in range(len(weights)):
-        in_specs[sum(map(len, groups)) + index] = pl.BlockSpec(memory_space=pltpu.HBM)
     if order is not None:
         operands.insert(0, order)
         in_specs.insert(0, pl.BlockSpec(memory_space=pltpu.SMEM))
@@ -150,8 +155,12 @@
             back_kernel, layout, tile, order is not None, seeds, len(hold)
         ),
         in_specs=in_specs,
-        out_specs=[pl.BlockSpec(memory_space=pltpu.VMEM)] * len(sizes),
-        out_shape=[jax.ShapeDtypeStruct((size, width), dtype) for size in sizes],
+        out_specs=[pl.BlockSpec(memory_space=pltpu.VMEM)] * (len(sizes) + 1),
+        out_shape=[
+            pltpu.HBM((size, width), dtype) if order is None else jax.ShapeDtypeStruct((size, width), dtype)
+            for size in sizes
+        ]
+        + [MARK],
         scratch_shapes=[
             pltpu.VMEM((rows, depth), jnp.bfloat16),
             pltpu.VMEM((width, depth), jnp.bfloat16),
@@ -166,25 +175,31 @@
 
 
 def weight_kernel(count, holds, places, *refs):
-    parts, grads, (out, normed) = refs[:4], refs[4 : 4 + count], refs[-2:]
+    parts, grads, (out, mark, normed) = refs[:4], refs[4 : 4 + count], refs[-3:]
 
     @pl.when(pl.program_id(0) == 0)
     def _():
         for index, part in enumerate(parts):
             size = part.shape[0]
             normed[pl.ds(pl.multiple_of(places[index] * size, size), size), :] = part[...]
+        mark[...] = jnp.zeros_like(mark)
 
     joined = jnp.concatenate([grad[...] for grad in grads], axis=0)
     out[...] = over_tokens(normed[...], joined).astype(out.dtype)
 
 
-def weight_grad(places, parts, grads, tile=768, low=0, high=None, held=None, hold=()):
+def weight_grad(
+    places, parts, grads, tile=768, low=0, high=None, held=None, hold=(), pin=True
+):
     width = parts[0].shape[1]
     tokens = sum(part.shape[0] for part in parts)
     columns = grads[0].shape[1]
     high = columns // tile if high is None else high
     extra = list(hold) + ([] if held is None else [held])
-    operands = [places] + list(parts) + list(grads) + extra
+    arrays = list(parts) + list(grads)
+    if pin:
+        arrays = [pltpu.with_memory_space_constraint(array, pltpu.HBM) for array in arrays]
+    operands = [places] + arrays + extra
     return pl.pallas_call(
         functools.partial(weight_kernel, len(grads), len(extra)),
         grid=(high - low,),
@@ -192,8 +207,11 @@
         + [pl.BlockSpec(part.shape, lambda i: (0, 0)) for part in parts]
         + [pl.BlockSpec((grad.shape[0], tile), lambda i: (0, i + low)) for grad in grads]
         + [pl.BlockSpec(memory_space=pl.ANY)] * len(extra),
-        out_specs=pl.BlockSpec((width, tile), lambda i: (0, i + low)),
-        out_shape=jax.ShapeDtypeStruct((width, columns), jnp.bfloat16),
+        out_specs=[
+            pl.BlockSpec((width, tile), lambda i: (0, i + low)),
+            pl.BlockSpec(MARK.shape, lambda i: (0, 0)),
+        ],
+        out_shape=[jax.ShapeDtypeStruct((width, columns), jnp.bfloat16), MARK],
         scratch_shapes=[pltpu.VMEM((tokens, width), jnp.bfloat16)],
         input_output_aliases={} if held is None else {len(operands) - 1: 0},
         compiler_params=params(),
@@ -206,12 +224,8 @@
 
 
 def row_sum(pair):
-    return (
-        pair
-        + lax.ppermute(pair, "row", CORE)
-        + lax.ppermute(pair, "row", CHIP)
-        + lax.ppermute(pair, "row", BOTH)
-    )
+    pair += lax.ppermute(pair, "row", CHIP)
+    return pair + lax.ppermute(pair, "row", CORE)
 
 
 def on_grid(
@@ -235,11 +249,9 @@
     order = jnp.stack([own_first, 1 - own_first])
 
     latents32 = latents.astype(jnp.float32)
-    moments = row_sum(
-        jnp.stack([jnp.sum(latents32, axis=1), jnp.sum(latents32 * latents32, axis=1)])
-    )
-
-    far_q = lax.ppermute(qkv_cotangent, "row", CHIP)
+    moments = jnp.stack([jnp.sum(latents32, axis=1), jnp.sum(latents32 * latents32, axis=1)])
+    far_q = lax.ppermute(after(qkv_cotangent, moments), "row", CHIP)
+    moments = row_sum(moments)
     side_q = lax.ppermute(qkv_cotangent, "row", CORE)
 
     sample_ids = jnp.arange(samples, dtype=jnp.int32)
@@ -269,7 +281,7 @@
     side_m = [lax.ppermute(part, "row", CORE) for part in own_m]
     far_m = [lax.ppermute(part, "row", CHIP) for part in own_m]
 
-    near_keep, near_send = back(
+    near_keep, near_send, mark = back(
         [
             [(0, qkv_cotangent), (tok_row, side_q)],
             [(start, part) for start, part in zip(STARTS, own_m)]
@@ -279,33 +291,35 @@
         [tok_row, tok_row],
         jnp.bfloat16,
         order=order,
-        hold=[normed],
     )
     near_next = lax.ppermute(near_send, "col", NEXT)
+
+    ready_q = after(far_q, near_send, across, normed_next)
+    farside_q = [
+        lax.ppermute(ready_q[low : low + PART], "row", CORE) for low in range(0, tok_row, PART)
+    ]
     across_next = lax.ppermute(after(across, near_send), "col", NEXT)
-
     places = jnp.stack([row_id ^ col_id ^ j for j in (0, 2, 1, 3)])
     parts = [normed, across, normed_next, across_next]
-
-    farside_q = lax.ppermute(after(far_q, near_send, across, normed_next, far_m[0]), "row", CORE)
-    far = back(
-        [[(0, far_q), (tok_row, farside_q)]],
+    takes_near = row_id // 2 == col_id // 2
+
+    far, mark = back(
+        [
+            [(0, far_q)]
+            + [(tok_row + place * PART, part) for place, part in enumerate(farside_q)]
+        ],
         [w_qkv],
         [2 * tok_row],
         jnp.float32,
-    )[0]
-    near_half = near_keep.astype(jnp.float32) + after(near_next, far).astype(jnp.float32)
-    takes_near = row_id // 2 == col_id // 2
-
-    qkv_total = weight_grad(
-        places, parts, [qkv_cotangent, side_q, far_q, farside_q], hold=[far]
-    )
-    farside_m, hold, halves = [], [qkv_total], []
-    for turn in TURNS:
+    )
+    q_parts = [qkv_cotangent, side_q, far_q] + farside_q
+    qkv_total, mark = weight_grad(places, parts, q_parts, high=1, hold=[mark])
+    ready, farside_m, halves = [mark], [], []
+    for index, turn in enumerate(TURNS):
         for k in turn:
-            farside_m.append(lax.ppermute(after(far_m[k], hold), "row", CORE))
+            farside_m.append(lax.ppermute(after(far_m[k], *ready), "row", CORE))
         start, size = STARTS[turn[0]], sum(PIECES[k] for k in turn)
-        keep, send = back(
+        keep, send, mark = back(
             [
                 [(STARTS[k] - start, far_m[k]) for k in turn]
                 + [(size + STARTS[k] - start, farside_m[k]) for k in turn]
@@ -316,25 +330,37 @@
             order=order,
             seed=far,
             seeds=((start, size), (tok_row + start, size)),
-            hold=hold,
+            hold=[mark],
+            pin=False,
         )
-        hold = [keep]
-        halves.append((start, size, keep, lax.ppermute(send, "col", NEXT)))
+        send = lax.ppermute(send, "col", NEXT)
+        if index == 0:
+            qkv_total, mark = weight_grad(
+                places, parts, q_parts, low=1, held=qkv_total, hold=[mark]
+            )
+            ready = [mark, send, near_next]
+        halves.append((start, size, keep, send))
 
     all_m = own_m + side_m + far_m + farside_m
-    mlp_total = weight_grad(places, parts, all_m, hold=hold)
-
+    mlp_total, mark = weight_grad(places, parts, all_m, high=1, hold=[mark])
     incoming = []
-    for start, size, keep, send in halves:
+    for index, (start, size, keep, send) in enumerate(halves):
+        if index == len(halves) - 1:
+            keep, send = after((keep, send), mark)
         far_half = keep.astype(jnp.float32) + send.astype(jnp.float32)
-        near_piece = near_half[start : start + size]
+        near_piece = near_keep[start : start + size].astype(jnp.float32)
+        near_piece += near_next[start : start + size].astype(jnp.float32)
         own = jnp.where(takes_near, near_piece, far_half)
         other = jnp.where(takes_near, far_half, near_piece).astype(jnp.bfloat16)
-        arrived = after(lax.ppermute(other, "col", SKIP), mlp_total)
-        incoming.append(own + arrived.astype(jnp.float32))
-    incoming = jnp.concatenate(incoming, axis=0) * scale_omega
-    own_terms = jnp.stack([jnp.sum(incoming, axis=1), jnp.sum(incoming * xhat, axis=1)])
-    terms = row_sum(own_terms) / MODEL_WIDTH
+        incoming.append((own, lax.ppermute(other, "col", SKIP)))
+    mlp_total, mark = weight_grad(places, parts, all_m, low=1, held=mlp_total, hold=[mark, other])
+
+    incoming = jnp.concatenate(
+        [own + after(arrived, mark).astype(jnp.float32) for own, arrived in incoming], axis=0
+    ) * scale_omega
+    terms = row_sum(
+        jnp.stack([jnp.sum(incoming, axis=1), jnp.sum(incoming * xhat, axis=1)])
+    ) / MODEL_WIDTH
     latent_input_gradient = rstd * (
         incoming - terms[0][:, None] - xhat * terms[1][:, None]
     )

time: 115 us -> 108 us (0.939)
  local copies, waits for them, and re-layouts: 13 us -> 4.78 us
  Pallas kernels: 42.4 us -> 48.7 us
  other arithmetic: 11.1 us -> 7.68 us
    unnamed x63 -> x47, local copies, waits for them, and re-layouts: 13 us -> 3.56 us
    pallas_call x2 -> x4, Pallas kernels: 16.1 us -> 23.1 us  [weight_grad(): pl.pallas_call(functools.partial(weight_kernel, len(grads), len(extra)),...]
    ppermute x1, waiting for transfers between devices: 0.01 us -> 3.83 us  [on_grid(): across = lax.ppermute(normed, 'col', SKIP)]
    add x4 -> x5, other arithmetic: 2.34 us -> 0.29 us  [the longest x2 0.26 us: on_grid(): own + after(arrived, mark).astype(jnp.float32)]
    ppermute x3 -> x2, waiting for transfers between devices: 2 us -> 0.01 us  [on_grid(): side_m = [lax.ppermute(part, 'row', CORE) for part in own_m]]
    ppermute x1, waiting for transfers between devices: 4.19 us -> 2.4 us  [on_grid(): across_next = lax.ppermute(after(across, near_send), 'col', NEXT)]
    slice x0 -> x1, local copies, waits for them, and re-layouts: none -> 1.22 us  [on_grid(): ready_q[low:low + PART]]
    ppermute x3 -> x2, starting transfers between devices: 2.8 us -> 2.22 us  [on_grid(): far_m = [lax.ppermute(part, 'row', CHIP) for part in own_m]]
  transfers between devices with their start and end apart: 26 -> 22, of which waited for: 10 -> 15; matrix products, arithmetic and copies ran while one was open for 9% -> 7% of each run, Pallas kernels for 37% -> 41%
where the time goes in v3:
time: 108 us
  Pallas kernels  48.7 us (45%)
  waiting for transfers between devices  23.4 us (22%)
  starting transfers between devices  21.4 us (20%)
  other arithmetic  7.68 us (7%)
  local copies, waits for them, and re-layouts  4.78 us (4%)
    pallas_call x4, Pallas kernels, back(): pl.pallas_call(functools.partial(back_kernel, layout, tile, order is not...  25.6 us
    pallas_call x4, Pallas kernels, weight_grad(): pl.pallas_call(functools.partial(weight_kernel, len(grads), len(extra)),...  23.1 us
    ppermute x2, waiting for transfers between devices, on_grid(): incoming.append((own, lax.ppermute(other, 'col', SKIP)))  4.45 us
    ppermute x2, starting transfers between devices, on_grid(): incoming.append((own, lax.ppermute(other, 'col', SKIP)))  3.9 us
    ppermute x1, waiting for transfers between devices, on_grid(): across = lax.ppermute(normed, 'col', SKIP)  3.83 us
    ppermute x2, starting transfers between devices, row_sum(): pair += lax.ppermute(pair, 'row', CHIP)  3.79 us
    unnamed x47, local copies, waits for them, and re-layouts  3.56 us
    convert_element_type x2, other arithmetic, on_grid(): own_m = [(mlp_cotangent[start:start + size].astype(jnp.float32) * gelu_sl...  3.15 us
  transfers between devices with their start and end apart: 22, of which 15 were waited for; matrix products, arithmetic and copies ran while one was open for 7% of the time, Pallas kernels for 41%

profile of v3, /device:TPU:0, one launch (start us, length us, event | category | flops | bytes accessed | tf_op | source)
XLA Modules:
  0.0 107.8 jit_solution(627748752655274783)
XLA Ops:
  0.7 1.3 %convert_reduce_fusion = (f32[256]{0:T(256)S(1)}, f32[256]{0:T(256)S(1)}) fusion(bf16[256,768]{1,0:T(8,128)(2,1)} %param.10), kind=kLoop, calls=%fused_computation.25 | loop fusion | flops 785920 | bytes 395264 | tf_op jit(solution)/shard_map/reduce_sum | solution.py:252
  2.0 3.0 %collective-permute-start = (f32[2,256]{1,0:T(2,128)S(1)}, f32[2,256]{1,0:T(2,128)S(1)}, u32[]{:S(2)}, u32[]{:S(2)}) collective-permute-start(f32[2,256]{1,0:T(2,128)S(1)} %pad_maximum_fusion), channel_id=1, source_target_pairs={{0,8},{8,0},{4,12},{12,4},{1,9},{9,1},{5,13},{13,5},{2,10},{10,2},... | collective-permute-start | bytes 6152 | tf_op jit(solution)/shard_map/ppermute | solution.py:227
  5.1 0.7 iota_compare_fusion
  5.8 0.8 copy.15
  6.6 0.8 fusion.32
  7.6 0.4 collective-permute-start.1
  8.2 0.7 collective-permute-done.1
  9.6 2.3 %fusion.7.refs_3_.refs_4_ = bf16[160,3072]{1,0:T(8,128)(2,1)} fusion(bf16[256,3072]{1,0:T(8,128)(2,1)S(1)} %copy-done.18, bf16[256,3072]{1,0:T(8,128)(2,1)S(1)} %copy-done.19), kind=kLoop, calls=%fused_computation.21 | loop fusion | flops 10321920 | bytes 2949120 | tf_op jit(solution)/shard_map/convert_element_type | solution.py:278
  12.3 0.8 fusion.16.refs_4_.refs_5_
  13.3 3.0 %collective-permute-start.7 = (bf16[256,768]{1,0:T(8,128)(2,1)S(1)}, bf16[256,768]{1,0:T(8,128)(2,1)}, u32[]{:S(2)}, u32[]{:S(2)}) collective-permute-start(bf16[256,768]{1,0:T(8,128)(2,1)S(1)} %fusion.25.refs_0_), channel_id=1, source_target_pairs={{0,2},{2,0},{1,3},{3,1},{4,6},{6,4},{5,7},{7,5},{8,10},{10,8},{9,1... | collective-permute-start | bytes 1179656 | tf_op jit(solution)/shard_map/ppermute | solution.py:270
  16.3 0.8 copy-done.15
  17.1 1.6 %collective-permute-start.8 = (bf16[256,768]{1,0:T(8,128)(2,1)S(1)}, bf16[256,768]{1,0:T(8,128)(2,1)}, u32[]{:S(2)}, u32[]{:S(2)}) collective-permute-start(bf16[256,768]{1,0:T(8,128)(2,1)S(1)} %fusion.25.refs_0_), channel_id=1, source_target_pairs={{0,1},{1,0},{2,3},{3,2},{4,5},{5,4},{6,7},{7,6},{8,9},{9,8},{10,11... | collective-permute-start | bytes 1179656 | tf_op jit(solution)/shard_map/ppermute | solution.py:271
  18.8 1.5 %collective-permute-start.6 = (bf16[160,3072]{1,0:T(8,128)(2,1)}, bf16[160,3072]{1,0:T(8,128)(2,1)S(1)}, u32[]{:S(2)}, u32[]{:S(2)}) collective-permute-start(bf16[160,3072]{1,0:T(8,128)(2,1)} %fusion.7.refs_3_.refs_4_), channel_id=1, source_target_pairs={{0,8},{8,0},{4,12},{12,4},{1,9},{9,1},{5,13},{13,5},{2,10},{10,2},... | collective-permute-start | bytes 2949128 | tf_op jit(solution)/shard_map/ppermute | solution.py:282
  20.3 9.6 %shard_map.121 = (bf16[256,768]{1,0:T(8,128)(2,1)S(1)}, bf16[256,768]{1,0:T(8,128)(2,1)S(1)}, f32[8,128]{1,0:T(8,128)}) custom-call(s32[2]{0:T(128)S(1)} %pad_add_fusion.refs_0_, bf16[256,2304]{1,0:T(8,128)(2,1)} %refs_4_.3, bf16[256,2304]{1,0:T(8,128)(2,1)} %collective-permute-done.2.refs_2_.refs_5_, bf16[160,3072]{1,0:T(8,128)(2,1)} %fusion.7.refs_3_.refs_4_, ...), custom_call_target="tpu_custom_call" | custom-call | flops 1 | bytes 1 | tf_op jit(solution)/shard_map/pallas_call | solution.py:153
  29.9 0.7 copy-done.4
  30.6 3.8 %collective-permute-done.7.refs_1_ = bf16[256,768]{1,0:T(8,128)(2,1)} collective-permute-done((bf16[256,768]{1,0:T(8,128)(2,1)S(1)}, bf16[256,768]{1,0:T(8,128)(2,1)}, u32[]{:S(2)}, u32[]{:S(2)}) %collective-permute-start.7) | collective-permute-done | bytes 393248 | tf_op jit(solution)/shard_map/ppermute | solution.py:270
  34.4 1.0 collective-permute-done.8.refs_2_
  35.5 1.2 %fusion.56 = (bf16[128,2304]{1,0:T(8,128)(2,1)}, bf16[128,2304]{1,0:T(8,128)(2,1)}) fusion(bf16[256,2304]{1,0:T(8,128)(2,1)S(1)} %collective-permute-done.10.refs_0_.refs_6_), kind=kLoop, calls=%fused_computation.94 | loop fusion | bytes 2359296 | tf_op jit(solution)/shard_map/slice | solution.py:299
  36.7 0.5 collective-permute-start.12
  37.2 0.6 collective-permute-start.9
  37.9 1.1 %collective-permute-done.11.refs_1_.refs_7_ = bf16[128,2304]{1,0:T(8,128)(2,1)} collective-permute-done((bf16[128,2304]{1,0:T(8,128)(2,1)}, bf16[128,2304]{1,0:T(8,128)(2,1)}, u32[]{:S(2)}, u32[]{:S(2)}) %collective-permute-start.11) | collective-permute-done | bytes 589856 | tf_op jit(solution)/shard_map/ppermute | solution.py:299
  39.0 0.8 collective-permute-done.12.refs_2_.refs_8_
  39.9 6.1 %shard_map.122 = (f32[512,768]{1,0:T(8,128)}, f32[8,128]{1,0:T(8,128)S(1)}) custom-call(bf16[256,2304]{1,0:T(8,128)(2,1)} %copy-done.6, bf16[128,2304]{1,0:T(8,128)(2,1)} %collective-permute-done.11.refs_1_.refs_7_, bf16[128,2304]{1,0:T(8,128)(2,1)} %collective-permute-done.12.refs_2_.refs_8_, bf16[768,2304]{1,0:T(8,128)(2,1)} %refs_3_.3), custom_call_target="tpu_custom_call" | custom-call | flops 1 | bytes 1 | tf_op jit(solution)/shard_map/pallas_call | solution.py:153
  46.0 2.4 %collective-permute-done.9.refs_3_ = bf16[256,768]{1,0:T(8,128)(2,1)S(1)} collective-permute-done((bf16[256,768]{1,0:T(8,128)(2,1)}, bf16[256,768]{1,0:T(8,128)(2,1)S(1)}, u32[]{:S(2)}, u32[]{:S(2)}) %collective-permute-start.9) | collective-permute-done | bytes 393248 | tf_op jit(solution)/shard_map/ppermute | solution.py:301
  48.4 0.7 copy-done.12
  49.2 4.5 %shard_map.123 = (bf16[768,2304]{1,0:T(8,128)(2,1)}, f32[8,128]{1,0:T(8,128)S(1)}) custom-call(s32[4]{0:T(128)S(1)} %pad_add_fusion.1.places, bf16[256,768]{1,0:T(8,128)(2,1)} %copy-done.7, bf16[256,768]{1,0:T(8,128)(2,1)} %collective-permute-done.7.refs_1_, bf16[256,768]{1,0:T(8,128)(2,1)} %collective-permute-done.8.refs_2_, bf16[256,768]{1,0:T(8,128)(2,1)} %copy-done.12, ...), custom_call_target="tpu_custom_call" | custom-call | flops 1 | bytes 1 | tf_op jit(solution)/shard_map/pallas_call | solution.py:203
  53.6 1.0 collective-permute-done.6.refs_1_.refs_8_
  54.6 0.7 collective-permute-start.16
  55.4 1.5 %collective-permute-start.5 = (bf16[256,768]{1,0:T(8,128)(2,1)S(1)}, bf16[256,768]{1,0:T(8,128)(2,1)S(1)}, u32[]{:S(2)}, u32[]{:S(2)}) collective-permute-start(bf16[256,768]{1,0:T(8,128)(2,1)S(1)} %copy-done.5), channel_id=1, source_target_pairs={{0,1},{1,0},{2,3},{3,2},{4,5},{5,4},{6,7},{7,6},{8,9},{9,8},{10,11... | collective-permute-start | bytes 1179656 | tf_op jit(solution)/shard_map/ppermute | solution.py:295
  56.8 0.4 collective-permute-done.13.refs_2_.refs_10_
  57.2 5.2 %shard_map.124 = (bf16[160,768]{1,0:T(8,128)(2,1)S(1)}, bf16[160,768]{1,0:T(8,128)(2,1)S(1)}, f32[8,128]{1,0:T(8,128)S(1)}) custom-call(s32[2]{0:T(128)S(1)} %pad_add_fusion.refs_0_, bf16[160,3072]{1,0:T(8,128)(2,1)S(1)} %collective-permute-done.6.refs_1_.refs_8_, bf16[160,3072]{1,0:T(8,128)(2,1)S(1)} %collective-permute-done.13.refs_2_.refs_10_, ...), custom_call_target="tpu_custom_call" | custom-call | flops 1 | bytes 1 | tf_op jit(solution)/shard_map/pallas_call | solution.py:153
  62.4 1.6 %collective-permute-start.14 = (bf16[160,768]{1,0:T(8,128)(2,1)S(1)}, bf16[160,768]{1,0:T(8,128)(2,1)S(1)}, u32[]{:S(2)}, u32[]{:S(2)}) collective-permute-start(bf16[160,768]{1,0:T(8,128)(2,1)S(1)} %get-tuple-element.42), channel_id=1, source_target_pairs={{0,1},{1,0},{2,3},{3,2},{4,5},{5,4},{6,7},{7,6},{8,9},{9,8},{10,11... | collective-permute-start | bytes 737288 | tf_op jit(solution)/shard_map/ppermute | solution.py:336
  64.0 6.1 %shard_map.125 = (bf16[768,2304]{1,0:T(8,128)(2,1)}, f32[8,128]{1,0:T(8,128)S(1)}) custom-call(s32[4]{0:T(128)S(1)} %pad_add_fusion.1.places, bf16[256,768]{1,0:T(8,128)(2,1)} %copy-done.7, bf16[256,768]{1,0:T(8,128)(2,1)} %collective-permute-done.7.refs_1_, bf16[256,768]{1,0:T(8,128)(2,1)} %collective-permute-done.8.refs_2_, ...), custom_call_target="tpu_custom_call", output_to_operand_aliasing={{0}: (11, {})} | custom-call | flops 1 | bytes 1 | tf_op jit(solution)/shard_map/pallas_call | solution.py:203
  70.4 1.4 %collective-permute-done.14 = bf16[160,768]{1,0:T(8,128)(2,1)S(1)} collective-permute-done((bf16[160,768]{1,0:T(8,128)(2,1)S(1)}, bf16[160,768]{1,0:T(8,128)(2,1)S(1)}, u32[]{:S(2)}, u32[]{:S(2)}) %collective-permute-start.14) | collective-permute-done | bytes 245792 | tf_op jit(solution)/shard_map/ppermute | solution.py:336
  71.8 2.0 %collective-permute-done.17.refs_2_.refs_11_ = bf16[96,3072]{1,0:T(8,128)(2,1)S(1)} collective-permute-done((bf16[96,3072]{1,0:T(8,128)(2,1)S(1)}, bf16[96,3072]{1,0:T(8,128)(2,1)S(1)}, u32[]{:S(2)}, u32[]{:S(2)}) %collective-permute-start.17) | collective-permute-done | bytes 589856 | tf_op jit(solution)/shard_map/ppermute | solution.py:320
  73.8 4.7 %shard_map.126 = (bf16[96,768]{1,0:T(8,128)(2,1)S(1)}, bf16[96,768]{1,0:T(8,128)(2,1)S(1)}, f32[8,128]{1,0:T(8,128)S(1)}) custom-call(s32[2]{0:T(128)S(1)} %pad_add_fusion.refs_0_, bf16[96,3072]{1,0:T(8,128)(2,1)S(1)} %collective-permute-done.16.refs_1_.refs_9_, bf16[96,3072]{1,0:T(8,128)(2,1)S(1)} %collective-permute-done.17.refs_2_.refs_11_, ...), custom_call_target="tpu_custom_call" | custom-call | flops 1 | bytes 1 | tf_op jit(solution)/shard_map/pallas_call | solution.py:153
  78.6 1.5 %collective-permute-start.18 = (bf16[96,768]{1,0:T(8,128)(2,1)S(1)}, bf16[96,768]{1,0:T(8,128)(2,1)S(1)}, u32[]{:S(2)}, u32[]{:S(2)}) collective-permute-start(bf16[96,768]{1,0:T(8,128)(2,1)S(1)} %get-tuple-element.50), channel_id=1, source_target_pairs={{0,1},{1,0},{2,3},{3,2},{4,5},{5,4},{6,7},{7,6},{8,9},{9,8},{10,11... | collective-permute-start | bytes 442376 | tf_op jit(solution)/shard_map/ppermute | solution.py:336
  80.2 3.5 %collective-permute-start.15 = (bf16[160,768]{1,0:T(8,128)(2,1)S(1)}, bf16[160,768]{1,0:T(8,128)(2,1)S(1)}, u32[]{:S(2)}, u32[]{:S(2)}) collective-permute-start(bf16[160,768]{1,0:T(8,128)(2,1)S(1)} %select_convert_fusion), channel_id=1, source_target_pairs={{0,2},{2,0},{1,3},{3,1},{4,6},{6,4},{5,7},{7,5},{8,10},{10,8},{9,1... | collective-permute-start | bytes 737288 | tf_op jit(solution)/shard_map/ppermute | solution.py:355
  83.7 4.4 %shard_map.127 = (bf16[768,3072]{1,0:T(8,128)(2,1)}, f32[8,128]{1,0:T(8,128)S(1)}) custom-call(s32[4]{0:T(128)S(1)} %pad_add_fusion.1.places, bf16[256,768]{1,0:T(8,128)(2,1)} %copy-done.7, bf16[256,768]{1,0:T(8,128)(2,1)} %collective-permute-done.7.refs_1_, bf16[256,768]{1,0:T(8,128)(2,1)} %collective-permute-done.8.refs_2_, bf16[256,768]{1,0:T(8,128)(2,1)} %copy-done.12, ...), custom_call_target="tpu_custom_call" | custom-call | flops 1 | bytes 1 | tf_op jit(solution)/shard_map/pallas_call | solution.py:203
  88.2 0.4 collective-permute-start.19
  88.6 8.1 %shard_map.128 = (bf16[768,3072]{1,0:T(8,128)(2,1)}, f32[8,128]{1,0:T(8,128)}) custom-call(s32[4]{0:T(128)S(1)} %pad_add_fusion.1.places, bf16[256,768]{1,0:T(8,128)(2,1)} %copy-done.7, bf16[256,768]{1,0:T(8,128)(2,1)} %collective-permute-done.7.refs_1_, bf16[256,768]{1,0:T(8,128)(2,1)} %collective-permute-done.8.refs_2_, ...), custom_call_target="tpu_custom_call", output_to_operand_aliasing={{0}: (15, {})} | custom-call | flops 1 | bytes 1 | tf_op jit(solution)/shard_map/pallas_call | solution.py:203
  96.7 2.3 %collective-permute-done.15 = bf16[160,768]{1,0:T(8,128)(2,1)S(1)} collective-permute-done((bf16[160,768]{1,0:T(8,128)(2,1)S(1)}, bf16[160,768]{1,0:T(8,128)(2,1)S(1)}, u32[]{:S(2)}, u32[]{:S(2)}) %collective-permute-start.15) | collective-permute-done | bytes 245792 | tf_op jit(solution)/shard_map/ppermute | solution.py:355
  99.1 2.2 %collective-permute-done.19 = bf16[96,768]{1,0:T(8,128)(2,1)S(1)} collective-permute-done((bf16[96,768]{1,0:T(8,128)(2,1)S(1)}, bf16[96,768]{1,0:T(8,128)(2,1)S(1)}, u32[]{:S(2)}, u32[]{:S(2)}) %collective-permute-start.19) | collective-permute-done | bytes 147488 | tf_op jit(solution)/shard_map/ppermute | solution.py:355
  101.4 0.5 fusion.55
  101.9 0.8 collective-permute-start.20
  102.7 2.9 %collective-permute-done.20 = f32[2,256]{1,0:T(2,128)S(1)} collective-permute-done((f32[2,256]{1,0:T(2,128)S(1)}, f32[2,256]{1,0:T(2,128)S(1)}, u32[]{:S(2)}, u32[]{:S(2)}) %collective-permute-start.20) | collective-permute-done | bytes 2080 | tf_op jit(solution)/shard_map/ppermute | solution.py:227
  105.7 1.1 %collective-permute-done.21 = f32[2,256]{1,0:T(2,128)S(1)} collective-permute-done((f32[2,256]{1,0:T(2,128)S(1)}, f32[2,256]{1,0:T(2,128)S(1)}, u32[]{:S(2)}, u32[]{:S(2)}) %collective-permute-start.21) | collective-permute-done | bytes 2080 | tf_op jit(solution)/shard_map/ppermute | solution.py:228
  106.8 1.0 fusion.29
  (77 shorter events, 2.7 us)
Async XLA Ops:
  0.6 8.3 %copy-start.13 = (bf16[256,768]{1,0:T(8,128)(2,1)S(1)}, bf16[256,768]{1,0:T(8,128)(2,1)}, u32[]{:S(2)}) copy-start(bf16[256,768]{1,0:T(8,128)(2,1)} %param.10) | copy-start | bytes 1179652
  0.6 6.8 %copy-start.20 = (s32[1024]{0:T(1024)S(1)}, s32[1024]{0:T(1024)}, u32[]{:S(2)}) copy-start(s32[1024]{0:T(1024)} %param.12) | copy-start | bytes 12292
  0.7 7.4 %copy-start.21 = (f32[8]{0:T(128)S(1)}, f32[8]{0:T(128)}, u32[]{:S(2)}) copy-start(f32[8]{0:T(128)} %param.14) | copy-start | bytes 100
  0.7 7.4 %copy-start.22 = (s32[8]{0:T(128)S(1)}, s32[8]{0:T(128)}, u32[]{:S(2)}) copy-start(s32[8]{0:T(128)} %param.13) | copy-start | bytes 100
  2.0 5.7 %collective-permute-start = (f32[2,256]{1,0:T(2,128)S(1)}, f32[2,256]{1,0:T(2,128)S(1)}, u32[]{:S(2)}, u32[]{:S(2)}) collective-permute-start(f32[2,256]{1,0:T(2,128)S(1)} %pad_maximum_fusion), channel_id=1, source_target_pairs={{0,8},{8,0},{4,12},{12,4},{1,9},{9,1},{5,13},{13,5},{2,10},{10,2},... | collective-permute-start | bytes 6152 | tf_op jit(solution)/shard_map/ppermute | solution.py:227
  5.0 15.3 %collective-permute-start.2 = (bf16[256,2304]{1,0:T(8,128)(2,1)}, bf16[256,2304]{1,0:T(8,128)(2,1)}, u32[]{:S(2)}, u32[]{:S(2)}) collective-permute-start(bf16[256,2304]{1,0:T(8,128)(2,1)} %refs_4_.3), channel_id=1, source_target_pairs={{0,4},{4,0},{8,12},{12,8},{1,5},{5,1},{9,13},{13,9},{2,6},{6,2},{1... | collective-permute-start | bytes 3538952 | tf_op jit(solution)/shard_map/ppermute | solution.py:255
  5.0 30.5 %collective-permute-start.10 = (bf16[256,2304]{1,0:T(8,128)(2,1)}, bf16[256,2304]{1,0:T(8,128)(2,1)S(1)}, u32[]{:S(2)}, u32[]{:S(2)}) collective-permute-start(bf16[256,2304]{1,0:T(8,128)(2,1)} %refs_4_.3), channel_id=1, source_target_pairs={{0,8},{8,0},{4,12},{12,4},{1,9},{9,1},{5,13},{13,5},{2,10},{10,2},... | collective-permute-start | bytes 3538952 | tf_op jit(solution)/shard_map/ppermute | solution.py:253
  6.6 2.6 %copy-start.19 = (bf16[256,3072]{1,0:T(8,128)(2,1)S(1)}, bf16[256,3072]{1,0:T(8,128)(2,1)}, u32[]{:S(2)}) copy-start(bf16[256,3072]{1,0:T(8,128)(2,1)} %param.16) | copy-start | bytes 4718596
  7.5 1.4 %copy-start.8 = (f32[256,1536]{1,0:T(8,128)}, f32[256,1536]{1,0:T(8,128)S(1)}, u32[]{:S(2)}) copy-start(f32[256,1536]{1,0:T(8,128)S(1)} %fusion.32) | copy-start | bytes 4718596
  7.5 2.1 %copy-start.18 = (bf16[256,3072]{1,0:T(8,128)(2,1)S(1)}, bf16[256,3072]{1,0:T(8,128)(2,1)}, u32[]{:S(2)}) copy-start(bf16[256,3072]{1,0:T(8,128)(2,1)} %param.17) | copy-start | bytes 4718596
  7.6 1.2 %collective-permute-start.1 = (f32[2,256]{1,0:T(2,128)S(1)}, f32[2,256]{1,0:T(2,128)S(1)}, u32[]{:S(2)}, u32[]{:S(2)}) collective-permute-start(f32[2,256]{1,0:T(2,128)S(1)} %fusion.54), channel_id=1, source_target_pairs={{0,4},{4,0},{8,12},{12,8},{1,5},{5,1},{9,13},{13,9},{2,6},{6,2},{1... | collective-permute-start | bytes 6152 | tf_op jit(solution)/shard_map/ppermute | solution.py:228
  9.6 6.7 %copy-start.7 = (bf16[256,768]{1,0:T(8,128)(2,1)}, bf16[256,768]{1,0:T(8,128)(2,1)S(1)}, u32[]{:S(2)}) copy-start(bf16[256,768]{1,0:T(8,128)(2,1)S(1)} %fusion.25.refs_0_) | copy-start | bytes 1179652
  11.9 6.9 %collective-permute-start.3 = (bf16[160,3072]{1,0:T(8,128)(2,1)}, bf16[160,3072]{1,0:T(8,128)(2,1)}, u32[]{:S(2)}, u32[]{:S(2)}) collective-permute-start(bf16[160,3072]{1,0:T(8,128)(2,1)} %fusion.7.refs_3_.refs_4_), channel_id=1, source_target_pairs={{0,4},{4,0},{8,12},{12,8},{1,5},{5,1},{9,13},{13,9},{2,6},{6,2},{1... | collective-permute-start | bytes 2949128 | tf_op jit(solution)/shard_map/ppermute | solution.py:281
  13.1 3.2 %copy-start.10 = (bf16[96,3072]{1,0:T(8,128)(2,1)}, bf16[96,3072]{1,0:T(8,128)(2,1)S(1)}, u32[]{:S(2)}) copy-start(bf16[96,3072]{1,0:T(8,128)(2,1)S(1)} %fusion.16.refs_4_.refs_5_) | copy-start | bytes 1769476
  13.1 3.2 %collective-permute-start.4 = (bf16[96,3072]{1,0:T(8,128)(2,1)S(1)}, bf16[96,3072]{1,0:T(8,128)(2,1)S(1)}, u32[]{:S(2)}, u32[]{:S(2)}) collective-permute-start(bf16[96,3072]{1,0:T(8,128)(2,1)S(1)} %fusion.16.refs_4_.refs_5_), channel_id=1, source_target_pairs={{0,4},{4,0},{8,12},{12,8},{1,5},{5,1},{9,13},{13,9},{2,6},{6,2},{1... | collective-permute-start | bytes 1769480 | tf_op jit(solution)/shard_map/ppermute | solution.py:281
  13.3 21.1 %collective-permute-start.7 = (bf16[256,768]{1,0:T(8,128)(2,1)S(1)}, bf16[256,768]{1,0:T(8,128)(2,1)}, u32[]{:S(2)}, u32[]{:S(2)}) collective-permute-start(bf16[256,768]{1,0:T(8,128)(2,1)S(1)} %fusion.25.refs_0_), channel_id=1, source_target_pairs={{0,2},{2,0},{1,3},{3,1},{4,6},{6,4},{5,7},{7,5},{8,10},{10,8},{9,1... | collective-permute-start | bytes 1179656 | tf_op jit(solution)/shard_map/ppermute | solution.py:270
  16.3 0.8 copy-start.15
  17.1 18.3 %collective-permute-start.8 = (bf16[256,768]{1,0:T(8,128)(2,1)S(1)}, bf16[256,768]{1,0:T(8,128)(2,1)}, u32[]{:S(2)}, u32[]{:S(2)}) collective-permute-start(bf16[256,768]{1,0:T(8,128)(2,1)S(1)} %fusion.25.refs_0_), channel_id=1, source_target_pairs={{0,1},{1,0},{2,3},{3,2},{4,5},{5,4},{6,7},{7,6},{8,9},{9,8},{10,11... | collective-permute-start | bytes 1179656 | tf_op jit(solution)/shard_map/ppermute | solution.py:271
  18.8 35.8 %collective-permute-start.6 = (bf16[160,3072]{1,0:T(8,128)(2,1)}, bf16[160,3072]{1,0:T(8,128)(2,1)S(1)}, u32[]{:S(2)}, u32[]{:S(2)}) collective-permute-start(bf16[160,3072]{1,0:T(8,128)(2,1)} %fusion.7.refs_3_.refs_4_), channel_id=1, source_target_pairs={{0,8},{8,0},{4,12},{12,4},{1,9},{9,1},{5,13},{13,5},{2,10},{10,2},... | collective-permute-start | bytes 2949128 | tf_op jit(solution)/shard_map/ppermute | solution.py:282
  29.9 0.7 copy-start.4
  35.5 4.4 %copy-start.6 = (bf16[256,2304]{1,0:T(8,128)(2,1)}, bf16[256,2304]{1,0:T(8,128)(2,1)S(1)}, u32[]{:S(2)}) copy-start(bf16[256,2304]{1,0:T(8,128)(2,1)S(1)} %collective-permute-done.10.refs_0_.refs_6_) | copy-start | bytes 3538948
  36.7 2.3 %collective-permute-start.11 = (bf16[128,2304]{1,0:T(8,128)(2,1)}, bf16[128,2304]{1,0:T(8,128)(2,1)}, u32[]{:S(2)}, u32[]{:S(2)}) collective-permute-start(bf16[128,2304]{1,0:T(8,128)(2,1)} %get-tuple-element.65), channel_id=1, source_target_pairs={{0,4},{4,0},{8,12},{12,8},{1,5},{5,1},{9,13},{13,9},{2,6},{6,2},{1... | collective-permute-start | bytes 1769480 | tf_op jit(solution)/shard_map/ppermute | solution.py:299
  36.7 3.2 %collective-permute-start.12 = (bf16[128,2304]{1,0:T(8,128)(2,1)}, bf16[128,2304]{1,0:T(8,128)(2,1)}, u32[]{:S(2)}, u32[]{:S(2)}) collective-permute-start(bf16[128,2304]{1,0:T(8,128)(2,1)} %get-tuple-element.64), channel_id=1, source_target_pairs={{0,4},{4,0},{8,12},{12,8},{1,5},{5,1},{9,13},{13,9},{2,6},{6,2},{1... | collective-permute-start | bytes 1769480 | tf_op jit(solution)/shard_map/ppermute | solution.py:299
  37.2 11.2 %collective-permute-start.9 = (bf16[256,768]{1,0:T(8,128)(2,1)}, bf16[256,768]{1,0:T(8,128)(2,1)S(1)}, u32[]{:S(2)}, u32[]{:S(2)}) collective-permute-start(bf16[256,768]{1,0:T(8,128)(2,1)} %collective-permute-done.7.refs_1_), channel_id=1, source_target_pairs={{0,1},{1,0},{2,3},{3,2},{4,5},{5,4},{6,7},{7,6},{8,9},{9,8},{10,11... | collective-permute-start | bytes 1179656 | tf_op jit(solution)/shard_map/ppermute | solution.py:301
  48.4 0.7 copy-start.12
  49.2 5.5 %copy-start.11 = (bf16[96,3072]{1,0:T(8,128)(2,1)S(1)}, bf16[96,3072]{1,0:T(8,128)(2,1)}, u32[]{:S(2)}) copy-start(bf16[96,3072]{1,0:T(8,128)(2,1)} %copy-done.10) | copy-start | bytes 1769476
  49.2 6.2 %copy-start.5 = (bf16[256,768]{1,0:T(8,128)(2,1)S(1)}, bf16[256,768]{1,0:T(8,128)(2,1)}, u32[]{:S(2)}) copy-start(bf16[256,768]{1,0:T(8,128)(2,1)} %copy-done.4) | copy-start | bytes 1179652
  54.6 7.8 %copy-start = (bf16[160,3072]{1,0:T(8,128)(2,1)}, bf16[160,3072]{1,0:T(8,128)(2,1)S(1)}, u32[]{:S(2)}) copy-start(bf16[160,3072]{1,0:T(8,128)(2,1)S(1)} %collective-permute-done.6.refs_1_.refs_8_) | copy-start | bytes 2949124
  54.6 2.6 %collective-permute-start.13 = (bf16[160,3072]{1,0:T(8,128)(2,1)S(1)}, bf16[160,3072]{1,0:T(8,128)(2,1)S(1)}, u32[]{:S(2)}, u32[]{:S(2)}) collective-permute-start(bf16[160,3072]{1,0:T(8,128)(2,1)S(1)} %collective-permute-done.6.refs_1_.refs_8_), channel_id=1, source_target_pairs={{0,4},{4,0},{8,12},{12,8},{1,5},{5,1},{9,13},{13,9},{2,6},{6,2},{1... | collective-permute-start | bytes 2949128 | tf_op jit(solution)/shard_map/ppermute | solution.py:320
  54.6 15.7 %collective-permute-start.16 = (bf16[96,3072]{1,0:T(8,128)(2,1)S(1)}, bf16[96,3072]{1,0:T(8,128)(2,1)S(1)}, u32[]{:S(2)}, u32[]{:S(2)}) collective-permute-start(bf16[96,3072]{1,0:T(8,128)(2,1)S(1)} %copy-done.11), channel_id=1, source_target_pairs={{0,8},{8,0},{4,12},{12,4},{1,9},{9,1},{5,13},{13,5},{2,10},{10,2},... | collective-permute-start | bytes 1769480 | tf_op jit(solution)/shard_map/ppermute | solution.py:282
  55.4 15.0 %collective-permute-start.5 = (bf16[256,768]{1,0:T(8,128)(2,1)S(1)}, bf16[256,768]{1,0:T(8,128)(2,1)S(1)}, u32[]{:S(2)}, u32[]{:S(2)}) collective-permute-start(bf16[256,768]{1,0:T(8,128)(2,1)S(1)} %copy-done.5), channel_id=1, source_target_pairs={{0,1},{1,0},{2,3},{3,2},{4,5},{5,4},{6,7},{7,6},{8,9},{9,8},{10,11... | collective-permute-start | bytes 1179656 | tf_op jit(solution)/shard_map/ppermute | solution.py:295
  57.2 5.2 %copy-start.1 = (bf16[160,3072]{1,0:T(8,128)(2,1)}, bf16[160,3072]{1,0:T(8,128)(2,1)S(1)}, u32[]{:S(2)}) copy-start(bf16[160,3072]{1,0:T(8,128)(2,1)S(1)} %collective-permute-done.13.refs_2_.refs_10_) | copy-start | bytes 2949124
  62.4 9.4 %collective-permute-start.14 = (bf16[160,768]{1,0:T(8,128)(2,1)S(1)}, bf16[160,768]{1,0:T(8,128)(2,1)S(1)}, u32[]{:S(2)}, u32[]{:S(2)}) collective-permute-start(bf16[160,768]{1,0:T(8,128)(2,1)S(1)} %get-tuple-element.42), channel_id=1, source_target_pairs={{0,1},{1,0},{2,3},{3,2},{4,5},{5,4},{6,7},{7,6},{8,9},{9,8},{10,11... | collective-permute-start | bytes 737288 | tf_op jit(solution)/shard_map/ppermute | solution.py:336
  70.4 8.2 %copy-start.2 = (bf16[96,3072]{1,0:T(8,128)(2,1)}, bf16[96,3072]{1,0:T(8,128)(2,1)S(1)}, u32[]{:S(2)}) copy-start(bf16[96,3072]{1,0:T(8,128)(2,1)S(1)} %collective-permute-done.16.refs_1_.refs_9_) | copy-start | bytes 1769476
  70.4 1.4 %copy-start.16 = (bf16[256,768]{1,0:T(8,128)(2,1)}, bf16[256,768]{1,0:T(8,128)(2,1)S(1)}, u32[]{:S(2)}) copy-start(bf16[256,768]{1,0:T(8,128)(2,1)S(1)} %collective-permute-done.5) | copy-start | bytes 1179652
  71.8 2.0 %collective-permute-start.17 = (bf16[96,3072]{1,0:T(8,128)(2,1)S(1)}, bf16[96,3072]{1,0:T(8,128)(2,1)S(1)}, u32[]{:S(2)}, u32[]{:S(2)}) collective-permute-start(bf16[96,3072]{1,0:T(8,128)(2,1)S(1)} %collective-permute-done.16.refs_1_.refs_9_), channel_id=1, source_target_pairs={{0,4},{4,0},{8,12},{12,8},{1,5},{5,1},{9,13},{13,9},{2,6},{6,2},{1... | collective-permute-start | bytes 1769480 | tf_op jit(solution)/shard_map/ppermute | solution.py:320
  71.8 8.3 %copy-start.17 = (bf16[256,768]{1,0:T(8,128)(2,1)S(1)}, bf16[256,768]{1,0:T(8,128)(2,1)}, u32[]{:S(2)}) copy-start(bf16[256,768]{1,0:T(8,128)(2,1)} %copy-done.16) | copy-start | bytes 1179652
  73.8 4.8 %copy-start.3 = (bf16[96,3072]{1,0:T(8,128)(2,1)}, bf16[96,3072]{1,0:T(8,128)(2,1)S(1)}, u32[]{:S(2)}) copy-start(bf16[96,3072]{1,0:T(8,128)(2,1)S(1)} %collective-permute-done.17.refs_2_.refs_11_) | copy-start | bytes 1769476
  78.6 9.5 %collective-permute-start.18 = (bf16[96,768]{1,0:T(8,128)(2,1)S(1)}, bf16[96,768]{1,0:T(8,128)(2,1)S(1)}, u32[]{:S(2)}, u32[]{:S(2)}) collective-permute-start(bf16[96,768]{1,0:T(8,128)(2,1)S(1)} %get-tuple-element.50), channel_id=1, source_target_pairs={{0,1},{1,0},{2,3},{3,2},{4,5},{5,4},{6,7},{7,6},{8,9},{9,8},{10,11... | collective-permute-start | bytes 442376 | tf_op jit(solution)/shard_map/ppermute | solution.py:336
  80.2 18.7 %collective-permute-start.15 = (bf16[160,768]{1,0:T(8,128)(2,1)S(1)}, bf16[160,768]{1,0:T(8,128)(2,1)S(1)}, u32[]{:S(2)}, u32[]{:S(2)}) collective-permute-start(bf16[160,768]{1,0:T(8,128)(2,1)S(1)} %select_convert_fusion), channel_id=1, source_target_pairs={{0,2},{2,0},{1,3},{3,1},{4,6},{6,4},{5,7},{7,5},{8,10},{10,8},{9,1... | collective-permute-start | bytes 737288 | tf_op jit(solution)/shard_map/ppermute | solution.py:355
  88.2 13.1 %collective-permute-start.19 = (bf16[96,768]{1,0:T(8,128)(2,1)S(1)}, bf16[96,768]{1,0:T(8,128)(2,1)S(1)}, u32[]{:S(2)}, u32[]{:S(2)}) collective-permute-start(bf16[96,768]{1,0:T(8,128)(2,1)S(1)} %select_convert_fusion.1.refs_13_), channel_id=1, source_target_pairs={{0,2},{2,0},{1,3},{3,1},{4,6},{6,4},{5,7},{7,5},{8,10},{10,8},{9,1... | collective-permute-start | bytes 442376 | tf_op jit(solution)/shard_map/ppermute | solution.py:355
  96.7 4.7 %copy-start.9 = (f32[256,1536]{1,0:T(8,128)S(1)}, f32[256,1536]{1,0:T(8,128)}, u32[]{:S(2)}) copy-start(f32[256,1536]{1,0:T(8,128)} %copy-done.8) | copy-start | bytes 4718596
  96.7 4.7 %copy-start.14 = (bf16[256,768]{1,0:T(8,128)(2,1)S(1)}, bf16[256,768]{1,0:T(8,128)(2,1)}, u32[]{:S(2)}) copy-start(bf16[256,768]{1,0:T(8,128)(2,1)} %param.10) | copy-start | bytes 1179652
  101.9 3.6 %collective-permute-start.20 = (f32[2,256]{1,0:T(2,128)S(1)}, f32[2,256]{1,0:T(2,128)S(1)}, u32[]{:S(2)}, u32[]{:S(2)}) collective-permute-start(f32[2,256]{1,0:T(2,128)S(1)} %pad_maximum_fusion.1), channel_id=1, source_target_pairs={{0,8},{8,0},{4,12},{12,4},{1,9},{9,1},{5,13},{13,5},{2,10},{10,2},... | collective-permute-start | bytes 6152 | tf_op jit(solution)/shard_map/ppermute | solution.py:227
  105.6 1.2 %collective-permute-start.21 = (f32[2,256]{1,0:T(2,128)S(1)}, f32[2,256]{1,0:T(2,128)S(1)}, u32[]{:S(2)}, u32[]{:S(2)}) collective-permute-start(f32[2,256]{1,0:T(2,128)S(1)} %fusion.53), channel_id=1, source_target_pairs={{0,4},{4,0},{8,12},{12,8},{1,5},{5,1},{9,13},{13,9},{2,6},{6,2},{1... | collective-permute-start | bytes 6152 | tf_op jit(solution)/shard_map/ppermute | solution.py:228

commit v4 on v3

--- a/solution.py
+++ b/solution.py
@@ -26,6 +26,7 @@
 PIECES = (160, 96)
 STARTS = tuple(sum(PIECES[:k]) for k in range(len(PIECES)))
 TURNS = ((0,), (1,))
+SWAPS = (((0, 112), (112, 160)), ((0, 96),))
 PART = 128
 
 
@@ -192,7 +193,7 @@
     places, parts, grads, tile=768, low=0, high=None, held=None, hold=(), pin=True
 ):
     width = parts[0].shape[1]
-    tokens = sum(part.shape[0] for part in parts)
+    tokens = parts[0].shape[0]
     columns = grads[0].shape[1]
     high = columns // tile if high is None else high
     extra = list(hold) + ([] if held is None else [held])
@@ -204,7 +205,7 @@
         functools.partial(weight_kernel, len(grads), len(extra)),
         grid=(high - low,),
         in_specs=[pl.BlockSpec(memory_space=pltpu.SMEM)]
-        + [pl.BlockSpec(part.shape, lambda i: (0, 0)) for part in parts]
+        + [pl.BlockSpec((tokens // 4, width), lambda i, j=j: (j, 0)) for j in range(4)]
         + [pl.BlockSpec((grad.shape[0], tile), lambda i: (0, i + low)) for grad in grads]
         + [pl.BlockSpec(memory_space=pl.ANY)] * len(extra),
         out_specs=[
@@ -254,10 +255,12 @@
     moments = row_sum(moments)
     side_q = lax.ppermute(qkv_cotangent, "row", CORE)
 
-    sample_ids = jnp.arange(samples, dtype=jnp.int32)
-    onehot = (sample_ids[:, None] == sample_of[None, :]).astype(jnp.float32)
-    omega_sample = sample_weights(onehot, timestep, reward)
-    own_onehot = lax.dynamic_slice_in_dim(onehot, col_id * tok_col, tok_col, 1)
+    sample_ids = jnp.arange(samples, dtype=jnp.int32)[:, None]
+    omega_sample = sample_weights(
+        (sample_ids == sample_of[None, :]).astype(jnp.float32), timestep, reward
+    )
+    own_samples = lax.dynamic_slice_in_dim(sample_of, col_id * tok_col, tok_col)
+    own_onehot = (sample_ids == own_samples[None, :]).astype(jnp.float32)
     own_mod = lookup(own_onehot, modulation.reshape(samples, 2 * width_row))
     own_omega = lookup(own_onehot, omega_sample[:, None])
     offset = own_mod[:, :width_row]
@@ -267,8 +270,10 @@
     xhat = (latents32 - mean) * rstd
     normed = ((xhat * scale + offset) * own_omega).astype(jnp.bfloat16)
     scale_omega = scale * own_omega
-    across = lax.ppermute(normed, "col", SKIP)
-    normed_next = lax.ppermute(normed, "col", NEXT)
+    gathered = lax.all_to_all(
+        jnp.broadcast_to(normed[None], (4,) + normed.shape), "col", 0, 0, tiled=False
+    )
+    parts = [gathered.reshape(-1, width_row)] * 4
 
     mlp_preact = after(mlp_preact, normed)
     own_m = [
@@ -294,13 +299,11 @@
     )
     near_next = lax.ppermute(near_send, "col", NEXT)
 
-    ready_q = after(far_q, near_send, across, normed_next)
+    ready_q = after(far_q, near_send)
     farside_q = [
         lax.ppermute(ready_q[low : low + PART], "row", CORE) for low in range(0, tok_row, PART)
     ]
-    across_next = lax.ppermute(after(across, near_send), "col", NEXT)
-    places = jnp.stack([row_id ^ col_id ^ j for j in (0, 2, 1, 3)])
-    parts = [normed, across, normed_next, across_next]
+    places = jnp.stack([row_id ^ j for j in range(4)])
     takes_near = row_id // 2 == col_id // 2
 
     far, mark = back(
@@ -313,7 +316,6 @@
         jnp.float32,
     )
     q_parts = [qkv_cotangent, side_q, far_q] + farside_q
-    qkv_total, mark = weight_grad(places, parts, q_parts, high=1, hold=[mark])
     ready, farside_m, halves = [mark], [], []
     for index, turn in enumerate(TURNS):
         for k in turn:
@@ -335,24 +337,23 @@
         )
         send = lax.ppermute(send, "col", NEXT)
         if index == 0:
-            qkv_total, mark = weight_grad(
-                places, parts, q_parts, low=1, held=qkv_total, hold=[mark]
-            )
+            qkv_total, mark = weight_grad(places, parts, q_parts, hold=[mark])
             ready = [mark, send, near_next]
         halves.append((start, size, keep, send))
 
     all_m = own_m + side_m + far_m + farside_m
     mlp_total, mark = weight_grad(places, parts, all_m, high=1, hold=[mark])
     incoming = []
-    for index, (start, size, keep, send) in enumerate(halves):
-        if index == len(halves) - 1:
-            keep, send = after((keep, send), mark)
+    for turn, (start, size, keep, send) in enumerate(halves):
+        if turn == len(halves) - 1:
+            keep, send = after((keep, send), mark, *[arrived for _, arrived in incoming])
         far_half = keep.astype(jnp.float32) + send.astype(jnp.float32)
         near_piece = near_keep[start : start + size].astype(jnp.float32)
         near_piece += near_next[start : start + size].astype(jnp.float32)
         own = jnp.where(takes_near, near_piece, far_half)
         other = jnp.where(takes_near, far_half, near_piece).astype(jnp.bfloat16)
-        incoming.append((own, lax.ppermute(other, "col", SKIP)))
+        for low, high in SWAPS[turn]:
+            incoming.append((own[low:high], lax.ppermute(other[low:high], "col", SKIP)))
     mlp_total, mark = weight_grad(places, parts, all_m, low=1, held=mlp_total, hold=[mark, other])
 
     incoming = jnp.concatenate(

time: 108 us -> 107 us (level)
  waiting for transfers between devices: 23.4 us -> 19.6 us
  starting transfers between devices: 21.4 us -> 23.4 us
  local copies, waits for them, and re-layouts: 4.78 us -> 6.72 us
  Pallas kernels: 48.7 us -> 46.9 us
    ppermute x5 -> x3, waiting for transfers between devices: 11.7 us -> 0.55 us  [on_grid(): incoming.append((own[low:high], lax.ppermute(other[low:high], 'col', SKIP)))]
    ppermute x2, waiting for transfers between devices: 1.18 us -> 9.37 us  [on_grid(): far_m = [lax.ppermute(part, 'row', CHIP) for part in own_m]]
    all_to_all x0 -> x1, starting transfers between devices: none -> 4.87 us  [on_grid(): lax.all_to_all(jnp.broadcast_to(normed[None], (4,) + normed.shape), 'col'...]
    ppermute x5 -> x3, starting transfers between devices: 9.09 us -> 5.31 us  [on_grid(): incoming.append((own[low:high], lax.ppermute(other[low:high], 'col', SKIP)))]
    pallas_call x4 -> x3, Pallas kernels: 23.1 us -> 20.4 us  [weight_grad(): pl.pallas_call(functools.partial(weight_kernel, len(grads), len(extra)),...]
    ppermute x2, waiting for transfers between devices: 2.38 us -> 0.45 us  [on_grid(): farside_m.append(lax.ppermute(after(far_m[k], *ready), 'row', CORE))]
    broadcast_in_dim x0 -> x1, local copies, waits for them, and re-layouts: none -> 1.24 us  [on_grid(): jnp.broadcast_to(normed[None], (4,) + normed.shape)]
    ppermute x1, waiting for transfers between devices: 0.01 us -> 1.09 us  [on_grid(): far_q = lax.ppermute(after(qkv_cotangent, moments), 'row', CHIP)]
  transfers between devices with their start and end apart: 22 -> 21, of which waited for: 15 -> 11; matrix products, arithmetic and copies ran while one was open for 7% -> 9% of each run, Pallas kernels for 41% -> 44%
where the time goes in v4:
time: 107 us; the launch traced here: 106 us
  Pallas kernels  46.9 us (44%)
  starting transfers between devices  23.4 us (22%)
  waiting for transfers between devices  19.6 us (18%)
  other arithmetic  7.48 us (7%)
  local copies, waits for them, and re-layouts  6.72 us (6%)
    pallas_call x4, Pallas kernels, back(): pl.pallas_call(functools.partial(back_kernel, layout, tile, order is not...  26.5 us
    pallas_call x3, Pallas kernels, weight_grad(): pl.pallas_call(functools.partial(weight_kernel, len(grads), len(extra)),...  20.4 us
    ppermute x2, waiting for transfers between devices, on_grid(): far_m = [lax.ppermute(part, 'row', CHIP) for part in own_m]  9.37 us
    ppermute x3, starting transfers between devices, on_grid(): incoming.append((own[low:high], lax.ppermute(other[low:high], 'col', SKIP)))  5.31 us
    all_to_all x1, starting transfers between devices, on_grid(): lax.all_to_all(jnp.broadcast_to(normed[None], (4,) + normed.shape), 'col'...  4.87 us
    ppermute x2, starting transfers between devices, row_sum(): pair += lax.ppermute(pair, 'row', CHIP)  4.44 us
    unnamed x37, local copies, waits for them, and re-layouts  3.37 us
    convert_element_type x2, other arithmetic, on_grid(): own_m = [(mlp_cotangent[start:start + size].astype(jnp.float32) * gelu_sl...  3.01 us
  transfers between devices with their start and end apart: 21, of which 11 were waited for; matrix products, arithmetic and copies ran while one was open for 9% of the time, Pallas kernels for 44%

profile of v4, /device:TPU:0, one launch (start us, length us, event | category | flops | bytes accessed | tf_op | source)
XLA Modules:
  0.0 106.0 jit_solution(17076475198863508483)
XLA Ops:
  0.7 1.3 %convert_reduce_fusion = (f32[256]{0:T(256)S(1)}, f32[256]{0:T(256)S(1)}) fusion(bf16[256,768]{1,0:T(8,128)(2,1)} %param.10), kind=kLoop, calls=%fused_computation.25 | loop fusion | flops 785920 | bytes 395264 | tf_op jit(solution)/shard_map/reduce_sum | solution.py:253
  2.0 3.0 %collective-permute-start = (f32[2,256]{1,0:T(2,128)S(1)}, f32[2,256]{1,0:T(2,128)S(1)}, u32[]{:S(2)}, u32[]{:S(2)}) collective-permute-start(f32[2,256]{1,0:T(2,128)S(1)} %pad_maximum_fusion), channel_id=1, source_target_pairs={{0,8},{8,0},{4,12},{12,4},{1,9},{9,1},{5,13},{13,5},{2,10},{10,2},... | collective-permute-start | bytes 6152 | tf_op jit(solution)/shard_map/ppermute | solution.py:228
  5.0 0.2 collective-permute-start.7
  5.1 0.8 copy.14
  5.9 0.8 dynamic_slice.3
  6.7 0.8 fusion.32
  7.7 0.4 collective-permute-start.1
  8.2 0.7 collective-permute-done.1
  9.0 1.0 fusion.25
  10.0 1.4 %fusion.7.refs_3_.refs_4_ = bf16[160,3072]{1,0:T(8,128)(2,1)S(1)} fusion(bf16[256,3072]{1,0:T(8,128)(2,1)S(1)} %copy-done.12, bf16[256,3072]{1,0:T(8,128)(2,1)S(1)} %copy-done.13), kind=kLoop, calls=%fused_computation.21 | loop fusion | flops 10321920 | bytes 2949120 | tf_op jit(solution)/shard_map/convert_element_type | solution.py:283
  11.4 0.4 collective-permute-start.3
  11.8 1.6 %fusion.16.refs_4_.refs_5_ = bf16[96,3072]{1,0:T(8,128)(2,1)} fusion(bf16[256,3072]{1,0:T(8,128)(2,1)S(1)} %copy-done.12, bf16[256,3072]{1,0:T(8,128)(2,1)S(1)} %copy-done.13), kind=kLoop, calls=%fused_computation.33 | loop fusion | flops 6193152 | bytes 1769472 | tf_op jit(solution)/shard_map/convert_element_type | solution.py:283
  13.4 0.2 collective-permute-start.4
  13.7 1.9 %collective-permute-start.6 = (bf16[160,3072]{1,0:T(8,128)(2,1)S(1)}, bf16[160,3072]{1,0:T(8,128)(2,1)S(1)}, u32[]{:S(2)}, u32[]{:S(2)}) collective-permute-start(bf16[160,3072]{1,0:T(8,128)(2,1)S(1)} %fusion.7.refs_3_.refs_4_), channel_id=1, source_target_pairs={{0,8},{8,0},{4,12},{12,4},{1,9},{9,1},{5,13},{13,5},{2,10},{10,2},... | collective-permute-start | bytes 2949128 | tf_op jit(solution)/shard_map/ppermute | solution.py:287
  15.5 1.2 %broadcast_in_dim.2 = bf16[4,256,768]{2,1,0:T(8,128)(2,1)} broadcast(bf16[256,768]{1,0:T(8,128)(2,1)S(1)} %copy-done.14), dimensions={1,2} | broadcast | bytes 1966080 | tf_op jit(solution)/shard_map/broadcast_in_dim | solution.py:274
  16.8 4.9 %all-to-all-start = ((bf16[4,256,768]{2,1,0:T(8,128)(2,1)}), bf16[4,256,768]{2,1,0:T(8,128)(2,1)}, u32[]{:S(2)}, u32[]{:S(2)}) async-start(bf16[4,256,768]{2,1,0:T(8,128)(2,1)} %broadcast_in_dim.2), calls=%async_computation | async-start | bytes 3145728 | tf_op jit(solution)/shard_map/all_to_all | solution.py:273
  21.7 0.9 copy-done.7
  22.6 10.3 %shard_map.121 = (bf16[256,768]{1,0:T(8,128)(2,1)S(1)}, bf16[256,768]{1,0:T(8,128)(2,1)}, f32[8,128]{1,0:T(8,128)}) custom-call(s32[2]{0:T(128)S(1)} %pad_add_fusion.refs_0_, bf16[256,2304]{1,0:T(8,128)(2,1)} %refs_4_.1, bf16[256,2304]{1,0:T(8,128)(2,1)} %collective-permute-done.2.refs_2_.refs_5_, bf16[160,3072]{1,0:T(8,128)(2,1)} %copy-done.4, ...), custom_call_target="tpu_custom_call" | custom-call | flops 1 | bytes 1 | tf_op jit(solution)/shard_map/pallas_call | solution.py:154
  33.0 1.1 %collective-permute-done.7.refs_0_.refs_6_ = bf16[256,2304]{1,0:T(8,128)(2,1)} collective-permute-done((bf16[256,2304]{1,0:T(8,128)(2,1)}, bf16[256,2304]{1,0:T(8,128)(2,1)}, u32[]{:S(2)}, u32[]{:S(2)}) %collective-permute-start.7) | collective-permute-done | bytes 1179680 | tf_op jit(solution)/shard_map/ppermute | solution.py:254
  34.0 1.3 %fusion.55 = (bf16[128,2304]{1,0:T(8,128)(2,1)S(1)}, bf16[128,2304]{1,0:T(8,128)(2,1)S(1)}) fusion(bf16[256,2304]{1,0:T(8,128)(2,1)} %collective-permute-done.7.refs_0_.refs_6_), kind=kLoop, calls=%fused_computation.95 | loop fusion | bytes 2359296 | tf_op jit(solution)/shard_map/slice | solution.py:304
  35.4 0.5 collective-permute-start.8
  35.9 1.5 %collective-permute-done.9.refs_2_.refs_8_ = bf16[128,2304]{1,0:T(8,128)(2,1)S(1)} collective-permute-done((bf16[128,2304]{1,0:T(8,128)(2,1)S(1)}, bf16[128,2304]{1,0:T(8,128)(2,1)S(1)}, u32[]{:S(2)}, u32[]{:S(2)}) %collective-permute-start.9) | collective-permute-done | bytes 589856 | tf_op jit(solution)/shard_map/ppermute | solution.py:304
  37.4 0.8 collective-permute-done.8.refs_1_.refs_7_
  38.3 0.8 copy-done.11
  39.1 6.1 %shard_map.122 = (f32[512,768]{1,0:T(8,128)}, f32[8,128]{1,0:T(8,128)S(1)}) custom-call(bf16[256,2304]{1,0:T(8,128)(2,1)} %collective-permute-done.7.refs_0_.refs_6_, bf16[128,2304]{1,0:T(8,128)(2,1)} %copy-done.11, bf16[128,2304]{1,0:T(8,128)(2,1)} %copy-done.10, bf16[768,2304]{1,0:T(8,128)(2,1)} %refs_3_.3), custom_call_target="tpu_custom_call" | custom-call | flops 1 | bytes 1 | tf_op jit(solution)/shard_map/pallas_call | solution.py:154
  45.3 9.4 %collective-permute-done.6.refs_1_.refs_8_ = bf16[160,3072]{1,0:T(8,128)(2,1)S(1)} collective-permute-done((bf16[160,3072]{1,0:T(8,128)(2,1)S(1)}, bf16[160,3072]{1,0:T(8,128)(2,1)S(1)}, u32[]{:S(2)}, u32[]{:S(2)}) %collective-permute-start.6) | collective-permute-done | bytes 983072 | tf_op jit(solution)/shard_map/ppermute | solution.py:287
  54.6 0.3 collective-permute-start.13
  54.9 1.8 %collective-permute-start.5 = (bf16[256,768]{1,0:T(8,128)(2,1)}, bf16[256,768]{1,0:T(8,128)(2,1)S(1)}, u32[]{:S(2)}, u32[]{:S(2)}) collective-permute-start(bf16[256,768]{1,0:T(8,128)(2,1)} %get-tuple-element.31), channel_id=1, source_target_pairs={{0,1},{1,0},{2,3},{3,2},{4,5},{5,4},{6,7},{7,6},{8,9},{9,8},{10,11... | collective-permute-start | bytes 1179656 | tf_op jit(solution)/shard_map/ppermute | solution.py:300
  56.7 0.5 collective-permute-done.10.refs_2_.refs_10_
  57.2 5.2 %shard_map.123 = (bf16[160,768]{1,0:T(8,128)(2,1)S(1)}, bf16[160,768]{1,0:T(8,128)(2,1)S(1)}, f32[8,128]{1,0:T(8,128)S(1)}) custom-call(s32[2]{0:T(128)S(1)} %pad_add_fusion.refs_0_, bf16[160,3072]{1,0:T(8,128)(2,1)S(1)} %collective-permute-done.6.refs_1_.refs_8_, bf16[160,3072]{1,0:T(8,128)(2,1)S(1)} %collective-permute-done.10.refs_2_.refs_10_, ...), custom_call_target="tpu_custom_call" | custom-call | flops 1 | bytes 1 | tf_op jit(solution)/shard_map/pallas_call | solution.py:154
  62.4 1.6 %collective-permute-start.11 = (bf16[160,768]{1,0:T(8,128)(2,1)S(1)}, bf16[160,768]{1,0:T(8,128)(2,1)S(1)}, u32[]{:S(2)}, u32[]{:S(2)}) collective-permute-start(bf16[160,768]{1,0:T(8,128)(2,1)S(1)} %get-tuple-element.38), channel_id=1, source_target_pairs={{0,1},{1,0},{2,3},{3,2},{4,5},{5,4},{6,7},{7,6},{8,9},{9,8},{10,11... | collective-permute-start | bytes 737288 | tf_op jit(solution)/shard_map/ppermute | solution.py:338
  64.1 7.9 %shard_map.124 = (bf16[768,2304]{1,0:T(8,128)(2,1)}, f32[8,128]{1,0:T(8,128)S(1)}) custom-call(s32[4]{0:T(128)S(1)} %pad_add_fusion.1.places, bf16[1024,768]{1,0:T(8,128)(2,1)} %bitcast.12.refs_0_.refs_1_.refs_2_.refs_3_, bf16[1024,768]{1,0:T(8,128)(2,1)} %bitcast.12.refs_0_.refs_1_.refs_2_.refs_3_, ...), custom_call_target="tpu_custom_call" | custom-call | flops 1 | bytes 1 | tf_op jit(solution)/shard_map/pallas_call | solution.py:204
  72.1 0.4 collective-permute-done.11
  72.7 2.3 %collective-permute-start.12 = (bf16[112,768]{1,0:T(8,128)(2,1)S(1)}, bf16[112,768]{1,0:T(8,128)(2,1)S(1)}, u32[]{:S(2)}, u32[]{:S(2)}) collective-permute-start(bf16[112,768]{1,0:T(8,128)(2,1)S(1)} %slice.86), channel_id=1, source_target_pairs={{0,2},{2,0},{1,3},{3,1},{4,6},{6,4},{5,7},{7,5},{8,10},{10,8},{9,1... | collective-permute-start | bytes 516104 | tf_op jit(solution)/shard_map/ppermute | solution.py:356
  75.0 4.8 %shard_map.125 = (bf16[96,768]{1,0:T(8,128)(2,1)S(1)}, bf16[96,768]{1,0:T(8,128)(2,1)S(1)}, f32[8,128]{1,0:T(8,128)S(1)}) custom-call(s32[2]{0:T(128)S(1)} %pad_add_fusion.refs_0_, bf16[96,3072]{1,0:T(8,128)(2,1)S(1)} %collective-permute-done.13.refs_1_.refs_9_, bf16[96,3072]{1,0:T(8,128)(2,1)S(1)} %collective-permute-done.14.refs_2_.refs_11_, ...), custom_call_target="tpu_custom_call" | custom-call | flops 1 | bytes 1 | tf_op jit(solution)/shard_map/pallas_call | solution.py:154
  79.9 1.4 %collective-permute-start.15 = (bf16[96,768]{1,0:T(8,128)(2,1)S(1)}, bf16[96,768]{1,0:T(8,128)(2,1)S(1)}, u32[]{:S(2)}, u32[]{:S(2)}) collective-permute-start(bf16[96,768]{1,0:T(8,128)(2,1)S(1)} %get-tuple-element.45), channel_id=1, source_target_pairs={{0,1},{1,0},{2,3},{3,2},{4,5},{5,4},{6,7},{7,6},{8,9},{9,8},{10,11... | collective-permute-start | bytes 442376 | tf_op jit(solution)/shard_map/ppermute | solution.py:338
  81.2 1.8 %collective-permute-start.16 = (bf16[48,768]{1,0:T(8,128)(2,1)S(1)}, bf16[48,768]{1,0:T(8,128)(2,1)S(1)}, u32[]{:S(2)}, u32[]{:S(2)}) collective-permute-start(bf16[48,768]{1,0:T(8,128)(2,1)S(1)} %slice.87), channel_id=1, source_target_pairs={{0,2},{2,0},{1,3},{3,1},{4,6},{6,4},{5,7},{7,5},{8,10},{10,8},{9,1... | collective-permute-start | bytes 221192 | tf_op jit(solution)/shard_map/ppermute | solution.py:356
  83.0 4.4 %shard_map.126 = (bf16[768,3072]{1,0:T(8,128)(2,1)}, f32[8,128]{1,0:T(8,128)S(1)}) custom-call(s32[4]{0:T(128)S(1)} %pad_add_fusion.1.places, bf16[1024,768]{1,0:T(8,128)(2,1)} %bitcast.12.refs_0_.refs_1_.refs_2_.refs_3_, bf16[1024,768]{1,0:T(8,128)(2,1)} %bitcast.12.refs_0_.refs_1_.refs_2_.refs_3_, ...), custom_call_target="tpu_custom_call" | custom-call | flops 1 | bytes 1 | tf_op jit(solution)/shard_map/pallas_call | solution.py:204
  87.4 1.4 %collective-permute-done.15 = bf16[96,768]{1,0:T(8,128)(2,1)S(1)} collective-permute-done((bf16[96,768]{1,0:T(8,128)(2,1)S(1)}, bf16[96,768]{1,0:T(8,128)(2,1)S(1)}, u32[]{:S(2)}, u32[]{:S(2)}) %collective-permute-start.15) | collective-permute-done | bytes 147488 | tf_op jit(solution)/shard_map/ppermute | solution.py:338
  88.9 1.2 %collective-permute-start.17 = (bf16[96,768]{1,0:T(8,128)(2,1)S(1)}, bf16[96,768]{1,0:T(8,128)(2,1)S(1)}, u32[]{:S(2)}, u32[]{:S(2)}) collective-permute-start(bf16[96,768]{1,0:T(8,128)(2,1)S(1)} %select_convert_fusion.1.refs_13_), channel_id=1, source_target_pairs={{0,2},{2,0},{1,3},{3,1},{4,6},{6,4},{5,7},{7,5},{8,10},{10,8},{9,1... | collective-permute-start | bytes 442376 | tf_op jit(solution)/shard_map/ppermute | solution.py:356
  90.1 8.1 %shard_map.127 = (bf16[768,3072]{1,0:T(8,128)(2,1)}, f32[8,128]{1,0:T(8,128)}) custom-call(s32[4]{0:T(128)S(1)} %pad_add_fusion.1.places, bf16[1024,768]{1,0:T(8,128)(2,1)} %bitcast.12.refs_0_.refs_1_.refs_2_.refs_3_, bf16[1024,768]{1,0:T(8,128)(2,1)} %bitcast.12.refs_0_.refs_1_.refs_2_.refs_3_, ...), custom_call_target="tpu_custom_call", output_to_operand_aliasing={{0}: (15, {})} | custom-call | flops 1 | bytes 1 | tf_op jit(solution)/shard_map/pallas_call | solution.py:204
  98.2 0.5 collective-permute-done.17
  98.9 0.7 copy-done.6
  99.6 0.5 fusion.54
  100.1 1.4 %collective-permute-start.18 = (f32[2,256]{1,0:T(2,128)S(1)}, f32[2,256]{1,0:T(2,128)S(1)}, u32[]{:S(2)}, u32[]{:S(2)}) collective-permute-start(f32[2,256]{1,0:T(2,128)S(1)} %pad_maximum_fusion.1), channel_id=1, source_target_pairs={{0,8},{8,0},{4,12},{12,4},{1,9},{9,1},{5,13},{13,5},{2,10},{10,2},... | collective-permute-start | bytes 6152 | tf_op jit(solution)/shard_map/ppermute | solution.py:228
  101.5 2.2 %collective-permute-done.18 = f32[2,256]{1,0:T(2,128)S(1)} collective-permute-done((f32[2,256]{1,0:T(2,128)S(1)}, f32[2,256]{1,0:T(2,128)S(1)}, u32[]{:S(2)}, u32[]{:S(2)}) %collective-permute-start.18) | collective-permute-done | bytes 2080 | tf_op jit(solution)/shard_map/ppermute | solution.py:228
  103.8 1.1 %collective-permute-done.19 = f32[2,256]{1,0:T(2,128)S(1)} collective-permute-done((f32[2,256]{1,0:T(2,128)S(1)}, f32[2,256]{1,0:T(2,128)S(1)}, u32[]{:S(2)}, u32[]{:S(2)}) %collective-permute-start.19) | collective-permute-done | bytes 2080 | tf_op jit(solution)/shard_map/ppermute | solution.py:229
  105.0 1.0 fusion.29
  (68 shorter events, 1.2 us)
Async XLA Ops:
  0.6 8.3 %copy-start.8 = (bf16[256,768]{1,0:T(8,128)(2,1)S(1)}, bf16[256,768]{1,0:T(8,128)(2,1)}, u32[]{:S(2)}) copy-start(bf16[256,768]{1,0:T(8,128)(2,1)} %param.10) | copy-start | bytes 1179652
  0.6 6.9 %copy-start.15 = (s32[1024]{0:T(1024)S(1)}, s32[1024]{0:T(1024)}, u32[]{:S(2)}) copy-start(s32[1024]{0:T(1024)} %param.12) | copy-start | bytes 12292
  0.7 7.5 %copy-start.16 = (f32[8]{0:T(128)S(1)}, f32[8]{0:T(128)}, u32[]{:S(2)}) copy-start(f32[8]{0:T(128)} %param.14) | copy-start | bytes 100
  0.7 7.4 %copy-start.17 = (s32[8]{0:T(128)S(1)}, s32[8]{0:T(128)}, u32[]{:S(2)}) copy-start(s32[8]{0:T(128)} %param.13) | copy-start | bytes 100
  2.0 5.7 %collective-permute-start = (f32[2,256]{1,0:T(2,128)S(1)}, f32[2,256]{1,0:T(2,128)S(1)}, u32[]{:S(2)}, u32[]{:S(2)}) collective-permute-start(f32[2,256]{1,0:T(2,128)S(1)} %pad_maximum_fusion), channel_id=1, source_target_pairs={{0,8},{8,0},{4,12},{12,4},{1,9},{9,1},{5,13},{13,5},{2,10},{10,2},... | collective-permute-start | bytes 6152 | tf_op jit(solution)/shard_map/ppermute | solution.py:228
  5.0 17.7 %collective-permute-start.2 = (bf16[256,2304]{1,0:T(8,128)(2,1)}, bf16[256,2304]{1,0:T(8,128)(2,1)}, u32[]{:S(2)}, u32[]{:S(2)}) collective-permute-start(bf16[256,2304]{1,0:T(8,128)(2,1)} %refs_4_.1), channel_id=1, source_target_pairs={{0,4},{4,0},{8,12},{12,8},{1,5},{5,1},{9,13},{13,9},{2,6},{6,2},{1... | collective-permute-start | bytes 3538952 | tf_op jit(solution)/shard_map/ppermute | solution.py:256
  5.0 29.1 %collective-permute-start.7 = (bf16[256,2304]{1,0:T(8,128)(2,1)}, bf16[256,2304]{1,0:T(8,128)(2,1)}, u32[]{:S(2)}, u32[]{:S(2)}) collective-permute-start(bf16[256,2304]{1,0:T(8,128)(2,1)} %refs_4_.1), channel_id=1, source_target_pairs={{0,8},{8,0},{4,12},{12,4},{1,9},{9,1},{5,13},{13,5},{2,10},{10,2},... | collective-permute-start | bytes 3538952 | tf_op jit(solution)/shard_map/ppermute | solution.py:254
  6.7 3.3 %copy-start.13 = (bf16[256,3072]{1,0:T(8,128)(2,1)S(1)}, bf16[256,3072]{1,0:T(8,128)(2,1)}, u32[]{:S(2)}) copy-start(bf16[256,3072]{1,0:T(8,128)(2,1)} %param.16) | copy-start | bytes 4718596
  7.5 1.4 %copy-start.5 = (f32[256,1536]{1,0:T(8,128)}, f32[256,1536]{1,0:T(8,128)S(1)}, u32[]{:S(2)}) copy-start(f32[256,1536]{1,0:T(8,128)S(1)} %fusion.32) | copy-start | bytes 4718596
  7.5 2.5 %copy-start.12 = (bf16[256,3072]{1,0:T(8,128)(2,1)S(1)}, bf16[256,3072]{1,0:T(8,128)(2,1)}, u32[]{:S(2)}) copy-start(bf16[256,3072]{1,0:T(8,128)(2,1)} %param.17) | copy-start | bytes 4718596
  7.7 1.2 %collective-permute-start.1 = (f32[2,256]{1,0:T(2,128)S(1)}, f32[2,256]{1,0:T(2,128)S(1)}, u32[]{:S(2)}, u32[]{:S(2)}) collective-permute-start(f32[2,256]{1,0:T(2,128)S(1)} %fusion.53), channel_id=1, source_target_pairs={{0,4},{4,0},{8,12},{12,8},{1,5},{5,1},{9,13},{13,9},{2,6},{6,2},{1... | collective-permute-start | bytes 6152 | tf_op jit(solution)/shard_map/ppermute | solution.py:229
  11.4 5.4 %copy-start.4 = (bf16[160,3072]{1,0:T(8,128)(2,1)}, bf16[160,3072]{1,0:T(8,128)(2,1)S(1)}, u32[]{:S(2)}) copy-start(bf16[160,3072]{1,0:T(8,128)(2,1)S(1)} %fusion.7.refs_3_.refs_4_) | copy-start | bytes 2949124
  11.4 4.2 %copy-start.14 = (bf16[256,768]{1,0:T(8,128)(2,1)S(1)}, bf16[256,768]{1,0:T(8,128)(2,1)}, u32[]{:S(2)}) copy-start(bf16[256,768]{1,0:T(8,128)(2,1)} %fusion.25) | copy-start | bytes 1179652
  11.4 10.3 %collective-permute-start.3 = (bf16[160,3072]{1,0:T(8,128)(2,1)S(1)}, bf16[160,3072]{1,0:T(8,128)(2,1)S(1)}, u32[]{:S(2)}, u32[]{:S(2)}) collective-permute-start(bf16[160,3072]{1,0:T(8,128)(2,1)S(1)} %fusion.7.refs_3_.refs_4_), channel_id=1, source_target_pairs={{0,4},{4,0},{8,12},{12,8},{1,5},{5,1},{9,13},{13,9},{2,6},{6,2},{1... | collective-permute-start | bytes 2949128 | tf_op jit(solution)/shard_map/ppermute | solution.py:286
  13.4 8.2 %collective-permute-start.4 = (bf16[96,3072]{1,0:T(8,128)(2,1)}, bf16[96,3072]{1,0:T(8,128)(2,1)}, u32[]{:S(2)}, u32[]{:S(2)}) collective-permute-start(bf16[96,3072]{1,0:T(8,128)(2,1)} %fusion.16.refs_4_.refs_5_), channel_id=1, source_target_pairs={{0,4},{4,0},{8,12},{12,8},{1,5},{5,1},{9,13},{13,9},{2,6},{6,2},{1... | collective-permute-start | bytes 1769480 | tf_op jit(solution)/shard_map/ppermute | solution.py:286
  13.7 40.9 %collective-permute-start.6 = (bf16[160,3072]{1,0:T(8,128)(2,1)S(1)}, bf16[160,3072]{1,0:T(8,128)(2,1)S(1)}, u32[]{:S(2)}, u32[]{:S(2)}) collective-permute-start(bf16[160,3072]{1,0:T(8,128)(2,1)S(1)} %fusion.7.refs_3_.refs_4_), channel_id=1, source_target_pairs={{0,8},{8,0},{4,12},{12,4},{1,9},{9,1},{5,13},{13,5},{2,10},{10,2},... | collective-permute-start | bytes 2949128 | tf_op jit(solution)/shard_map/ppermute | solution.py:287
  16.8 47.3 %all-to-all-start = ((bf16[4,256,768]{2,1,0:T(8,128)(2,1)}), bf16[4,256,768]{2,1,0:T(8,128)(2,1)}, u32[]{:S(2)}, u32[]{:S(2)}) async-start(bf16[4,256,768]{2,1,0:T(8,128)(2,1)} %broadcast_in_dim.2), calls=%async_computation | async-start | bytes 3145728 | tf_op jit(solution)/shard_map/all_to_all | solution.py:273
  21.7 1.0 copy-start.7
  35.4 2.1 %collective-permute-start.9 = (bf16[128,2304]{1,0:T(8,128)(2,1)S(1)}, bf16[128,2304]{1,0:T(8,128)(2,1)S(1)}, u32[]{:S(2)}, u32[]{:S(2)}) collective-permute-start(bf16[128,2304]{1,0:T(8,128)(2,1)S(1)} %get-tuple-element.62), channel_id=1, source_target_pairs={{0,4},{4,0},{8,12},{12,8},{1,5},{5,1},{9,13},{13,9},{2,6},{6,2},{1... | collective-permute-start | bytes 1769480 | tf_op jit(solution)/shard_map/ppermute | solution.py:304
  35.4 2.8 %collective-permute-start.8 = (bf16[128,2304]{1,0:T(8,128)(2,1)S(1)}, bf16[128,2304]{1,0:T(8,128)(2,1)S(1)}, u32[]{:S(2)}, u32[]{:S(2)}) collective-permute-start(bf16[128,2304]{1,0:T(8,128)(2,1)S(1)} %get-tuple-element.63), channel_id=1, source_target_pairs={{0,4},{4,0},{8,12},{12,8},{1,5},{5,1},{9,13},{13,9},{2,6},{6,2},{1... | collective-permute-start | bytes 1769480 | tf_op jit(solution)/shard_map/ppermute | solution.py:304
  37.4 0.8 copy-start.10
  38.3 0.8 copy-start.11
  54.6 7.8 %copy-start = (bf16[160,3072]{1,0:T(8,128)(2,1)}, bf16[160,3072]{1,0:T(8,128)(2,1)S(1)}, u32[]{:S(2)}) copy-start(bf16[160,3072]{1,0:T(8,128)(2,1)S(1)} %collective-permute-done.6.refs_1_.refs_8_) | copy-start | bytes 2949124
  54.6 2.6 %collective-permute-start.10 = (bf16[160,3072]{1,0:T(8,128)(2,1)S(1)}, bf16[160,3072]{1,0:T(8,128)(2,1)S(1)}, u32[]{:S(2)}, u32[]{:S(2)}) collective-permute-start(bf16[160,3072]{1,0:T(8,128)(2,1)S(1)} %collective-permute-done.6.refs_1_.refs_8_), channel_id=1, source_target_pairs={{0,4},{4,0},{8,12},{12,8},{1,5},{5,1},{9,13},{13,9},{2,6},{6,2},{1... | collective-permute-start | bytes 2949128 | tf_op jit(solution)/shard_map/ppermute | solution.py:322
  54.6 17.4 %collective-permute-start.13 = (bf16[96,3072]{1,0:T(8,128)(2,1)}, bf16[96,3072]{1,0:T(8,128)(2,1)S(1)}, u32[]{:S(2)}, u32[]{:S(2)}) collective-permute-start(bf16[96,3072]{1,0:T(8,128)(2,1)} %fusion.16.refs_4_.refs_5_), channel_id=1, source_target_pairs={{0,8},{8,0},{4,12},{12,4},{1,9},{9,1},{5,13},{13,5},{2,10},{10,2},... | collective-permute-start | bytes 1769480 | tf_op jit(solution)/shard_map/ppermute | solution.py:287
  54.9 17.1 %collective-permute-start.5 = (bf16[256,768]{1,0:T(8,128)(2,1)}, bf16[256,768]{1,0:T(8,128)(2,1)S(1)}, u32[]{:S(2)}, u32[]{:S(2)}) collective-permute-start(bf16[256,768]{1,0:T(8,128)(2,1)} %get-tuple-element.31), channel_id=1, source_target_pairs={{0,1},{1,0},{2,3},{3,2},{4,5},{5,4},{6,7},{7,6},{8,9},{9,8},{10,11... | collective-permute-start | bytes 1179656 | tf_op jit(solution)/shard_map/ppermute | solution.py:300
  57.2 5.2 %copy-start.1 = (bf16[160,3072]{1,0:T(8,128)(2,1)}, bf16[160,3072]{1,0:T(8,128)(2,1)S(1)}, u32[]{:S(2)}) copy-start(bf16[160,3072]{1,0:T(8,128)(2,1)S(1)} %collective-permute-done.10.refs_2_.refs_10_) | copy-start | bytes 2949124
  62.4 10.0 %collective-permute-start.11 = (bf16[160,768]{1,0:T(8,128)(2,1)S(1)}, bf16[160,768]{1,0:T(8,128)(2,1)S(1)}, u32[]{:S(2)}, u32[]{:S(2)}) collective-permute-start(bf16[160,768]{1,0:T(8,128)(2,1)S(1)} %get-tuple-element.38), channel_id=1, source_target_pairs={{0,1},{1,0},{2,3},{3,2},{4,5},{5,4},{6,7},{7,6},{8,9},{9,8},{10,11... | collective-permute-start | bytes 737288 | tf_op jit(solution)/shard_map/ppermute | solution.py:338
  72.0 7.8 %copy-start.2 = (bf16[96,3072]{1,0:T(8,128)(2,1)}, bf16[96,3072]{1,0:T(8,128)(2,1)S(1)}, u32[]{:S(2)}) copy-start(bf16[96,3072]{1,0:T(8,128)(2,1)S(1)} %collective-permute-done.13.refs_1_.refs_9_) | copy-start | bytes 1769476
  72.4 2.6 %collective-permute-start.14 = (bf16[96,3072]{1,0:T(8,128)(2,1)S(1)}, bf16[96,3072]{1,0:T(8,128)(2,1)S(1)}, u32[]{:S(2)}, u32[]{:S(2)}) collective-permute-start(bf16[96,3072]{1,0:T(8,128)(2,1)S(1)} %collective-permute-done.13.refs_1_.refs_9_), channel_id=1, source_target_pairs={{0,4},{4,0},{8,12},{12,8},{1,5},{5,1},{9,13},{13,9},{2,6},{6,2},{1... | collective-permute-start | bytes 1769480 | tf_op jit(solution)/shard_map/ppermute | solution.py:322
  72.7 14.7 %collective-permute-start.12 = (bf16[112,768]{1,0:T(8,128)(2,1)S(1)}, bf16[112,768]{1,0:T(8,128)(2,1)S(1)}, u32[]{:S(2)}, u32[]{:S(2)}) collective-permute-start(bf16[112,768]{1,0:T(8,128)(2,1)S(1)} %slice.86), channel_id=1, source_target_pairs={{0,2},{2,0},{1,3},{3,1},{4,6},{6,4},{5,7},{7,5},{8,10},{10,8},{9,1... | collective-permute-start | bytes 516104 | tf_op jit(solution)/shard_map/ppermute | solution.py:356
  75.0 4.9 %copy-start.3 = (bf16[96,3072]{1,0:T(8,128)(2,1)}, bf16[96,3072]{1,0:T(8,128)(2,1)S(1)}, u32[]{:S(2)}) copy-start(bf16[96,3072]{1,0:T(8,128)(2,1)S(1)} %collective-permute-done.14.refs_2_.refs_11_) | copy-start | bytes 1769476
  79.9 8.9 %collective-permute-start.15 = (bf16[96,768]{1,0:T(8,128)(2,1)S(1)}, bf16[96,768]{1,0:T(8,128)(2,1)S(1)}, u32[]{:S(2)}, u32[]{:S(2)}) collective-permute-start(bf16[96,768]{1,0:T(8,128)(2,1)S(1)} %get-tuple-element.45), channel_id=1, source_target_pairs={{0,1},{1,0},{2,3},{3,2},{4,5},{5,4},{6,7},{7,6},{8,9},{9,8},{10,11... | collective-permute-start | bytes 442376 | tf_op jit(solution)/shard_map/ppermute | solution.py:338
  81.2 6.1 %collective-permute-start.16 = (bf16[48,768]{1,0:T(8,128)(2,1)S(1)}, bf16[48,768]{1,0:T(8,128)(2,1)S(1)}, u32[]{:S(2)}, u32[]{:S(2)}) collective-permute-start(bf16[48,768]{1,0:T(8,128)(2,1)S(1)} %slice.87), channel_id=1, source_target_pairs={{0,2},{2,0},{1,3},{3,1},{4,6},{6,4},{5,7},{7,5},{8,10},{10,8},{9,1... | collective-permute-start | bytes 221192 | tf_op jit(solution)/shard_map/ppermute | solution.py:356
  88.9 9.9 %collective-permute-start.17 = (bf16[96,768]{1,0:T(8,128)(2,1)S(1)}, bf16[96,768]{1,0:T(8,128)(2,1)S(1)}, u32[]{:S(2)}, u32[]{:S(2)}) collective-permute-start(bf16[96,768]{1,0:T(8,128)(2,1)S(1)} %select_convert_fusion.1.refs_13_), channel_id=1, source_target_pairs={{0,2},{2,0},{1,3},{3,1},{4,6},{6,4},{5,7},{7,5},{8,10},{10,8},{9,1... | collective-permute-start | bytes 442376 | tf_op jit(solution)/shard_map/ppermute | solution.py:356
  98.1 1.4 %copy-start.6 = (f32[256,1536]{1,0:T(8,128)S(1)}, f32[256,1536]{1,0:T(8,128)}, u32[]{:S(2)}) copy-start(f32[256,1536]{1,0:T(8,128)} %copy-done.5) | copy-start | bytes 4718596
  98.2 1.5 %copy-start.9 = (bf16[256,768]{1,0:T(8,128)(2,1)S(1)}, bf16[256,768]{1,0:T(8,128)(2,1)}, u32[]{:S(2)}) copy-start(bf16[256,768]{1,0:T(8,128)(2,1)} %param.10) | copy-start | bytes 1179652
  100.1 3.6 %collective-permute-start.18 = (f32[2,256]{1,0:T(2,128)S(1)}, f32[2,256]{1,0:T(2,128)S(1)}, u32[]{:S(2)}, u32[]{:S(2)}) collective-permute-start(f32[2,256]{1,0:T(2,128)S(1)} %pad_maximum_fusion.1), channel_id=1, source_target_pairs={{0,8},{8,0},{4,12},{12,4},{1,9},{9,1},{5,13},{13,5},{2,10},{10,2},... | collective-permute-start | bytes 6152 | tf_op jit(solution)/shard_map/ppermute | solution.py:228
  103.7 1.2 %collective-permute-start.19 = (f32[2,256]{1,0:T(2,128)S(1)}, f32[2,256]{1,0:T(2,128)S(1)}, u32[]{:S(2)}, u32[]{:S(2)}) collective-permute-start(f32[2,256]{1,0:T(2,128)S(1)} %fusion.52), channel_id=1, source_target_pairs={{0,4},{4,0},{8,12},{12,8},{1,5},{5,1},{9,13},{13,9},{2,6},{6,2},{1... | collective-permute-start | bytes 6152 | tf_op jit(solution)/shard_map/ppermute | solution.py:229

commit v5 on v4

--- a/solution.py
+++ b/solution.py
@@ -22,6 +22,7 @@
 
 CORE = [(0, 1), (1, 0), (2, 3), (3, 2)]
 CHIP = [(0, 2), (2, 0), (1, 3), (3, 1)]
+BOTH = [(0, 3), (3, 0), (1, 2), (2, 1)]
 NEXT, SKIP = CORE, CHIP
 PIECES = (160, 96)
 STARTS = tuple(sum(PIECES[:k]) for k in range(len(PIECES)))
@@ -229,6 +230,15 @@
     return pair + lax.ppermute(pair, "row", CORE)
 
 
+def row_sum_direct(pair):
+    return (
+        pair
+        + lax.ppermute(pair, "row", CORE)
+        + lax.ppermute(pair, "row", CHIP)
+        + lax.ppermute(pair, "row", BOTH)
+    )
+
+
 def on_grid(
     latents,
     modulation,
@@ -342,7 +352,7 @@
         halves.append((start, size, keep, send))
 
     all_m = own_m + side_m + far_m + farside_m
-    mlp_total, mark = weight_grad(places, parts, all_m, high=1, hold=[mark])
+    mlp_total, mark = weight_grad(places, parts, all_m, tile=1024, high=1, hold=[mark])
     incoming = []
     for turn, (start, size, keep, send) in enumerate(halves):
         if turn == len(halves) - 1:
@@ -354,12 +364,14 @@
         other = jnp.where(takes_near, far_half, near_piece).astype(jnp.bfloat16)
         for low, high in SWAPS[turn]:
             incoming.append((own[low:high], lax.ppermute(other[low:high], "col", SKIP)))
-    mlp_total, mark = weight_grad(places, parts, all_m, low=1, held=mlp_total, hold=[mark, other])
+    mlp_total, mark = weight_grad(
+        places, parts, all_m, tile=1024, low=1, held=mlp_total, hold=[mark, other]
+    )
 
     incoming = jnp.concatenate(
         [own + after(arrived, mark).astype(jnp.float32) for own, arrived in incoming], axis=0
     ) * scale_omega
-    terms = row_sum(
+    terms = row_sum_direct(
         jnp.stack([jnp.sum(incoming, axis=1), jnp.sum(incoming * xhat, axis=1)])
     ) / MODEL_WIDTH
     latent_input_gradient = rstd * (

time: 107 us -> 105 us (0.981)
  waiting for transfers between devices: 19.6 us -> 18.5 us
    ppermute x2 -> x1, waiting for transfers between devices: 2.21 us -> 0.01 us  [row_sum(): pair += lax.ppermute(pair, 'row', CHIP)]
    ppermute x0 -> x3, starting transfers between devices: none -> 2.2 us  [the longest x1 1.39 us: row_sum_direct(): lax.ppermute(pair, 'row', CHIP)]
    ppermute x0 -> x3, waiting for transfers between devices: none -> 2.2 us  [the longest x1 1.44 us: row_sum_direct(): lax.ppermute(pair, 'row', CHIP)]
    ppermute x2 -> x1, starting transfers between devices: 4.44 us -> 3 us  [row_sum(): pair += lax.ppermute(pair, 'row', CHIP)]
    ppermute x2 -> x1, waiting for transfers between devices: 1.83 us -> 0.69 us  [row_sum(): return pair + lax.ppermute(pair, 'row', CORE)]
  transfers between devices with their start and end apart: 21 -> 22, of which waited for: 11 -> 11; matrix products, arithmetic and copies ran while one was open for 9% -> 9% of each run, Pallas kernels for 44% -> 45%
where the time goes in v5:
time: 105 us
  Pallas kernels  46.8 us (45%)
  starting transfers between devices  24.2 us (23%)
  waiting for transfers between devices  18.5 us (18%)
  other arithmetic  7.47 us (7%)
  local copies, waits for them, and re-layouts  5.98 us (6%)
    pallas_call x4, Pallas kernels, back(): pl.pallas_call(functools.partial(back_kernel, layout, tile, order is not...  26.5 us
    pallas_call x3, Pallas kernels, weight_grad(): pl.pallas_call(functools.partial(weight_kernel, len(grads), len(extra)),...  20.3 us
    ppermute x2, waiting for transfers between devices, on_grid(): far_m = [lax.ppermute(part, 'row', CHIP) for part in own_m]  9.37 us
    ppermute x3, starting transfers between devices, on_grid(): incoming.append((own[low:high], lax.ppermute(other[low:high], 'col', SKIP)))  5.32 us
    all_to_all x1, starting transfers between devices, on_grid(): lax.all_to_all(jnp.broadcast_to(normed[None], (4,) + normed.shape), 'col'...  4.87 us
    ppermute x2, starting transfers between devices, on_grid(): send = lax.ppermute(send, 'col', NEXT)  3.01 us
    ppermute x1, starting transfers between devices, row_sum(): pair += lax.ppermute(pair, 'row', CHIP)  3 us
    convert_element_type x2, other arithmetic, on_grid(): own_m = [(mlp_cotangent[start:start + size].astype(jnp.float32) * gelu_sl...  3 us
  transfers between devices with their start and end apart: 22, of which 11 were waited for; matrix products, arithmetic and copies ran while one was open for 9% of the time, Pallas kernels for 45%

profile of v5, /device:TPU:0, one launch (start us, length us, event | category | flops | bytes accessed | tf_op | source)
XLA Modules:
  0.0 104.8 jit_solution(4948131871300710269)
XLA Ops:
  0.7 1.3 %convert_reduce_fusion = (f32[256]{0:T(256)S(1)}, f32[256]{0:T(256)S(1)}) fusion(bf16[256,768]{1,0:T(8,128)(2,1)} %param.10), kind=kLoop, calls=%fused_computation.25 | loop fusion | flops 785920 | bytes 395264 | tf_op jit(solution)/shard_map/reduce_sum | solution.py:263
  2.0 3.0 %collective-permute-start = (f32[2,256]{1,0:T(2,128)S(1)}, f32[2,256]{1,0:T(2,128)S(1)}, u32[]{:S(2)}, u32[]{:S(2)}) collective-permute-start(f32[2,256]{1,0:T(2,128)S(1)} %pad_maximum_fusion), channel_id=1, source_target_pairs={{0,8},{8,0},{4,12},{12,4},{1,9},{9,1},{5,13},{13,5},{2,10},{10,2},... | collective-permute-start | bytes 6152 | tf_op jit(solution)/shard_map/ppermute | solution.py:229
  5.0 0.2 collective-permute-start.7
  5.1 0.8 copy.14
  5.9 0.8 dynamic_slice.3
  6.7 0.8 fusion.32
  7.7 0.4 collective-permute-start.1
  8.2 0.7 collective-permute-done.1
  9.0 1.0 fusion.25
  10.0 1.4 %fusion.7.refs_3_.refs_4_ = bf16[160,3072]{1,0:T(8,128)(2,1)S(1)} fusion(bf16[256,3072]{1,0:T(8,128)(2,1)S(1)} %copy-done.12, bf16[256,3072]{1,0:T(8,128)(2,1)S(1)} %copy-done.13), kind=kLoop, calls=%fused_computation.21 | loop fusion | flops 10321920 | bytes 2949120 | tf_op jit(solution)/shard_map/convert_element_type | solution.py:293
  11.4 0.4 collective-permute-start.3
  11.8 1.6 %fusion.16.refs_4_.refs_5_ = bf16[96,3072]{1,0:T(8,128)(2,1)} fusion(bf16[256,3072]{1,0:T(8,128)(2,1)S(1)} %copy-done.12, bf16[256,3072]{1,0:T(8,128)(2,1)S(1)} %copy-done.13), kind=kLoop, calls=%fused_computation.33 | loop fusion | flops 6193152 | bytes 1769472 | tf_op jit(solution)/shard_map/convert_element_type | solution.py:293
  13.4 0.2 collective-permute-start.4
  13.7 1.9 %collective-permute-start.6 = (bf16[160,3072]{1,0:T(8,128)(2,1)S(1)}, bf16[160,3072]{1,0:T(8,128)(2,1)S(1)}, u32[]{:S(2)}, u32[]{:S(2)}) collective-permute-start(bf16[160,3072]{1,0:T(8,128)(2,1)S(1)} %fusion.7.refs_3_.refs_4_), channel_id=1, source_target_pairs={{0,8},{8,0},{4,12},{12,4},{1,9},{9,1},{5,13},{13,5},{2,10},{10,2},... | collective-permute-start | bytes 2949128 | tf_op jit(solution)/shard_map/ppermute | solution.py:297
  15.5 1.2 %broadcast_in_dim.2 = bf16[4,256,768]{2,1,0:T(8,128)(2,1)} broadcast(bf16[256,768]{1,0:T(8,128)(2,1)S(1)} %copy-done.14), dimensions={1,2} | broadcast | bytes 1966080 | tf_op jit(solution)/shard_map/broadcast_in_dim | solution.py:284
  16.8 4.9 %all-to-all-start = ((bf16[4,256,768]{2,1,0:T(8,128)(2,1)}), bf16[4,256,768]{2,1,0:T(8,128)(2,1)}, u32[]{:S(2)}, u32[]{:S(2)}) async-start(bf16[4,256,768]{2,1,0:T(8,128)(2,1)} %broadcast_in_dim.2), calls=%async_computation | async-start | bytes 3145728 | tf_op jit(solution)/shard_map/all_to_all | solution.py:283
  21.7 0.9 copy-done.7
  22.6 10.3 %shard_map.121 = (bf16[256,768]{1,0:T(8,128)(2,1)S(1)}, bf16[256,768]{1,0:T(8,128)(2,1)}, f32[8,128]{1,0:T(8,128)}) custom-call(s32[2]{0:T(128)S(1)} %pad_add_fusion.refs_0_, bf16[256,2304]{1,0:T(8,128)(2,1)} %refs_4_.1, bf16[256,2304]{1,0:T(8,128)(2,1)} %collective-permute-done.2.refs_2_.refs_5_, bf16[160,3072]{1,0:T(8,128)(2,1)} %copy-done.4, ...), custom_call_target="tpu_custom_call" | custom-call | flops 1 | bytes 1 | tf_op jit(solution)/shard_map/pallas_call | solution.py:155
  32.9 1.1 %collective-permute-done.7.refs_0_.refs_6_ = bf16[256,2304]{1,0:T(8,128)(2,1)} collective-permute-done((bf16[256,2304]{1,0:T(8,128)(2,1)}, bf16[256,2304]{1,0:T(8,128)(2,1)}, u32[]{:S(2)}, u32[]{:S(2)}) %collective-permute-start.7) | collective-permute-done | bytes 1179680 | tf_op jit(solution)/shard_map/ppermute | solution.py:264
  34.0 1.3 %fusion.54 = (bf16[128,2304]{1,0:T(8,128)(2,1)S(1)}, bf16[128,2304]{1,0:T(8,128)(2,1)S(1)}) fusion(bf16[256,2304]{1,0:T(8,128)(2,1)} %collective-permute-done.7.refs_0_.refs_6_), kind=kLoop, calls=%fused_computation.94 | loop fusion | bytes 2359296 | tf_op jit(solution)/shard_map/slice | solution.py:314
  35.4 0.5 collective-permute-start.8
  35.9 1.5 %collective-permute-done.9.refs_2_.refs_8_ = bf16[128,2304]{1,0:T(8,128)(2,1)S(1)} collective-permute-done((bf16[128,2304]{1,0:T(8,128)(2,1)S(1)}, bf16[128,2304]{1,0:T(8,128)(2,1)S(1)}, u32[]{:S(2)}, u32[]{:S(2)}) %collective-permute-start.9) | collective-permute-done | bytes 589856 | tf_op jit(solution)/shard_map/ppermute | solution.py:314
  37.4 0.8 collective-permute-done.8.refs_1_.refs_7_
  38.3 0.8 copy-done.11
  39.1 6.1 %shard_map.122 = (f32[512,768]{1,0:T(8,128)}, f32[8,128]{1,0:T(8,128)S(1)}) custom-call(bf16[256,2304]{1,0:T(8,128)(2,1)} %collective-permute-done.7.refs_0_.refs_6_, bf16[128,2304]{1,0:T(8,128)(2,1)} %copy-done.11, bf16[128,2304]{1,0:T(8,128)(2,1)} %copy-done.10, bf16[768,2304]{1,0:T(8,128)(2,1)} %refs_3_.3), custom_call_target="tpu_custom_call" | custom-call | flops 1 | bytes 1 | tf_op jit(solution)/shard_map/pallas_call | solution.py:155
  45.3 9.4 %collective-permute-done.6.refs_1_.refs_8_ = bf16[160,3072]{1,0:T(8,128)(2,1)S(1)} collective-permute-done((bf16[160,3072]{1,0:T(8,128)(2,1)S(1)}, bf16[160,3072]{1,0:T(8,128)(2,1)S(1)}, u32[]{:S(2)}, u32[]{:S(2)}) %collective-permute-start.6) | collective-permute-done | bytes 983072 | tf_op jit(solution)/shard_map/ppermute | solution.py:297
  54.6 0.3 collective-permute-start.13
  54.9 1.8 %collective-permute-start.5 = (bf16[256,768]{1,0:T(8,128)(2,1)}, bf16[256,768]{1,0:T(8,128)(2,1)S(1)}, u32[]{:S(2)}, u32[]{:S(2)}) collective-permute-start(bf16[256,768]{1,0:T(8,128)(2,1)} %get-tuple-element.31), channel_id=1, source_target_pairs={{0,1},{1,0},{2,3},{3,2},{4,5},{5,4},{6,7},{7,6},{8,9},{9,8},{10,11... | collective-permute-start | bytes 1179656 | tf_op jit(solution)/shard_map/ppermute | solution.py:310
  56.7 0.5 collective-permute-done.10.refs_2_.refs_10_
  57.2 5.2 %shard_map.123 = (bf16[160,768]{1,0:T(8,128)(2,1)S(1)}, bf16[160,768]{1,0:T(8,128)(2,1)S(1)}, f32[8,128]{1,0:T(8,128)S(1)}) custom-call(s32[2]{0:T(128)S(1)} %pad_add_fusion.refs_0_, bf16[160,3072]{1,0:T(8,128)(2,1)S(1)} %collective-permute-done.6.refs_1_.refs_8_, bf16[160,3072]{1,0:T(8,128)(2,1)S(1)} %collective-permute-done.10.refs_2_.refs_10_, ...), custom_call_target="tpu_custom_call" | custom-call | flops 1 | bytes 1 | tf_op jit(solution)/shard_map/pallas_call | solution.py:155
  62.4 1.6 %collective-permute-start.11 = (bf16[160,768]{1,0:T(8,128)(2,1)S(1)}, bf16[160,768]{1,0:T(8,128)(2,1)S(1)}, u32[]{:S(2)}, u32[]{:S(2)}) collective-permute-start(bf16[160,768]{1,0:T(8,128)(2,1)S(1)} %get-tuple-element.38), channel_id=1, source_target_pairs={{0,1},{1,0},{2,3},{3,2},{4,5},{5,4},{6,7},{7,6},{8,9},{9,8},{10,11... | collective-permute-start | bytes 737288 | tf_op jit(solution)/shard_map/ppermute | solution.py:348
  64.1 7.9 %shard_map.124 = (bf16[768,2304]{1,0:T(8,128)(2,1)}, f32[8,128]{1,0:T(8,128)S(1)}) custom-call(s32[4]{0:T(128)S(1)} %pad_add_fusion.1.places, bf16[1024,768]{1,0:T(8,128)(2,1)} %bitcast.12.refs_0_.refs_1_.refs_2_.refs_3_, bf16[1024,768]{1,0:T(8,128)(2,1)} %bitcast.12.refs_0_.refs_1_.refs_2_.refs_3_, ...), custom_call_target="tpu_custom_call" | custom-call | flops 1 | bytes 1 | tf_op jit(solution)/shard_map/pallas_call | solution.py:205
  72.1 0.4 collective-permute-done.11
  72.6 2.3 %collective-permute-start.12 = (bf16[112,768]{1,0:T(8,128)(2,1)S(1)}, bf16[112,768]{1,0:T(8,128)(2,1)S(1)}, u32[]{:S(2)}, u32[]{:S(2)}) collective-permute-start(bf16[112,768]{1,0:T(8,128)(2,1)S(1)} %slice.86), channel_id=1, source_target_pairs={{0,2},{2,0},{1,3},{3,1},{4,6},{6,4},{5,7},{7,5},{8,10},{10,8},{9,1... | collective-permute-start | bytes 516104 | tf_op jit(solution)/shard_map/ppermute | solution.py:366
  75.0 4.8 %shard_map.125 = (bf16[96,768]{1,0:T(8,128)(2,1)S(1)}, bf16[96,768]{1,0:T(8,128)(2,1)S(1)}, f32[8,128]{1,0:T(8,128)S(1)}) custom-call(s32[2]{0:T(128)S(1)} %pad_add_fusion.refs_0_, bf16[96,3072]{1,0:T(8,128)(2,1)S(1)} %collective-permute-done.13.refs_1_.refs_9_, bf16[96,3072]{1,0:T(8,128)(2,1)S(1)} %collective-permute-done.14.refs_2_.refs_11_, ...), custom_call_target="tpu_custom_call" | custom-call | flops 1 | bytes 1 | tf_op jit(solution)/shard_map/pallas_call | solution.py:155
  79.9 1.4 %collective-permute-start.15 = (bf16[96,768]{1,0:T(8,128)(2,1)S(1)}, bf16[96,768]{1,0:T(8,128)(2,1)S(1)}, u32[]{:S(2)}, u32[]{:S(2)}) collective-permute-start(bf16[96,768]{1,0:T(8,128)(2,1)S(1)} %get-tuple-element.45), channel_id=1, source_target_pairs={{0,1},{1,0},{2,3},{3,2},{4,5},{5,4},{6,7},{7,6},{8,9},{9,8},{10,11... | collective-permute-start | bytes 442376 | tf_op jit(solution)/shard_map/ppermute | solution.py:348
  81.2 1.8 %collective-permute-start.16 = (bf16[48,768]{1,0:T(8,128)(2,1)S(1)}, bf16[48,768]{1,0:T(8,128)(2,1)S(1)}, u32[]{:S(2)}, u32[]{:S(2)}) collective-permute-start(bf16[48,768]{1,0:T(8,128)(2,1)S(1)} %slice.87), channel_id=1, source_target_pairs={{0,2},{2,0},{1,3},{3,1},{4,6},{6,4},{5,7},{7,5},{8,10},{10,8},{9,1... | collective-permute-start | bytes 221192 | tf_op jit(solution)/shard_map/ppermute | solution.py:366
  83.0 5.1 %shard_map.126 = (bf16[768,3072]{1,0:T(8,128)(2,1)}, f32[8,128]{1,0:T(8,128)S(1)}) custom-call(s32[4]{0:T(128)S(1)} %pad_add_fusion.1.places, bf16[1024,768]{1,0:T(8,128)(2,1)} %bitcast.12.refs_0_.refs_1_.refs_2_.refs_3_, bf16[1024,768]{1,0:T(8,128)(2,1)} %bitcast.12.refs_0_.refs_1_.refs_2_.refs_3_, ...), custom_call_target="tpu_custom_call" | custom-call | flops 1 | bytes 1 | tf_op jit(solution)/shard_map/pallas_call | solution.py:205
  88.1 0.7 collective-permute-done.15
  88.9 1.2 %collective-permute-start.17 = (bf16[96,768]{1,0:T(8,128)(2,1)S(1)}, bf16[96,768]{1,0:T(8,128)(2,1)S(1)}, u32[]{:S(2)}, u32[]{:S(2)}) collective-permute-start(bf16[96,768]{1,0:T(8,128)(2,1)S(1)} %select_convert_fusion.1.refs_13_), channel_id=1, source_target_pairs={{0,2},{2,0},{1,3},{3,1},{4,6},{6,4},{5,7},{7,5},{8,10},{10,8},{9,1... | collective-permute-start | bytes 442376 | tf_op jit(solution)/shard_map/ppermute | solution.py:366
  90.1 7.3 %shard_map.127 = (bf16[768,3072]{1,0:T(8,128)(2,1)}, f32[8,128]{1,0:T(8,128)}) custom-call(s32[4]{0:T(128)S(1)} %pad_add_fusion.1.places, bf16[1024,768]{1,0:T(8,128)(2,1)} %bitcast.12.refs_0_.refs_1_.refs_2_.refs_3_, bf16[1024,768]{1,0:T(8,128)(2,1)} %bitcast.12.refs_0_.refs_1_.refs_2_.refs_3_, ...), custom_call_target="tpu_custom_call", output_to_operand_aliasing={{0}: (15, {})} | custom-call | flops 1 | bytes 1 | tf_op jit(solution)/shard_map/pallas_call | solution.py:205
  97.5 1.3 %collective-permute-done.17 = bf16[96,768]{1,0:T(8,128)(2,1)S(1)} collective-permute-done((bf16[96,768]{1,0:T(8,128)(2,1)S(1)}, bf16[96,768]{1,0:T(8,128)(2,1)S(1)}, u32[]{:S(2)}, u32[]{:S(2)}) %collective-permute-start.17) | collective-permute-done | bytes 147488 | tf_op jit(solution)/shard_map/ppermute | solution.py:366
  98.9 0.5 fusion.53
  99.4 1.4 %collective-permute-start.19 = (f32[2,256]{1,0:T(2,128)S(1)}, f32[2,256]{1,0:T(2,128)S(1)}, u32[]{:S(2)}, u32[]{:S(2)}) collective-permute-start(f32[2,256]{1,0:T(2,128)S(1)} %pad_maximum_fusion.1), channel_id=1, source_target_pairs={{0,8},{8,0},{4,12},{12,4},{1,9},{9,1},{5,13},{13,5},{2,10},{10,2},... | collective-permute-start | bytes 6152 | tf_op jit(solution)/shard_map/ppermute | solution.py:237
  100.8 0.8 collective-permute-start.18
  101.6 1.4 %collective-permute-done.19 = f32[2,256]{1,0:T(2,128)S(1)} collective-permute-done((f32[2,256]{1,0:T(2,128)S(1)}, f32[2,256]{1,0:T(2,128)S(1)}, u32[]{:S(2)}, u32[]{:S(2)}) %collective-permute-start.19) | collective-permute-done | bytes 2080 | tf_op jit(solution)/shard_map/ppermute | solution.py:237
  103.0 0.8 collective-permute-done.20
  103.8 1.0 fusion.29
  (69 shorter events, 1.1 us)
Async XLA Ops:
  0.6 8.3 %copy-start.8 = (bf16[256,768]{1,0:T(8,128)(2,1)S(1)}, bf16[256,768]{1,0:T(8,128)(2,1)}, u32[]{:S(2)}) copy-start(bf16[256,768]{1,0:T(8,128)(2,1)} %param.10) | copy-start | bytes 1179652
  0.6 6.9 %copy-start.15 = (s32[1024]{0:T(1024)S(1)}, s32[1024]{0:T(1024)}, u32[]{:S(2)}) copy-start(s32[1024]{0:T(1024)} %param.12) | copy-start | bytes 12292
  0.7 7.5 %copy-start.16 = (f32[8]{0:T(128)S(1)}, f32[8]{0:T(128)}, u32[]{:S(2)}) copy-start(f32[8]{0:T(128)} %param.14) | copy-start | bytes 100
  0.7 7.4 %copy-start.17 = (s32[8]{0:T(128)S(1)}, s32[8]{0:T(128)}, u32[]{:S(2)}) copy-start(s32[8]{0:T(128)} %param.13) | copy-start | bytes 100
  2.0 5.7 %collective-permute-start = (f32[2,256]{1,0:T(2,128)S(1)}, f32[2,256]{1,0:T(2,128)S(1)}, u32[]{:S(2)}, u32[]{:S(2)}) collective-permute-start(f32[2,256]{1,0:T(2,128)S(1)} %pad_maximum_fusion), channel_id=1, source_target_pairs={{0,8},{8,0},{4,12},{12,4},{1,9},{9,1},{5,13},{13,5},{2,10},{10,2},... | collective-permute-start | bytes 6152 | tf_op jit(solution)/shard_map/ppermute | solution.py:229
  5.0 17.7 %collective-permute-start.2 = (bf16[256,2304]{1,0:T(8,128)(2,1)}, bf16[256,2304]{1,0:T(8,128)(2,1)}, u32[]{:S(2)}, u32[]{:S(2)}) collective-permute-start(bf16[256,2304]{1,0:T(8,128)(2,1)} %refs_4_.1), channel_id=1, source_target_pairs={{0,4},{4,0},{8,12},{12,8},{1,5},{5,1},{9,13},{13,9},{2,6},{6,2},{1... | collective-permute-start | bytes 3538952 | tf_op jit(solution)/shard_map/ppermute | solution.py:266
  5.0 29.1 %collective-permute-start.7 = (bf16[256,2304]{1,0:T(8,128)(2,1)}, bf16[256,2304]{1,0:T(8,128)(2,1)}, u32[]{:S(2)}, u32[]{:S(2)}) collective-permute-start(bf16[256,2304]{1,0:T(8,128)(2,1)} %refs_4_.1), channel_id=1, source_target_pairs={{0,8},{8,0},{4,12},{12,4},{1,9},{9,1},{5,13},{13,5},{2,10},{10,2},... | collective-permute-start | bytes 3538952 | tf_op jit(solution)/shard_map/ppermute | solution.py:264
  6.7 3.3 %copy-start.13 = (bf16[256,3072]{1,0:T(8,128)(2,1)S(1)}, bf16[256,3072]{1,0:T(8,128)(2,1)}, u32[]{:S(2)}) copy-start(bf16[256,3072]{1,0:T(8,128)(2,1)} %param.16) | copy-start | bytes 4718596
  7.5 1.4 %copy-start.5 = (f32[256,1536]{1,0:T(8,128)}, f32[256,1536]{1,0:T(8,128)S(1)}, u32[]{:S(2)}) copy-start(f32[256,1536]{1,0:T(8,128)S(1)} %fusion.32) | copy-start | bytes 4718596
  7.5 2.5 %copy-start.12 = (bf16[256,3072]{1,0:T(8,128)(2,1)S(1)}, bf16[256,3072]{1,0:T(8,128)(2,1)}, u32[]{:S(2)}) copy-start(bf16[256,3072]{1,0:T(8,128)(2,1)} %param.17) | copy-start | bytes 4718596
  7.7 1.2 %collective-permute-start.1 = (f32[2,256]{1,0:T(2,128)S(1)}, f32[2,256]{1,0:T(2,128)S(1)}, u32[]{:S(2)}, u32[]{:S(2)}) collective-permute-start(f32[2,256]{1,0:T(2,128)S(1)} %fusion.52), channel_id=1, source_target_pairs={{0,4},{4,0},{8,12},{12,8},{1,5},{5,1},{9,13},{13,9},{2,6},{6,2},{1... | collective-permute-start | bytes 6152 | tf_op jit(solution)/shard_map/ppermute | solution.py:230
  11.4 5.4 %copy-start.4 = (bf16[160,3072]{1,0:T(8,128)(2,1)}, bf16[160,3072]{1,0:T(8,128)(2,1)S(1)}, u32[]{:S(2)}) copy-start(bf16[160,3072]{1,0:T(8,128)(2,1)S(1)} %fusion.7.refs_3_.refs_4_) | copy-start | bytes 2949124
  11.4 4.2 %copy-start.14 = (bf16[256,768]{1,0:T(8,128)(2,1)S(1)}, bf16[256,768]{1,0:T(8,128)(2,1)}, u32[]{:S(2)}) copy-start(bf16[256,768]{1,0:T(8,128)(2,1)} %fusion.25) | copy-start | bytes 1179652
  11.4 10.3 %collective-permute-start.3 = (bf16[160,3072]{1,0:T(8,128)(2,1)S(1)}, bf16[160,3072]{1,0:T(8,128)(2,1)S(1)}, u32[]{:S(2)}, u32[]{:S(2)}) collective-permute-start(bf16[160,3072]{1,0:T(8,128)(2,1)S(1)} %fusion.7.refs_3_.refs_4_), channel_id=1, source_target_pairs={{0,4},{4,0},{8,12},{12,8},{1,5},{5,1},{9,13},{13,9},{2,6},{6,2},{1... | collective-permute-start | bytes 2949128 | tf_op jit(solution)/shard_map/ppermute | solution.py:296
  13.4 8.2 %collective-permute-start.4 = (bf16[96,3072]{1,0:T(8,128)(2,1)}, bf16[96,3072]{1,0:T(8,128)(2,1)}, u32[]{:S(2)}, u32[]{:S(2)}) collective-permute-start(bf16[96,3072]{1,0:T(8,128)(2,1)} %fusion.16.refs_4_.refs_5_), channel_id=1, source_target_pairs={{0,4},{4,0},{8,12},{12,8},{1,5},{5,1},{9,13},{13,9},{2,6},{6,2},{1... | collective-permute-start | bytes 1769480 | tf_op jit(solution)/shard_map/ppermute | solution.py:296
  13.7 40.9 %collective-permute-start.6 = (bf16[160,3072]{1,0:T(8,128)(2,1)S(1)}, bf16[160,3072]{1,0:T(8,128)(2,1)S(1)}, u32[]{:S(2)}, u32[]{:S(2)}) collective-permute-start(bf16[160,3072]{1,0:T(8,128)(2,1)S(1)} %fusion.7.refs_3_.refs_4_), channel_id=1, source_target_pairs={{0,8},{8,0},{4,12},{12,4},{1,9},{9,1},{5,13},{13,5},{2,10},{10,2},... | collective-permute-start | bytes 2949128 | tf_op jit(solution)/shard_map/ppermute | solution.py:297
  16.8 47.3 %all-to-all-start = ((bf16[4,256,768]{2,1,0:T(8,128)(2,1)}), bf16[4,256,768]{2,1,0:T(8,128)(2,1)}, u32[]{:S(2)}, u32[]{:S(2)}) async-start(bf16[4,256,768]{2,1,0:T(8,128)(2,1)} %broadcast_in_dim.2), calls=%async_computation | async-start | bytes 3145728 | tf_op jit(solution)/shard_map/all_to_all | solution.py:283
  21.7 0.9 copy-start.7
  35.4 2.1 %collective-permute-start.9 = (bf16[128,2304]{1,0:T(8,128)(2,1)S(1)}, bf16[128,2304]{1,0:T(8,128)(2,1)S(1)}, u32[]{:S(2)}, u32[]{:S(2)}) collective-permute-start(bf16[128,2304]{1,0:T(8,128)(2,1)S(1)} %get-tuple-element.62), channel_id=1, source_target_pairs={{0,4},{4,0},{8,12},{12,8},{1,5},{5,1},{9,13},{13,9},{2,6},{6,2},{1... | collective-permute-start | bytes 1769480 | tf_op jit(solution)/shard_map/ppermute | solution.py:314
  35.4 2.8 %collective-permute-start.8 = (bf16[128,2304]{1,0:T(8,128)(2,1)S(1)}, bf16[128,2304]{1,0:T(8,128)(2,1)S(1)}, u32[]{:S(2)}, u32[]{:S(2)}) collective-permute-start(bf16[128,2304]{1,0:T(8,128)(2,1)S(1)} %get-tuple-element.63), channel_id=1, source_target_pairs={{0,4},{4,0},{8,12},{12,8},{1,5},{5,1},{9,13},{13,9},{2,6},{6,2},{1... | collective-permute-start | bytes 1769480 | tf_op jit(solution)/shard_map/ppermute | solution.py:314
  37.4 0.8 copy-start.10
  38.3 0.8 copy-start.11
  54.6 7.8 %copy-start = (bf16[160,3072]{1,0:T(8,128)(2,1)}, bf16[160,3072]{1,0:T(8,128)(2,1)S(1)}, u32[]{:S(2)}) copy-start(bf16[160,3072]{1,0:T(8,128)(2,1)S(1)} %collective-permute-done.6.refs_1_.refs_8_) | copy-start | bytes 2949124
  54.6 2.6 %collective-permute-start.10 = (bf16[160,3072]{1,0:T(8,128)(2,1)S(1)}, bf16[160,3072]{1,0:T(8,128)(2,1)S(1)}, u32[]{:S(2)}, u32[]{:S(2)}) collective-permute-start(bf16[160,3072]{1,0:T(8,128)(2,1)S(1)} %collective-permute-done.6.refs_1_.refs_8_), channel_id=1, source_target_pairs={{0,4},{4,0},{8,12},{12,8},{1,5},{5,1},{9,13},{13,9},{2,6},{6,2},{1... | collective-permute-start | bytes 2949128 | tf_op jit(solution)/shard_map/ppermute | solution.py:332
  54.6 17.4 %collective-permute-start.13 = (bf16[96,3072]{1,0:T(8,128)(2,1)}, bf16[96,3072]{1,0:T(8,128)(2,1)S(1)}, u32[]{:S(2)}, u32[]{:S(2)}) collective-permute-start(bf16[96,3072]{1,0:T(8,128)(2,1)} %fusion.16.refs_4_.refs_5_), channel_id=1, source_target_pairs={{0,8},{8,0},{4,12},{12,4},{1,9},{9,1},{5,13},{13,5},{2,10},{10,2},... | collective-permute-start | bytes 1769480 | tf_op jit(solution)/shard_map/ppermute | solution.py:297
  54.9 17.1 %collective-permute-start.5 = (bf16[256,768]{1,0:T(8,128)(2,1)}, bf16[256,768]{1,0:T(8,128)(2,1)S(1)}, u32[]{:S(2)}, u32[]{:S(2)}) collective-permute-start(bf16[256,768]{1,0:T(8,128)(2,1)} %get-tuple-element.31), channel_id=1, source_target_pairs={{0,1},{1,0},{2,3},{3,2},{4,5},{5,4},{6,7},{7,6},{8,9},{9,8},{10,11... | collective-permute-start | bytes 1179656 | tf_op jit(solution)/shard_map/ppermute | solution.py:310
  57.2 5.2 %copy-start.1 = (bf16[160,3072]{1,0:T(8,128)(2,1)}, bf16[160,3072]{1,0:T(8,128)(2,1)S(1)}, u32[]{:S(2)}) copy-start(bf16[160,3072]{1,0:T(8,128)(2,1)S(1)} %collective-permute-done.10.refs_2_.refs_10_) | copy-start | bytes 2949124
  62.4 10.0 %collective-permute-start.11 = (bf16[160,768]{1,0:T(8,128)(2,1)S(1)}, bf16[160,768]{1,0:T(8,128)(2,1)S(1)}, u32[]{:S(2)}, u32[]{:S(2)}) collective-permute-start(bf16[160,768]{1,0:T(8,128)(2,1)S(1)} %get-tuple-element.38), channel_id=1, source_target_pairs={{0,1},{1,0},{2,3},{3,2},{4,5},{5,4},{6,7},{7,6},{8,9},{9,8},{10,11... | collective-permute-start | bytes 737288 | tf_op jit(solution)/shard_map/ppermute | solution.py:348
  72.0 7.8 %copy-start.2 = (bf16[96,3072]{1,0:T(8,128)(2,1)}, bf16[96,3072]{1,0:T(8,128)(2,1)S(1)}, u32[]{:S(2)}) copy-start(bf16[96,3072]{1,0:T(8,128)(2,1)S(1)} %collective-permute-done.13.refs_1_.refs_9_) | copy-start | bytes 1769476
  72.4 2.6 %collective-permute-start.14 = (bf16[96,3072]{1,0:T(8,128)(2,1)S(1)}, bf16[96,3072]{1,0:T(8,128)(2,1)S(1)}, u32[]{:S(2)}, u32[]{:S(2)}) collective-permute-start(bf16[96,3072]{1,0:T(8,128)(2,1)S(1)} %collective-permute-done.13.refs_1_.refs_9_), channel_id=1, source_target_pairs={{0,4},{4,0},{8,12},{12,8},{1,5},{5,1},{9,13},{13,9},{2,6},{6,2},{1... | collective-permute-start | bytes 1769480 | tf_op jit(solution)/shard_map/ppermute | solution.py:332
  72.6 15.5 %collective-permute-start.12 = (bf16[112,768]{1,0:T(8,128)(2,1)S(1)}, bf16[112,768]{1,0:T(8,128)(2,1)S(1)}, u32[]{:S(2)}, u32[]{:S(2)}) collective-permute-start(bf16[112,768]{1,0:T(8,128)(2,1)S(1)} %slice.86), channel_id=1, source_target_pairs={{0,2},{2,0},{1,3},{3,1},{4,6},{6,4},{5,7},{7,5},{8,10},{10,8},{9,1... | collective-permute-start | bytes 516104 | tf_op jit(solution)/shard_map/ppermute | solution.py:366
  75.0 4.9 %copy-start.3 = (bf16[96,3072]{1,0:T(8,128)(2,1)}, bf16[96,3072]{1,0:T(8,128)(2,1)S(1)}, u32[]{:S(2)}) copy-start(bf16[96,3072]{1,0:T(8,128)(2,1)S(1)} %collective-permute-done.14.refs_2_.refs_11_) | copy-start | bytes 1769476
  79.9 8.9 %collective-permute-start.15 = (bf16[96,768]{1,0:T(8,128)(2,1)S(1)}, bf16[96,768]{1,0:T(8,128)(2,1)S(1)}, u32[]{:S(2)}, u32[]{:S(2)}) collective-permute-start(bf16[96,768]{1,0:T(8,128)(2,1)S(1)} %get-tuple-element.45), channel_id=1, source_target_pairs={{0,1},{1,0},{2,3},{3,2},{4,5},{5,4},{6,7},{7,6},{8,9},{9,8},{10,11... | collective-permute-start | bytes 442376 | tf_op jit(solution)/shard_map/ppermute | solution.py:348
  81.2 6.9 %collective-permute-start.16 = (bf16[48,768]{1,0:T(8,128)(2,1)S(1)}, bf16[48,768]{1,0:T(8,128)(2,1)S(1)}, u32[]{:S(2)}, u32[]{:S(2)}) collective-permute-start(bf16[48,768]{1,0:T(8,128)(2,1)S(1)} %slice.87), channel_id=1, source_target_pairs={{0,2},{2,0},{1,3},{3,1},{4,6},{6,4},{5,7},{7,5},{8,10},{10,8},{9,1... | collective-permute-start | bytes 221192 | tf_op jit(solution)/shard_map/ppermute | solution.py:366
  88.9 9.9 %collective-permute-start.17 = (bf16[96,768]{1,0:T(8,128)(2,1)S(1)}, bf16[96,768]{1,0:T(8,128)(2,1)S(1)}, u32[]{:S(2)}, u32[]{:S(2)}) collective-permute-start(bf16[96,768]{1,0:T(8,128)(2,1)S(1)} %select_convert_fusion.1.refs_13_), channel_id=1, source_target_pairs={{0,2},{2,0},{1,3},{3,1},{4,6},{6,4},{5,7},{7,5},{8,10},{10,8},{9,1... | collective-permute-start | bytes 442376 | tf_op jit(solution)/shard_map/ppermute | solution.py:366
  97.4 1.5 %copy-start.6 = (f32[256,1536]{1,0:T(8,128)S(1)}, f32[256,1536]{1,0:T(8,128)}, u32[]{:S(2)}) copy-start(f32[256,1536]{1,0:T(8,128)} %copy-done.5) | copy-start | bytes 4718596
  97.4 1.5 %copy-start.9 = (bf16[256,768]{1,0:T(8,128)(2,1)S(1)}, bf16[256,768]{1,0:T(8,128)(2,1)}, u32[]{:S(2)}) copy-start(bf16[256,768]{1,0:T(8,128)(2,1)} %param.10) | copy-start | bytes 1179652
  99.4 3.6 %collective-permute-start.19 = (f32[2,256]{1,0:T(2,128)S(1)}, f32[2,256]{1,0:T(2,128)S(1)}, u32[]{:S(2)}, u32[]{:S(2)}) collective-permute-start(f32[2,256]{1,0:T(2,128)S(1)} %pad_maximum_fusion.1), channel_id=1, source_target_pairs={{0,8},{8,0},{4,12},{12,4},{1,9},{9,1},{5,13},{13,5},{2,10},{10,2},... | collective-permute-start | bytes 6152 | tf_op jit(solution)/shard_map/ppermute | solution.py:237
  100.8 3.0 %collective-permute-start.20 = (f32[2,256]{1,0:T(2,128)S(1)}, f32[2,256]{1,0:T(2,128)S(1)}, u32[]{:S(2)}, u32[]{:S(2)}) collective-permute-start(f32[2,256]{1,0:T(2,128)S(1)} %pad_maximum_fusion.1), channel_id=1, source_target_pairs={{0,12},{12,0},{4,8},{8,4},{1,13},{13,1},{5,9},{9,5},{2,14},{14,2},... | collective-permute-start | bytes 6152 | tf_op jit(solution)/shard_map/ppermute | solution.py:238
  100.8 3.0 %collective-permute-start.18 = (f32[2,256]{1,0:T(2,128)S(1)}, f32[2,256]{1,0:T(2,128)S(1)}, u32[]{:S(2)}, u32[]{:S(2)}) collective-permute-start(f32[2,256]{1,0:T(2,128)S(1)} %pad_maximum_fusion.1), channel_id=1, source_target_pairs={{0,4},{4,0},{8,12},{12,8},{1,5},{5,1},{9,13},{13,9},{2,6},{6,2},{1... | collective-permute-start | bytes 6152 | tf_op jit(solution)/shard_map/ppermute | solution.py:236

commit v6 on v5

--- a/solution.py
+++ b/solution.py
@@ -24,10 +24,10 @@
 CHIP = [(0, 2), (2, 0), (1, 3), (3, 1)]
 BOTH = [(0, 3), (3, 0), (1, 2), (2, 1)]
 NEXT, SKIP = CORE, CHIP
-PIECES = (160, 96)
+PIECES = (144, 112)
 STARTS = tuple(sum(PIECES[:k]) for k in range(len(PIECES)))
 TURNS = ((0,), (1,))
-SWAPS = (((0, 112), (112, 160)), ((0, 96),))
+SWAPS = (((0, 112), (112, 144)), ((0, 112),))
 PART = 128
 
 
@@ -344,10 +344,11 @@
             seeds=((start, size), (tok_row + start, size)),
             hold=[mark],
             pin=False,
+            tile=1536,
         )
         send = lax.ppermute(send, "col", NEXT)
         if index == 0:
-            qkv_total, mark = weight_grad(places, parts, q_parts, hold=[mark])
+            qkv_total, mark = weight_grad(places, parts, q_parts, tile=1152, hold=[mark])
             ready = [mark, send, near_next]
         halves.append((start, size, keep, send))
 

time: 105 us -> 105 us (level)
  waiting for transfers between devices: 18.5 us -> 19.7 us
    ppermute x2, waiting for transfers between devices: 9.37 us -> 7.52 us  [on_grid(): far_m = [lax.ppermute(part, 'row', CHIP) for part in own_m]]
    ppermute x3, waiting for transfers between devices: 1.31 us -> 2.78 us  [on_grid(): incoming.append((own[low:high], lax.ppermute(other[low:high], 'col', SKIP)))]
    ppermute x2, waiting for transfers between devices: 1.01 us -> 2.19 us  [on_grid(): send = lax.ppermute(send, 'col', NEXT)]
    ppermute x1, waiting for transfers between devices: 1.11 us -> 2.22 us  [on_grid(): far_q = lax.ppermute(after(qkv_cotangent, moments), 'row', CHIP)]
    unnamed x37 -> x35, local copies, waits for them, and re-layouts: 2.63 us -> 2.98 us
  transfers between devices with their start and end apart: 22 -> 22, of which waited for: 11 -> 12; matrix products, arithmetic and copies ran while one was open for 9% -> 8% of each run, Pallas kernels for 45% -> 44%
where the time goes in v6:
time: 105 us; the launch traced here: 104 us
  Pallas kernels  46.3 us (44%)
  starting transfers between devices  23.3 us (22%)
  waiting for transfers between devices  19.7 us (19%)
  other arithmetic  6.8 us (6%)
  local copies, waits for them, and re-layouts  6.32 us (6%)
    pallas_call x4, Pallas kernels, back(): pl.pallas_call(functools.partial(back_kernel, layout, tile, order is not...  25.6 us
    pallas_call x3, Pallas kernels, weight_grad(): pl.pallas_call(functools.partial(weight_kernel, len(grads), len(extra)),...  20.7 us
    ppermute x2, waiting for transfers between devices, on_grid(): far_m = [lax.ppermute(part, 'row', CHIP) for part in own_m]  7.52 us
    all_to_all x1, starting transfers between devices, on_grid(): lax.all_to_all(jnp.broadcast_to(normed[None], (4,) + normed.shape), 'col'...  4.87 us
    ppermute x3, starting transfers between devices, on_grid(): incoming.append((own[low:high], lax.ppermute(other[low:high], 'col', SKIP)))  4.34 us
    ppermute x2, starting transfers between devices, on_grid(): send = lax.ppermute(send, 'col', NEXT)  3.08 us
    convert_element_type x2, other arithmetic, on_grid(): own_m = [(mlp_cotangent[start:start + size].astype(jnp.float32) * gelu_sl...  3.04 us
    ppermute x1, starting transfers between devices, row_sum(): pair += lax.ppermute(pair, 'row', CHIP)  3 us
  transfers between devices with their start and end apart: 22, of which 12 were waited for; matrix products, arithmetic and copies ran while one was open for 8% of the time, Pallas kernels for 44%

profile of v6, /device:TPU:0, one launch (start us, length us, event | category | flops | bytes accessed | tf_op | source)
XLA Modules:
  0.0 104.3 jit_solution(4180221955615535664)
XLA Ops:
  0.7 1.3 %convert_reduce_fusion = (f32[256]{0:T(256)S(1)}, f32[256]{0:T(256)S(1)}) fusion(bf16[256,768]{1,0:T(8,128)(2,1)} %param.10), kind=kLoop, calls=%fused_computation.34 | loop fusion | flops 785920 | bytes 395264 | tf_op jit(solution)/shard_map/reduce_sum | solution.py:263
  2.0 3.0 %collective-permute-start = (f32[2,256]{1,0:T(2,128)S(1)}, f32[2,256]{1,0:T(2,128)S(1)}, u32[]{:S(2)}, u32[]{:S(2)}) collective-permute-start(f32[2,256]{1,0:T(2,128)S(1)} %pad_maximum_fusion), channel_id=1, source_target_pairs={{0,8},{8,0},{4,12},{12,4},{1,9},{9,1},{5,13},{13,5},{2,10},{10,2},... | collective-permute-start | bytes 6152 | tf_op jit(solution)/shard_map/ppermute | solution.py:229
  5.1 0.8 copy.14
  5.9 0.8 dynamic_slice.3
  6.7 0.8 fusion.32
  7.7 0.4 collective-permute-start.1
  8.2 0.7 collective-permute-done.1
  9.0 0.3 fusion.25
  9.3 0.4 copy-done.12
  9.6 1.2 %fusion.7.refs_3_.refs_4_ = bf16[144,3072]{1,0:T(8,128)(2,1)S(1)} fusion(bf16[256,3072]{1,0:T(8,128)(2,1)S(1)} %copy-done.12, bf16[256,3072]{1,0:T(8,128)(2,1)S(1)} %copy-done.13), kind=kLoop, calls=%fused_computation.21 | loop fusion | flops 9289728 | bytes 2654208 | tf_op jit(solution)/shard_map/convert_element_type | solution.py:293
  10.9 0.4 collective-permute-start.3
  11.3 1.8 %fusion.16.refs_4_.refs_5_ = bf16[112,3072]{1,0:T(8,128)(2,1)} fusion(bf16[256,3072]{1,0:T(8,128)(2,1)S(1)} %copy-done.12, bf16[256,3072]{1,0:T(8,128)(2,1)S(1)} %copy-done.13), kind=kLoop, calls=%fused_computation.30 | loop fusion | flops 7225344 | bytes 2064384 | tf_op jit(solution)/shard_map/convert_element_type | solution.py:293
  13.3 1.9 %collective-permute-start.6 = (bf16[144,3072]{1,0:T(8,128)(2,1)S(1)}, bf16[144,3072]{1,0:T(8,128)(2,1)S(1)}, u32[]{:S(2)}, u32[]{:S(2)}) collective-permute-start(bf16[144,3072]{1,0:T(8,128)(2,1)S(1)} %fusion.7.refs_3_.refs_4_), channel_id=1, source_target_pairs={{0,8},{8,0},{4,12},{12,4},{1,9},{9,1},{5,13},{13,5},{2,10},{10,2},... | collective-permute-start | bytes 2654216 | tf_op jit(solution)/shard_map/ppermute | solution.py:297
  15.2 1.2 %broadcast_in_dim.2 = bf16[4,256,768]{2,1,0:T(8,128)(2,1)} broadcast(bf16[256,768]{1,0:T(8,128)(2,1)S(1)} %fusion.25), dimensions={1,2} | broadcast | bytes 1966080 | tf_op jit(solution)/shard_map/broadcast_in_dim | solution.py:284
  16.5 4.9 %all-to-all-start = ((bf16[4,256,768]{2,1,0:T(8,128)(2,1)}), bf16[4,256,768]{2,1,0:T(8,128)(2,1)}, u32[]{:S(2)}, u32[]{:S(2)}) async-start(bf16[4,256,768]{2,1,0:T(8,128)(2,1)} %broadcast_in_dim.2), calls=%async_computation | async-start | bytes 3145728 | tf_op jit(solution)/shard_map/all_to_all | solution.py:283
  21.3 0.9 copy-done.7
  22.3 9.6 %shard_map.121 = (bf16[256,768]{1,0:T(8,128)(2,1)S(1)}, bf16[256,768]{1,0:T(8,128)(2,1)S(1)}, f32[8,128]{1,0:T(8,128)}) custom-call(s32[2]{0:T(128)S(1)} %pad_add_fusion.refs_0_, bf16[256,2304]{1,0:T(8,128)(2,1)} %refs_4_.1, bf16[256,2304]{1,0:T(8,128)(2,1)} %collective-permute-done.2.refs_2_.refs_5_, bf16[144,3072]{1,0:T(8,128)(2,1)} %copy-done.4, ...), custom_call_target="tpu_custom_call" | custom-call | flops 1 | bytes 1 | tf_op jit(solution)/shard_map/pallas_call | solution.py:155
  31.8 2.2 %collective-permute-done.7.refs_0_.refs_6_ = bf16[256,2304]{1,0:T(8,128)(2,1)} collective-permute-done((bf16[256,2304]{1,0:T(8,128)(2,1)}, bf16[256,2304]{1,0:T(8,128)(2,1)}, u32[]{:S(2)}, u32[]{:S(2)}) %collective-permute-start.7) | collective-permute-done | bytes 1179680 | tf_op jit(solution)/shard_map/ppermute | solution.py:264
  34.0 1.3 %fusion.54 = (bf16[128,2304]{1,0:T(8,128)(2,1)S(1)}, bf16[128,2304]{1,0:T(8,128)(2,1)S(1)}) fusion(bf16[256,2304]{1,0:T(8,128)(2,1)} %collective-permute-done.7.refs_0_.refs_6_), kind=kLoop, calls=%fused_computation.94 | loop fusion | bytes 2359296 | tf_op jit(solution)/shard_map/slice | solution.py:314
  35.4 0.5 collective-permute-start.8
  35.9 1.5 %collective-permute-done.9.refs_2_.refs_8_ = bf16[128,2304]{1,0:T(8,128)(2,1)S(1)} collective-permute-done((bf16[128,2304]{1,0:T(8,128)(2,1)S(1)}, bf16[128,2304]{1,0:T(8,128)(2,1)S(1)}, u32[]{:S(2)}, u32[]{:S(2)}) %collective-permute-start.9) | collective-permute-done | bytes 589856 | tf_op jit(solution)/shard_map/ppermute | solution.py:314
  37.4 0.8 collective-permute-done.8.refs_1_.refs_7_
  38.3 0.8 copy-done.11
  39.1 6.1 %shard_map.122 = (f32[512,768]{1,0:T(8,128)}, f32[8,128]{1,0:T(8,128)S(1)}) custom-call(bf16[256,2304]{1,0:T(8,128)(2,1)} %collective-permute-done.7.refs_0_.refs_6_, bf16[128,2304]{1,0:T(8,128)(2,1)} %copy-done.11, bf16[128,2304]{1,0:T(8,128)(2,1)} %copy-done.10, bf16[768,2304]{1,0:T(8,128)(2,1)} %refs_3_.3), custom_call_target="tpu_custom_call" | custom-call | flops 1 | bytes 1 | tf_op jit(solution)/shard_map/pallas_call | solution.py:155
  45.3 7.2 %collective-permute-done.6.refs_1_.refs_8_ = bf16[144,3072]{1,0:T(8,128)(2,1)S(1)} collective-permute-done((bf16[144,3072]{1,0:T(8,128)(2,1)S(1)}, bf16[144,3072]{1,0:T(8,128)(2,1)S(1)}, u32[]{:S(2)}, u32[]{:S(2)}) %collective-permute-start.6) | collective-permute-done | bytes 884768 | tf_op jit(solution)/shard_map/ppermute | solution.py:297
  52.5 0.3 collective-permute-start.13
  52.8 1.8 %collective-permute-start.5 = (bf16[256,768]{1,0:T(8,128)(2,1)S(1)}, bf16[256,768]{1,0:T(8,128)(2,1)S(1)}, u32[]{:S(2)}, u32[]{:S(2)}) collective-permute-start(bf16[256,768]{1,0:T(8,128)(2,1)S(1)} %get-tuple-element.31), channel_id=1, source_target_pairs={{0,1},{1,0},{2,3},{3,2},{4,5},{5,4},{6,7},{7,6},{8,9},{9,8},{10,11... | collective-permute-start | bytes 1179656 | tf_op jit(solution)/shard_map/ppermute | solution.py:310
  54.6 0.3 collective-permute-done.10.refs_2_.refs_10_
  54.9 5.4 %shard_map.123 = (bf16[144,768]{1,0:T(8,128)(2,1)S(1)}, bf16[144,768]{1,0:T(8,128)(2,1)}, f32[8,128]{1,0:T(8,128)S(1)}) custom-call(s32[2]{0:T(128)S(1)} %pad_add_fusion.refs_0_, bf16[144,3072]{1,0:T(8,128)(2,1)S(1)} %collective-permute-done.6.refs_1_.refs_8_, bf16[144,3072]{1,0:T(8,128)(2,1)S(1)} %collective-permute-done.10.refs_2_.refs_10_, ...), custom_call_target="tpu_custom_call" | custom-call | flops 1 | bytes 1 | tf_op jit(solution)/shard_map/pallas_call | solution.py:155
  60.4 1.6 %collective-permute-start.11 = (bf16[144,768]{1,0:T(8,128)(2,1)}, bf16[144,768]{1,0:T(8,128)(2,1)S(1)}, u32[]{:S(2)}, u32[]{:S(2)}) collective-permute-start(bf16[144,768]{1,0:T(8,128)(2,1)} %get-tuple-element.38), channel_id=1, source_target_pairs={{0,1},{1,0},{2,3},{3,2},{4,5},{5,4},{6,7},{7,6},{8,9},{9,8},{10,11... | collective-permute-start | bytes 663560 | tf_op jit(solution)/shard_map/ppermute | solution.py:349
  62.1 8.2 %shard_map.124 = (bf16[768,2304]{1,0:T(8,128)(2,1)}, f32[8,128]{1,0:T(8,128)S(1)}) custom-call(s32[4]{0:T(128)S(1)} %pad_add_fusion.1.places, bf16[1024,768]{1,0:T(8,128)(2,1)} %bitcast.12.refs_0_.refs_1_.refs_2_.refs_3_, bf16[1024,768]{1,0:T(8,128)(2,1)} %bitcast.12.refs_0_.refs_1_.refs_2_.refs_3_, ...), custom_call_target="tpu_custom_call" | custom-call | flops 1 | bytes 1 | tf_op jit(solution)/shard_map/pallas_call | solution.py:205
  70.3 0.3 collective-permute-done.13.refs_1_.refs_9_
  70.6 1.0 collective-permute-done.11
  71.8 1.7 %collective-permute-start.12 = (bf16[112,768]{1,0:T(8,128)(2,1)S(1)}, bf16[112,768]{1,0:T(8,128)(2,1)S(1)}, u32[]{:S(2)}, u32[]{:S(2)}) collective-permute-start(bf16[112,768]{1,0:T(8,128)(2,1)S(1)} %slice.86), channel_id=1, source_target_pairs={{0,2},{2,0},{1,3},{3,1},{4,6},{6,4},{5,7},{7,5},{8,10},{10,8},{9,1... | collective-permute-start | bytes 516104 | tf_op jit(solution)/shard_map/ppermute | solution.py:367
  73.7 4.5 %shard_map.125 = (bf16[112,768]{1,0:T(8,128)(2,1)S(1)}, bf16[112,768]{1,0:T(8,128)(2,1)S(1)}, f32[8,128]{1,0:T(8,128)S(1)}) custom-call(s32[2]{0:T(128)S(1)} %pad_add_fusion.refs_0_, bf16[112,3072]{1,0:T(8,128)(2,1)S(1)} %collective-permute-done.13.refs_1_.refs_9_, bf16[112,3072]{1,0:T(8,128)(2,1)S(1)} %collective-permute-done.14.refs_2_.refs_11_, ...), custom_call_target="tpu_custom_call" | custom-call | flops 1 | bytes 1 | tf_op jit(solution)/shard_map/pallas_call | solution.py:155
  78.3 1.4 %collective-permute-start.15 = (bf16[112,768]{1,0:T(8,128)(2,1)S(1)}, bf16[112,768]{1,0:T(8,128)(2,1)S(1)}, u32[]{:S(2)}, u32[]{:S(2)}) collective-permute-start(bf16[112,768]{1,0:T(8,128)(2,1)S(1)} %get-tuple-element.45), channel_id=1, source_target_pairs={{0,1},{1,0},{2,3},{3,2},{4,5},{5,4},{6,7},{7,6},{8,9},{9,8},{10,11... | collective-permute-start | bytes 516104 | tf_op jit(solution)/shard_map/ppermute | solution.py:349
  79.7 1.9 %collective-permute-start.16 = (bf16[32,768]{1,0:T(8,128)(2,1)S(1)}, bf16[32,768]{1,0:T(8,128)(2,1)S(1)}, u32[]{:S(2)}, u32[]{:S(2)}) collective-permute-start(bf16[32,768]{1,0:T(8,128)(2,1)S(1)} %slice.87), channel_id=1, source_target_pairs={{0,2},{2,0},{1,3},{3,1},{4,6},{6,4},{5,7},{7,5},{8,10},{10,8},{9,1... | collective-permute-start | bytes 147464 | tf_op jit(solution)/shard_map/ppermute | solution.py:367
  81.6 5.1 %shard_map.126 = (bf16[768,3072]{1,0:T(8,128)(2,1)}, f32[8,128]{1,0:T(8,128)S(1)}) custom-call(s32[4]{0:T(128)S(1)} %pad_add_fusion.1.places, bf16[1024,768]{1,0:T(8,128)(2,1)} %bitcast.12.refs_0_.refs_1_.refs_2_.refs_3_, bf16[1024,768]{1,0:T(8,128)(2,1)} %bitcast.12.refs_0_.refs_1_.refs_2_.refs_3_, ...), custom_call_target="tpu_custom_call" | custom-call | flops 1 | bytes 1 | tf_op jit(solution)/shard_map/pallas_call | solution.py:205
  86.7 1.2 %collective-permute-done.15 = bf16[112,768]{1,0:T(8,128)(2,1)S(1)} collective-permute-done((bf16[112,768]{1,0:T(8,128)(2,1)S(1)}, bf16[112,768]{1,0:T(8,128)(2,1)S(1)}, u32[]{:S(2)}, u32[]{:S(2)}) %collective-permute-start.15) | collective-permute-done | bytes 172064 | tf_op jit(solution)/shard_map/ppermute | solution.py:349
  88.0 0.7 collective-permute-start.17
  88.7 7.4 %shard_map.127 = (bf16[768,3072]{1,0:T(8,128)(2,1)}, f32[8,128]{1,0:T(8,128)}) custom-call(s32[4]{0:T(128)S(1)} %pad_add_fusion.1.places, bf16[1024,768]{1,0:T(8,128)(2,1)} %bitcast.12.refs_0_.refs_1_.refs_2_.refs_3_, bf16[1024,768]{1,0:T(8,128)(2,1)} %bitcast.12.refs_0_.refs_1_.refs_2_.refs_3_, ...), custom_call_target="tpu_custom_call", output_to_operand_aliasing={{0}: (15, {})} | custom-call | flops 1 | bytes 1 | tf_op jit(solution)/shard_map/pallas_call | solution.py:205
  96.1 2.8 %collective-permute-done.17 = bf16[112,768]{1,0:T(8,128)(2,1)S(1)} collective-permute-done((bf16[112,768]{1,0:T(8,128)(2,1)S(1)}, bf16[112,768]{1,0:T(8,128)(2,1)S(1)}, u32[]{:S(2)}, u32[]{:S(2)}) %collective-permute-start.17) | collective-permute-done | bytes 172064 | tf_op jit(solution)/shard_map/ppermute | solution.py:367
  99.1 0.5 fusion.53
  99.6 0.6 collective-permute-start.19
  100.2 0.8 collective-permute-start.20
  101.0 0.8 collective-permute-start.18
  101.8 1.4 %collective-permute-done.19 = f32[2,256]{1,0:T(2,128)S(1)} collective-permute-done((f32[2,256]{1,0:T(2,128)S(1)}, f32[2,256]{1,0:T(2,128)S(1)}, u32[]{:S(2)}, u32[]{:S(2)}) %collective-permute-start.19) | collective-permute-done | bytes 2080 | tf_op jit(solution)/shard_map/ppermute | solution.py:237
  103.3 1.0 fusion.29
  (66 shorter events, 1.6 us)
Async XLA Ops:
  0.6 8.3 %copy-start.8 = (bf16[256,768]{1,0:T(8,128)(2,1)S(1)}, bf16[256,768]{1,0:T(8,128)(2,1)}, u32[]{:S(2)}) copy-start(bf16[256,768]{1,0:T(8,128)(2,1)} %param.10) | copy-start | bytes 1179652
  0.6 6.9 %copy-start.14 = (s32[1024]{0:T(1024)S(1)}, s32[1024]{0:T(1024)}, u32[]{:S(2)}) copy-start(s32[1024]{0:T(1024)} %param.12) | copy-start | bytes 12292
  0.7 7.5 %copy-start.15 = (f32[8]{0:T(128)S(1)}, f32[8]{0:T(128)}, u32[]{:S(2)}) copy-start(f32[8]{0:T(128)} %param.14) | copy-start | bytes 100
  0.7 7.4 %copy-start.16 = (s32[8]{0:T(128)S(1)}, s32[8]{0:T(128)}, u32[]{:S(2)}) copy-start(s32[8]{0:T(128)} %param.13) | copy-start | bytes 100
  2.0 5.7 %collective-permute-start = (f32[2,256]{1,0:T(2,128)S(1)}, f32[2,256]{1,0:T(2,128)S(1)}, u32[]{:S(2)}, u32[]{:S(2)}) collective-permute-start(f32[2,256]{1,0:T(2,128)S(1)} %pad_maximum_fusion), channel_id=1, source_target_pairs={{0,8},{8,0},{4,12},{12,4},{1,9},{9,1},{5,13},{13,5},{2,10},{10,2},... | collective-permute-start | bytes 6152 | tf_op jit(solution)/shard_map/ppermute | solution.py:229
  5.0 17.3 %collective-permute-start.2 = (bf16[256,2304]{1,0:T(8,128)(2,1)}, bf16[256,2304]{1,0:T(8,128)(2,1)}, u32[]{:S(2)}, u32[]{:S(2)}) collective-permute-start(bf16[256,2304]{1,0:T(8,128)(2,1)} %refs_4_.1), channel_id=1, source_target_pairs={{0,4},{4,0},{8,12},{12,8},{1,5},{5,1},{9,13},{13,9},{2,6},{6,2},{1... | collective-permute-start | bytes 3538952 | tf_op jit(solution)/shard_map/ppermute | solution.py:266
  5.0 29.1 %collective-permute-start.7 = (bf16[256,2304]{1,0:T(8,128)(2,1)}, bf16[256,2304]{1,0:T(8,128)(2,1)}, u32[]{:S(2)}, u32[]{:S(2)}) collective-permute-start(bf16[256,2304]{1,0:T(8,128)(2,1)} %refs_4_.1), channel_id=1, source_target_pairs={{0,8},{8,0},{4,12},{12,4},{1,9},{9,1},{5,13},{13,5},{2,10},{10,2},... | collective-permute-start | bytes 3538952 | tf_op jit(solution)/shard_map/ppermute | solution.py:264
  6.7 2.6 %copy-start.13 = (bf16[256,3072]{1,0:T(8,128)(2,1)S(1)}, bf16[256,3072]{1,0:T(8,128)(2,1)}, u32[]{:S(2)}) copy-start(bf16[256,3072]{1,0:T(8,128)(2,1)} %param.16) | copy-start | bytes 4718596
  7.5 1.4 %copy-start.5 = (f32[256,1536]{1,0:T(8,128)}, f32[256,1536]{1,0:T(8,128)S(1)}, u32[]{:S(2)}) copy-start(f32[256,1536]{1,0:T(8,128)S(1)} %fusion.32) | copy-start | bytes 4718596
  7.5 2.1 %copy-start.12 = (bf16[256,3072]{1,0:T(8,128)(2,1)S(1)}, bf16[256,3072]{1,0:T(8,128)(2,1)}, u32[]{:S(2)}) copy-start(bf16[256,3072]{1,0:T(8,128)(2,1)} %param.17) | copy-start | bytes 4718596
  7.7 1.2 %collective-permute-start.1 = (f32[2,256]{1,0:T(2,128)S(1)}, f32[2,256]{1,0:T(2,128)S(1)}, u32[]{:S(2)}, u32[]{:S(2)}) collective-permute-start(f32[2,256]{1,0:T(2,128)S(1)} %fusion.52), channel_id=1, source_target_pairs={{0,4},{4,0},{8,12},{12,8},{1,5},{5,1},{9,13},{13,9},{2,6},{6,2},{1... | collective-permute-start | bytes 6152 | tf_op jit(solution)/shard_map/ppermute | solution.py:230
  10.9 5.6 %copy-start.4 = (bf16[144,3072]{1,0:T(8,128)(2,1)}, bf16[144,3072]{1,0:T(8,128)(2,1)S(1)}, u32[]{:S(2)}) copy-start(bf16[144,3072]{1,0:T(8,128)(2,1)S(1)} %fusion.7.refs_3_.refs_4_) | copy-start | bytes 2654212
  10.9 10.4 %collective-permute-start.3 = (bf16[144,3072]{1,0:T(8,128)(2,1)S(1)}, bf16[144,3072]{1,0:T(8,128)(2,1)S(1)}, u32[]{:S(2)}, u32[]{:S(2)}) collective-permute-start(bf16[144,3072]{1,0:T(8,128)(2,1)S(1)} %fusion.7.refs_3_.refs_4_), channel_id=1, source_target_pairs={{0,4},{4,0},{8,12},{12,8},{1,5},{5,1},{9,13},{13,9},{2,6},{6,2},{1... | collective-permute-start | bytes 2654216 | tf_op jit(solution)/shard_map/ppermute | solution.py:296
  13.1 8.2 %collective-permute-start.4 = (bf16[112,3072]{1,0:T(8,128)(2,1)}, bf16[112,3072]{1,0:T(8,128)(2,1)}, u32[]{:S(2)}, u32[]{:S(2)}) collective-permute-start(bf16[112,3072]{1,0:T(8,128)(2,1)} %fusion.16.refs_4_.refs_5_), channel_id=1, source_target_pairs={{0,4},{4,0},{8,12},{12,8},{1,5},{5,1},{9,13},{13,9},{2,6},{6,2},{1... | collective-permute-start | bytes 2064392 | tf_op jit(solution)/shard_map/ppermute | solution.py:296
  13.3 39.2 %collective-permute-start.6 = (bf16[144,3072]{1,0:T(8,128)(2,1)S(1)}, bf16[144,3072]{1,0:T(8,128)(2,1)S(1)}, u32[]{:S(2)}, u32[]{:S(2)}) collective-permute-start(bf16[144,3072]{1,0:T(8,128)(2,1)S(1)} %fusion.7.refs_3_.refs_4_), channel_id=1, source_target_pairs={{0,8},{8,0},{4,12},{12,4},{1,9},{9,1},{5,13},{13,5},{2,10},{10,2},... | collective-permute-start | bytes 2654216 | tf_op jit(solution)/shard_map/ppermute | solution.py:297
  16.5 45.6 %all-to-all-start = ((bf16[4,256,768]{2,1,0:T(8,128)(2,1)}), bf16[4,256,768]{2,1,0:T(8,128)(2,1)}, u32[]{:S(2)}, u32[]{:S(2)}) async-start(bf16[4,256,768]{2,1,0:T(8,128)(2,1)} %broadcast_in_dim.2), calls=%async_computation | async-start | bytes 3145728 | tf_op jit(solution)/shard_map/all_to_all | solution.py:283
  21.3 0.9 copy-start.7
  35.4 2.1 %collective-permute-start.9 = (bf16[128,2304]{1,0:T(8,128)(2,1)S(1)}, bf16[128,2304]{1,0:T(8,128)(2,1)S(1)}, u32[]{:S(2)}, u32[]{:S(2)}) collective-permute-start(bf16[128,2304]{1,0:T(8,128)(2,1)S(1)} %get-tuple-element.62), channel_id=1, source_target_pairs={{0,4},{4,0},{8,12},{12,8},{1,5},{5,1},{9,13},{13,9},{2,6},{6,2},{1... | collective-permute-start | bytes 1769480 | tf_op jit(solution)/shard_map/ppermute | solution.py:314
  35.4 2.8 %collective-permute-start.8 = (bf16[128,2304]{1,0:T(8,128)(2,1)S(1)}, bf16[128,2304]{1,0:T(8,128)(2,1)S(1)}, u32[]{:S(2)}, u32[]{:S(2)}) collective-permute-start(bf16[128,2304]{1,0:T(8,128)(2,1)S(1)} %get-tuple-element.63), channel_id=1, source_target_pairs={{0,4},{4,0},{8,12},{12,8},{1,5},{5,1},{9,13},{13,9},{2,6},{6,2},{1... | collective-permute-start | bytes 1769480 | tf_op jit(solution)/shard_map/ppermute | solution.py:314
  37.4 0.8 copy-start.10
  38.3 0.8 copy-start.11
  52.5 7.8 %copy-start = (bf16[144,3072]{1,0:T(8,128)(2,1)}, bf16[144,3072]{1,0:T(8,128)(2,1)S(1)}, u32[]{:S(2)}) copy-start(bf16[144,3072]{1,0:T(8,128)(2,1)S(1)} %collective-permute-done.6.refs_1_.refs_8_) | copy-start | bytes 2654212
  52.5 2.4 %collective-permute-start.10 = (bf16[144,3072]{1,0:T(8,128)(2,1)S(1)}, bf16[144,3072]{1,0:T(8,128)(2,1)S(1)}, u32[]{:S(2)}, u32[]{:S(2)}) collective-permute-start(bf16[144,3072]{1,0:T(8,128)(2,1)S(1)} %collective-permute-done.6.refs_1_.refs_8_), channel_id=1, source_target_pairs={{0,4},{4,0},{8,12},{12,8},{1,5},{5,1},{9,13},{13,9},{2,6},{6,2},{1... | collective-permute-start | bytes 2654216 | tf_op jit(solution)/shard_map/ppermute | solution.py:332
  52.5 18.1 %collective-permute-start.13 = (bf16[112,3072]{1,0:T(8,128)(2,1)}, bf16[112,3072]{1,0:T(8,128)(2,1)S(1)}, u32[]{:S(2)}, u32[]{:S(2)}) collective-permute-start(bf16[112,3072]{1,0:T(8,128)(2,1)} %fusion.16.refs_4_.refs_5_), channel_id=1, source_target_pairs={{0,8},{8,0},{4,12},{12,4},{1,9},{9,1},{5,13},{13,5},{2,10},{10,2},... | collective-permute-start | bytes 2064392 | tf_op jit(solution)/shard_map/ppermute | solution.py:297
  52.8 17.8 %collective-permute-start.5 = (bf16[256,768]{1,0:T(8,128)(2,1)S(1)}, bf16[256,768]{1,0:T(8,128)(2,1)S(1)}, u32[]{:S(2)}, u32[]{:S(2)}) collective-permute-start(bf16[256,768]{1,0:T(8,128)(2,1)S(1)} %get-tuple-element.31), channel_id=1, source_target_pairs={{0,1},{1,0},{2,3},{3,2},{4,5},{5,4},{6,7},{7,6},{8,9},{9,8},{10,11... | collective-permute-start | bytes 1179656 | tf_op jit(solution)/shard_map/ppermute | solution.py:310
  54.9 5.4 %copy-start.1 = (bf16[144,3072]{1,0:T(8,128)(2,1)}, bf16[144,3072]{1,0:T(8,128)(2,1)S(1)}, u32[]{:S(2)}) copy-start(bf16[144,3072]{1,0:T(8,128)(2,1)S(1)} %collective-permute-done.10.refs_2_.refs_10_) | copy-start | bytes 2654212
  60.4 11.2 %collective-permute-start.11 = (bf16[144,768]{1,0:T(8,128)(2,1)}, bf16[144,768]{1,0:T(8,128)(2,1)S(1)}, u32[]{:S(2)}, u32[]{:S(2)}) collective-permute-start(bf16[144,768]{1,0:T(8,128)(2,1)} %get-tuple-element.38), channel_id=1, source_target_pairs={{0,1},{1,0},{2,3},{3,2},{4,5},{5,4},{6,7},{7,6},{8,9},{9,8},{10,11... | collective-permute-start | bytes 663560 | tf_op jit(solution)/shard_map/ppermute | solution.py:349
  70.6 7.7 %copy-start.2 = (bf16[112,3072]{1,0:T(8,128)(2,1)}, bf16[112,3072]{1,0:T(8,128)(2,1)S(1)}, u32[]{:S(2)}) copy-start(bf16[112,3072]{1,0:T(8,128)(2,1)S(1)} %collective-permute-done.13.refs_1_.refs_9_) | copy-start | bytes 2064388
  71.6 2.1 %collective-permute-start.14 = (bf16[112,3072]{1,0:T(8,128)(2,1)S(1)}, bf16[112,3072]{1,0:T(8,128)(2,1)S(1)}, u32[]{:S(2)}, u32[]{:S(2)}) collective-permute-start(bf16[112,3072]{1,0:T(8,128)(2,1)S(1)} %collective-permute-done.13.refs_1_.refs_9_), channel_id=1, source_target_pairs={{0,4},{4,0},{8,12},{12,8},{1,5},{5,1},{9,13},{13,9},{2,6},{6,2},{1... | collective-permute-start | bytes 2064392 | tf_op jit(solution)/shard_map/ppermute | solution.py:332
  71.8 14.9 %collective-permute-start.12 = (bf16[112,768]{1,0:T(8,128)(2,1)S(1)}, bf16[112,768]{1,0:T(8,128)(2,1)S(1)}, u32[]{:S(2)}, u32[]{:S(2)}) collective-permute-start(bf16[112,768]{1,0:T(8,128)(2,1)S(1)} %slice.86), channel_id=1, source_target_pairs={{0,2},{2,0},{1,3},{3,1},{4,6},{6,4},{5,7},{7,5},{8,10},{10,8},{9,1... | collective-permute-start | bytes 516104 | tf_op jit(solution)/shard_map/ppermute | solution.py:367
  73.7 4.5 %copy-start.3 = (bf16[112,3072]{1,0:T(8,128)(2,1)}, bf16[112,3072]{1,0:T(8,128)(2,1)S(1)}, u32[]{:S(2)}) copy-start(bf16[112,3072]{1,0:T(8,128)(2,1)S(1)} %collective-permute-done.14.refs_2_.refs_11_) | copy-start | bytes 2064388
  78.3 9.6 %collective-permute-start.15 = (bf16[112,768]{1,0:T(8,128)(2,1)S(1)}, bf16[112,768]{1,0:T(8,128)(2,1)S(1)}, u32[]{:S(2)}, u32[]{:S(2)}) collective-permute-start(bf16[112,768]{1,0:T(8,128)(2,1)S(1)} %get-tuple-element.45), channel_id=1, source_target_pairs={{0,1},{1,0},{2,3},{3,2},{4,5},{5,4},{6,7},{7,6},{8,9},{9,8},{10,11... | collective-permute-start | bytes 516104 | tf_op jit(solution)/shard_map/ppermute | solution.py:349
  79.7 7.0 %collective-permute-start.16 = (bf16[32,768]{1,0:T(8,128)(2,1)S(1)}, bf16[32,768]{1,0:T(8,128)(2,1)S(1)}, u32[]{:S(2)}, u32[]{:S(2)}) collective-permute-start(bf16[32,768]{1,0:T(8,128)(2,1)S(1)} %slice.87), channel_id=1, source_target_pairs={{0,2},{2,0},{1,3},{3,1},{4,6},{6,4},{5,7},{7,5},{8,10},{10,8},{9,1... | collective-permute-start | bytes 147464 | tf_op jit(solution)/shard_map/ppermute | solution.py:367
  88.0 10.9 %collective-permute-start.17 = (bf16[112,768]{1,0:T(8,128)(2,1)S(1)}, bf16[112,768]{1,0:T(8,128)(2,1)S(1)}, u32[]{:S(2)}, u32[]{:S(2)}) collective-permute-start(bf16[112,768]{1,0:T(8,128)(2,1)S(1)} %select_convert_fusion.1.refs_13_), channel_id=1, source_target_pairs={{0,2},{2,0},{1,3},{3,1},{4,6},{6,4},{5,7},{7,5},{8,10},{10,8},{9,1... | collective-permute-start | bytes 516104 | tf_op jit(solution)/shard_map/ppermute | solution.py:367
  96.1 3.0 %copy-start.6 = (f32[256,1536]{1,0:T(8,128)S(1)}, f32[256,1536]{1,0:T(8,128)}, u32[]{:S(2)}) copy-start(f32[256,1536]{1,0:T(8,128)} %copy-done.5) | copy-start | bytes 4718596
  96.1 3.0 %copy-start.9 = (bf16[256,768]{1,0:T(8,128)(2,1)S(1)}, bf16[256,768]{1,0:T(8,128)(2,1)}, u32[]{:S(2)}) copy-start(bf16[256,768]{1,0:T(8,128)(2,1)} %param.10) | copy-start | bytes 1179652
  99.6 3.6 %collective-permute-start.19 = (f32[2,256]{1,0:T(2,128)S(1)}, f32[2,256]{1,0:T(2,128)S(1)}, u32[]{:S(2)}, u32[]{:S(2)}) collective-permute-start(f32[2,256]{1,0:T(2,128)S(1)} %pad_maximum_fusion.1), channel_id=1, source_target_pairs={{0,8},{8,0},{4,12},{12,4},{1,9},{9,1},{5,13},{13,5},{2,10},{10,2},... | collective-permute-start | bytes 6152 | tf_op jit(solution)/shard_map/ppermute | solution.py:237
  100.2 3.1 %collective-permute-start.20 = (f32[2,256]{1,0:T(2,128)S(1)}, f32[2,256]{1,0:T(2,128)S(1)}, u32[]{:S(2)}, u32[]{:S(2)}) collective-permute-start(f32[2,256]{1,0:T(2,128)S(1)} %pad_maximum_fusion.1), channel_id=1, source_target_pairs={{0,12},{12,0},{4,8},{8,4},{1,13},{13,1},{5,9},{9,5},{2,14},{14,2},... | collective-permute-start | bytes 6152 | tf_op jit(solution)/shard_map/ppermute | solution.py:238
  101.0 2.2 %collective-permute-start.18 = (f32[2,256]{1,0:T(2,128)S(1)}, f32[2,256]{1,0:T(2,128)S(1)}, u32[]{:S(2)}, u32[]{:S(2)}) collective-permute-start(f32[2,256]{1,0:T(2,128)S(1)} %pad_maximum_fusion.1), channel_id=1, source_target_pairs={{0,4},{4,0},{8,12},{12,8},{1,5},{5,1},{9,13},{13,9},{2,6},{6,2},{1... | collective-permute-start | bytes 6152 | tf_op jit(solution)/shard_map/ppermute | solution.py:236

commit v7 on v5

--- a/solution.py
+++ b/solution.py
@@ -344,10 +344,11 @@
             seeds=((start, size), (tok_row + start, size)),
             hold=[mark],
             pin=False,
+            tile=1536,
         )
         send = lax.ppermute(send, "col", NEXT)
         if index == 0:
-            qkv_total, mark = weight_grad(places, parts, q_parts, hold=[mark])
+            qkv_total, mark = weight_grad(places, parts, q_parts, tile=1152, hold=[mark])
             ready = [mark, send, near_next]
         halves.append((start, size, keep, send))
 

time: 105 us -> 105 us (level)
  transfers between devices with their start and end apart: 22 -> 22, of which waited for: 11 -> 11; matrix products, arithmetic and copies ran while one was open for 9% -> 9% of each run, Pallas kernels for 45% -> 44%
where the time goes in v7:
time: 105 us
  Pallas kernels  46.6 us (44%)
  starting transfers between devices  24.2 us (23%)
  waiting for transfers between devices  18.7 us (18%)
  other arithmetic  7.47 us (7%)
  local copies, waits for them, and re-layouts  5.98 us (6%)
    pallas_call x4, Pallas kernels, back(): pl.pallas_call(functools.partial(back_kernel, layout, tile, order is not...  26 us
    pallas_call x3, Pallas kernels, weight_grad(): pl.pallas_call(functools.partial(weight_kernel, len(grads), len(extra)),...  20.6 us
    ppermute x2, waiting for transfers between devices, on_grid(): far_m = [lax.ppermute(part, 'row', CHIP) for part in own_m]  9.37 us
    ppermute x3, starting transfers between devices, on_grid(): incoming.append((own[low:high], lax.ppermute(other[low:high], 'col', SKIP)))  5.39 us
    all_to_all x1, starting transfers between devices, on_grid(): lax.all_to_all(jnp.broadcast_to(normed[None], (4,) + normed.shape), 'col'...  4.87 us
    ppermute x1, starting transfers between devices, row_sum(): pair += lax.ppermute(pair, 'row', CHIP)  3 us
    convert_element_type x2, other arithmetic, on_grid(): own_m = [(mlp_cotangent[start:start + size].astype(jnp.float32) * gelu_sl...  3 us
    ppermute x2, starting transfers between devices, on_grid(): send = lax.ppermute(send, 'col', NEXT)  2.94 us
  transfers between devices with their start and end apart: 22, of which 11 were waited for; matrix products, arithmetic and copies ran while one was open for 9% of the time, Pallas kernels for 44%

profile of v7, /device:TPU:0, one launch (start us, length us, event | category | flops | bytes accessed | tf_op | source)
XLA Modules:
  0.0 104.8 jit_solution(8346190787407429103)
XLA Ops:
  0.7 1.3 %convert_reduce_fusion = (f32[256]{0:T(256)S(1)}, f32[256]{0:T(256)S(1)}) fusion(bf16[256,768]{1,0:T(8,128)(2,1)} %param.10), kind=kLoop, calls=%fused_computation.25 | loop fusion | flops 785920 | bytes 395264 | tf_op jit(solution)/shard_map/reduce_sum | solution.py:263
  2.0 3.0 %collective-permute-start = (f32[2,256]{1,0:T(2,128)S(1)}, f32[2,256]{1,0:T(2,128)S(1)}, u32[]{:S(2)}, u32[]{:S(2)}) collective-permute-start(f32[2,256]{1,0:T(2,128)S(1)} %pad_maximum_fusion), channel_id=1, source_target_pairs={{0,8},{8,0},{4,12},{12,4},{1,9},{9,1},{5,13},{13,5},{2,10},{10,2},... | collective-permute-start | bytes 6152 | tf_op jit(solution)/shard_map/ppermute | solution.py:229
  5.0 0.2 collective-permute-start.7
  5.1 0.8 copy.14
  5.9 0.8 dynamic_slice.3
  6.7 0.8 fusion.32
  7.7 0.4 collective-permute-start.1
  8.2 0.7 collective-permute-done.1
  9.0 1.0 fusion.25
  10.0 1.4 %fusion.7.refs_3_.refs_4_ = bf16[160,3072]{1,0:T(8,128)(2,1)S(1)} fusion(bf16[256,3072]{1,0:T(8,128)(2,1)S(1)} %copy-done.12, bf16[256,3072]{1,0:T(8,128)(2,1)S(1)} %copy-done.13), kind=kLoop, calls=%fused_computation.21 | loop fusion | flops 10321920 | bytes 2949120 | tf_op jit(solution)/shard_map/convert_element_type | solution.py:293
  11.4 0.4 collective-permute-start.3
  11.8 1.6 %fusion.16.refs_4_.refs_5_ = bf16[96,3072]{1,0:T(8,128)(2,1)} fusion(bf16[256,3072]{1,0:T(8,128)(2,1)S(1)} %copy-done.12, bf16[256,3072]{1,0:T(8,128)(2,1)S(1)} %copy-done.13), kind=kLoop, calls=%fused_computation.33 | loop fusion | flops 6193152 | bytes 1769472 | tf_op jit(solution)/shard_map/convert_element_type | solution.py:293
  13.4 0.2 collective-permute-start.4
  13.7 1.9 %collective-permute-start.6 = (bf16[160,3072]{1,0:T(8,128)(2,1)S(1)}, bf16[160,3072]{1,0:T(8,128)(2,1)S(1)}, u32[]{:S(2)}, u32[]{:S(2)}) collective-permute-start(bf16[160,3072]{1,0:T(8,128)(2,1)S(1)} %fusion.7.refs_3_.refs_4_), channel_id=1, source_target_pairs={{0,8},{8,0},{4,12},{12,4},{1,9},{9,1},{5,13},{13,5},{2,10},{10,2},... | collective-permute-start | bytes 2949128 | tf_op jit(solution)/shard_map/ppermute | solution.py:297
  15.5 1.2 %broadcast_in_dim.2 = bf16[4,256,768]{2,1,0:T(8,128)(2,1)} broadcast(bf16[256,768]{1,0:T(8,128)(2,1)S(1)} %copy-done.14), dimensions={1,2} | broadcast | bytes 1966080 | tf_op jit(solution)/shard_map/broadcast_in_dim | solution.py:284
  16.8 4.9 %all-to-all-start = ((bf16[4,256,768]{2,1,0:T(8,128)(2,1)}), bf16[4,256,768]{2,1,0:T(8,128)(2,1)}, u32[]{:S(2)}, u32[]{:S(2)}) async-start(bf16[4,256,768]{2,1,0:T(8,128)(2,1)} %broadcast_in_dim.2), calls=%async_computation | async-start | bytes 3145728 | tf_op jit(solution)/shard_map/all_to_all | solution.py:283
  21.7 0.9 copy-done.7
  22.6 10.3 %shard_map.121 = (bf16[256,768]{1,0:T(8,128)(2,1)S(1)}, bf16[256,768]{1,0:T(8,128)(2,1)}, f32[8,128]{1,0:T(8,128)}) custom-call(s32[2]{0:T(128)S(1)} %pad_add_fusion.refs_0_, bf16[256,2304]{1,0:T(8,128)(2,1)} %refs_4_.1, bf16[256,2304]{1,0:T(8,128)(2,1)} %collective-permute-done.2.refs_2_.refs_5_, bf16[160,3072]{1,0:T(8,128)(2,1)} %copy-done.4, ...), custom_call_target="tpu_custom_call" | custom-call | flops 1 | bytes 1 | tf_op jit(solution)/shard_map/pallas_call | solution.py:155
  32.9 1.1 %collective-permute-done.7.refs_0_.refs_6_ = bf16[256,2304]{1,0:T(8,128)(2,1)} collective-permute-done((bf16[256,2304]{1,0:T(8,128)(2,1)}, bf16[256,2304]{1,0:T(8,128)(2,1)}, u32[]{:S(2)}, u32[]{:S(2)}) %collective-permute-start.7) | collective-permute-done | bytes 1179680 | tf_op jit(solution)/shard_map/ppermute | solution.py:264
  34.0 1.3 %fusion.54 = (bf16[128,2304]{1,0:T(8,128)(2,1)S(1)}, bf16[128,2304]{1,0:T(8,128)(2,1)S(1)}) fusion(bf16[256,2304]{1,0:T(8,128)(2,1)} %collective-permute-done.7.refs_0_.refs_6_), kind=kLoop, calls=%fused_computation.94 | loop fusion | bytes 2359296 | tf_op jit(solution)/shard_map/slice | solution.py:314
  35.4 0.5 collective-permute-start.8
  35.9 1.5 %collective-permute-done.9.refs_2_.refs_8_ = bf16[128,2304]{1,0:T(8,128)(2,1)S(1)} collective-permute-done((bf16[128,2304]{1,0:T(8,128)(2,1)S(1)}, bf16[128,2304]{1,0:T(8,128)(2,1)S(1)}, u32[]{:S(2)}, u32[]{:S(2)}) %collective-permute-start.9) | collective-permute-done | bytes 589856 | tf_op jit(solution)/shard_map/ppermute | solution.py:314
  37.4 0.8 collective-permute-done.8.refs_1_.refs_7_
  38.3 0.8 copy-done.11
  39.1 6.1 %shard_map.122 = (f32[512,768]{1,0:T(8,128)}, f32[8,128]{1,0:T(8,128)S(1)}) custom-call(bf16[256,2304]{1,0:T(8,128)(2,1)} %collective-permute-done.7.refs_0_.refs_6_, bf16[128,2304]{1,0:T(8,128)(2,1)} %copy-done.11, bf16[128,2304]{1,0:T(8,128)(2,1)} %copy-done.10, bf16[768,2304]{1,0:T(8,128)(2,1)} %refs_3_.3), custom_call_target="tpu_custom_call" | custom-call | flops 1 | bytes 1 | tf_op jit(solution)/shard_map/pallas_call | solution.py:155
  45.3 9.4 %collective-permute-done.6.refs_1_.refs_8_ = bf16[160,3072]{1,0:T(8,128)(2,1)S(1)} collective-permute-done((bf16[160,3072]{1,0:T(8,128)(2,1)S(1)}, bf16[160,3072]{1,0:T(8,128)(2,1)S(1)}, u32[]{:S(2)}, u32[]{:S(2)}) %collective-permute-start.6) | collective-permute-done | bytes 983072 | tf_op jit(solution)/shard_map/ppermute | solution.py:297
  54.6 0.3 collective-permute-start.13
  54.9 1.8 %collective-permute-start.5 = (bf16[256,768]{1,0:T(8,128)(2,1)}, bf16[256,768]{1,0:T(8,128)(2,1)S(1)}, u32[]{:S(2)}, u32[]{:S(2)}) collective-permute-start(bf16[256,768]{1,0:T(8,128)(2,1)} %get-tuple-element.31), channel_id=1, source_target_pairs={{0,1},{1,0},{2,3},{3,2},{4,5},{5,4},{6,7},{7,6},{8,9},{9,8},{10,11... | collective-permute-start | bytes 1179656 | tf_op jit(solution)/shard_map/ppermute | solution.py:310
  56.7 0.5 collective-permute-done.10.refs_2_.refs_10_
  57.2 4.9 %shard_map.123 = (bf16[160,768]{1,0:T(8,128)(2,1)S(1)}, bf16[160,768]{1,0:T(8,128)(2,1)S(1)}, f32[8,128]{1,0:T(8,128)S(1)}) custom-call(s32[2]{0:T(128)S(1)} %pad_add_fusion.refs_0_, bf16[160,3072]{1,0:T(8,128)(2,1)S(1)} %collective-permute-done.6.refs_1_.refs_8_, bf16[160,3072]{1,0:T(8,128)(2,1)S(1)} %collective-permute-done.10.refs_2_.refs_10_, ...), custom_call_target="tpu_custom_call" | custom-call | flops 1 | bytes 1 | tf_op jit(solution)/shard_map/pallas_call | solution.py:155
  62.2 1.6 %collective-permute-start.11 = (bf16[160,768]{1,0:T(8,128)(2,1)S(1)}, bf16[160,768]{1,0:T(8,128)(2,1)S(1)}, u32[]{:S(2)}, u32[]{:S(2)}) collective-permute-start(bf16[160,768]{1,0:T(8,128)(2,1)S(1)} %get-tuple-element.38), channel_id=1, source_target_pairs={{0,1},{1,0},{2,3},{3,2},{4,5},{5,4},{6,7},{7,6},{8,9},{9,8},{10,11... | collective-permute-start | bytes 737288 | tf_op jit(solution)/shard_map/ppermute | solution.py:349
  63.9 8.2 %shard_map.124 = (bf16[768,2304]{1,0:T(8,128)(2,1)}, f32[8,128]{1,0:T(8,128)S(1)}) custom-call(s32[4]{0:T(128)S(1)} %pad_add_fusion.1.places, bf16[1024,768]{1,0:T(8,128)(2,1)} %bitcast.12.refs_0_.refs_1_.refs_2_.refs_3_, bf16[1024,768]{1,0:T(8,128)(2,1)} %bitcast.12.refs_0_.refs_1_.refs_2_.refs_3_, ...), custom_call_target="tpu_custom_call" | custom-call | flops 1 | bytes 1 | tf_op jit(solution)/shard_map/pallas_call | solution.py:205
  72.1 0.3 collective-permute-done.11
  72.6 2.4 %collective-permute-start.12 = (bf16[112,768]{1,0:T(8,128)(2,1)S(1)}, bf16[112,768]{1,0:T(8,128)(2,1)S(1)}, u32[]{:S(2)}, u32[]{:S(2)}) collective-permute-start(bf16[112,768]{1,0:T(8,128)(2,1)S(1)} %slice.86), channel_id=1, source_target_pairs={{0,2},{2,0},{1,3},{3,1},{4,6},{6,4},{5,7},{7,5},{8,10},{10,8},{9,1... | collective-permute-start | bytes 516104 | tf_op jit(solution)/shard_map/ppermute | solution.py:367
  75.1 4.5 %shard_map.125 = (bf16[96,768]{1,0:T(8,128)(2,1)S(1)}, bf16[96,768]{1,0:T(8,128)(2,1)S(1)}, f32[8,128]{1,0:T(8,128)S(1)}) custom-call(s32[2]{0:T(128)S(1)} %pad_add_fusion.refs_0_, bf16[96,3072]{1,0:T(8,128)(2,1)S(1)} %collective-permute-done.13.refs_1_.refs_9_, bf16[96,3072]{1,0:T(8,128)(2,1)S(1)} %collective-permute-done.14.refs_2_.refs_11_, ...), custom_call_target="tpu_custom_call" | custom-call | flops 1 | bytes 1 | tf_op jit(solution)/shard_map/pallas_call | solution.py:155
  79.6 1.3 %collective-permute-start.15 = (bf16[96,768]{1,0:T(8,128)(2,1)S(1)}, bf16[96,768]{1,0:T(8,128)(2,1)S(1)}, u32[]{:S(2)}, u32[]{:S(2)}) collective-permute-start(bf16[96,768]{1,0:T(8,128)(2,1)S(1)} %get-tuple-element.45), channel_id=1, source_target_pairs={{0,1},{1,0},{2,3},{3,2},{4,5},{5,4},{6,7},{7,6},{8,9},{9,8},{10,11... | collective-permute-start | bytes 442376 | tf_op jit(solution)/shard_map/ppermute | solution.py:349
  80.9 1.8 %collective-permute-start.16 = (bf16[48,768]{1,0:T(8,128)(2,1)S(1)}, bf16[48,768]{1,0:T(8,128)(2,1)S(1)}, u32[]{:S(2)}, u32[]{:S(2)}) collective-permute-start(bf16[48,768]{1,0:T(8,128)(2,1)S(1)} %slice.87), channel_id=1, source_target_pairs={{0,2},{2,0},{1,3},{3,1},{4,6},{6,4},{5,7},{7,5},{8,10},{10,8},{9,1... | collective-permute-start | bytes 221192 | tf_op jit(solution)/shard_map/ppermute | solution.py:367
  82.7 5.1 %shard_map.126 = (bf16[768,3072]{1,0:T(8,128)(2,1)}, f32[8,128]{1,0:T(8,128)S(1)}) custom-call(s32[4]{0:T(128)S(1)} %pad_add_fusion.1.places, bf16[1024,768]{1,0:T(8,128)(2,1)} %bitcast.12.refs_0_.refs_1_.refs_2_.refs_3_, bf16[1024,768]{1,0:T(8,128)(2,1)} %bitcast.12.refs_0_.refs_1_.refs_2_.refs_3_, ...), custom_call_target="tpu_custom_call" | custom-call | flops 1 | bytes 1 | tf_op jit(solution)/shard_map/pallas_call | solution.py:205
  87.8 0.9 collective-permute-done.15
  88.9 1.2 %collective-permute-start.17 = (bf16[96,768]{1,0:T(8,128)(2,1)S(1)}, bf16[96,768]{1,0:T(8,128)(2,1)S(1)}, u32[]{:S(2)}, u32[]{:S(2)}) collective-permute-start(bf16[96,768]{1,0:T(8,128)(2,1)S(1)} %select_convert_fusion.1.refs_13_), channel_id=1, source_target_pairs={{0,2},{2,0},{1,3},{3,1},{4,6},{6,4},{5,7},{7,5},{8,10},{10,8},{9,1... | collective-permute-start | bytes 442376 | tf_op jit(solution)/shard_map/ppermute | solution.py:367
  90.1 7.3 %shard_map.127 = (bf16[768,3072]{1,0:T(8,128)(2,1)}, f32[8,128]{1,0:T(8,128)}) custom-call(s32[4]{0:T(128)S(1)} %pad_add_fusion.1.places, bf16[1024,768]{1,0:T(8,128)(2,1)} %bitcast.12.refs_0_.refs_1_.refs_2_.refs_3_, bf16[1024,768]{1,0:T(8,128)(2,1)} %bitcast.12.refs_0_.refs_1_.refs_2_.refs_3_, ...), custom_call_target="tpu_custom_call", output_to_operand_aliasing={{0}: (15, {})} | custom-call | flops 1 | bytes 1 | tf_op jit(solution)/shard_map/pallas_call | solution.py:205
  97.5 1.3 %collective-permute-done.17 = bf16[96,768]{1,0:T(8,128)(2,1)S(1)} collective-permute-done((bf16[96,768]{1,0:T(8,128)(2,1)S(1)}, bf16[96,768]{1,0:T(8,128)(2,1)S(1)}, u32[]{:S(2)}, u32[]{:S(2)}) %collective-permute-start.17) | collective-permute-done | bytes 147488 | tf_op jit(solution)/shard_map/ppermute | solution.py:367
  98.9 0.5 fusion.53
  99.4 1.4 %collective-permute-start.19 = (f32[2,256]{1,0:T(2,128)S(1)}, f32[2,256]{1,0:T(2,128)S(1)}, u32[]{:S(2)}, u32[]{:S(2)}) collective-permute-start(f32[2,256]{1,0:T(2,128)S(1)} %pad_maximum_fusion.1), channel_id=1, source_target_pairs={{0,8},{8,0},{4,12},{12,4},{1,9},{9,1},{5,13},{13,5},{2,10},{10,2},... | collective-permute-start | bytes 6152 | tf_op jit(solution)/shard_map/ppermute | solution.py:237
  100.8 0.8 collective-permute-start.18
  101.6 1.4 %collective-permute-done.19 = f32[2,256]{1,0:T(2,128)S(1)} collective-permute-done((f32[2,256]{1,0:T(2,128)S(1)}, f32[2,256]{1,0:T(2,128)S(1)}, u32[]{:S(2)}, u32[]{:S(2)}) %collective-permute-start.19) | collective-permute-done | bytes 2080 | tf_op jit(solution)/shard_map/ppermute | solution.py:237
  103.0 0.8 collective-permute-done.20
  103.8 1.0 fusion.29
  (69 shorter events, 1.1 us)
Async XLA Ops:
  0.6 8.3 %copy-start.8 = (bf16[256,768]{1,0:T(8,128)(2,1)S(1)}, bf16[256,768]{1,0:T(8,128)(2,1)}, u32[]{:S(2)}) copy-start(bf16[256,768]{1,0:T(8,128)(2,1)} %param.10) | copy-start | bytes 1179652
  0.6 6.9 %copy-start.15 = (s32[1024]{0:T(1024)S(1)}, s32[1024]{0:T(1024)}, u32[]{:S(2)}) copy-start(s32[1024]{0:T(1024)} %param.12) | copy-start | bytes 12292
  0.7 7.5 %copy-start.16 = (f32[8]{0:T(128)S(1)}, f32[8]{0:T(128)}, u32[]{:S(2)}) copy-start(f32[8]{0:T(128)} %param.14) | copy-start | bytes 100
  0.7 7.4 %copy-start.17 = (s32[8]{0:T(128)S(1)}, s32[8]{0:T(128)}, u32[]{:S(2)}) copy-start(s32[8]{0:T(128)} %param.13) | copy-start | bytes 100
  2.0 5.7 %collective-permute-start = (f32[2,256]{1,0:T(2,128)S(1)}, f32[2,256]{1,0:T(2,128)S(1)}, u32[]{:S(2)}, u32[]{:S(2)}) collective-permute-start(f32[2,256]{1,0:T(2,128)S(1)} %pad_maximum_fusion), channel_id=1, source_target_pairs={{0,8},{8,0},{4,12},{12,4},{1,9},{9,1},{5,13},{13,5},{2,10},{10,2},... | collective-permute-start | bytes 6152 | tf_op jit(solution)/shard_map/ppermute | solution.py:229
  5.0 17.7 %collective-permute-start.2 = (bf16[256,2304]{1,0:T(8,128)(2,1)}, bf16[256,2304]{1,0:T(8,128)(2,1)}, u32[]{:S(2)}, u32[]{:S(2)}) collective-permute-start(bf16[256,2304]{1,0:T(8,128)(2,1)} %refs_4_.1), channel_id=1, source_target_pairs={{0,4},{4,0},{8,12},{12,8},{1,5},{5,1},{9,13},{13,9},{2,6},{6,2},{1... | collective-permute-start | bytes 3538952 | tf_op jit(solution)/shard_map/ppermute | solution.py:266
  5.0 29.1 %collective-permute-start.7 = (bf16[256,2304]{1,0:T(8,128)(2,1)}, bf16[256,2304]{1,0:T(8,128)(2,1)}, u32[]{:S(2)}, u32[]{:S(2)}) collective-permute-start(bf16[256,2304]{1,0:T(8,128)(2,1)} %refs_4_.1), channel_id=1, source_target_pairs={{0,8},{8,0},{4,12},{12,4},{1,9},{9,1},{5,13},{13,5},{2,10},{10,2},... | collective-permute-start | bytes 3538952 | tf_op jit(solution)/shard_map/ppermute | solution.py:264
  6.7 3.3 %copy-start.13 = (bf16[256,3072]{1,0:T(8,128)(2,1)S(1)}, bf16[256,3072]{1,0:T(8,128)(2,1)}, u32[]{:S(2)}) copy-start(bf16[256,3072]{1,0:T(8,128)(2,1)} %param.16) | copy-start | bytes 4718596
  7.5 1.4 %copy-start.5 = (f32[256,1536]{1,0:T(8,128)}, f32[256,1536]{1,0:T(8,128)S(1)}, u32[]{:S(2)}) copy-start(f32[256,1536]{1,0:T(8,128)S(1)} %fusion.32) | copy-start | bytes 4718596
  7.5 2.5 %copy-start.12 = (bf16[256,3072]{1,0:T(8,128)(2,1)S(1)}, bf16[256,3072]{1,0:T(8,128)(2,1)}, u32[]{:S(2)}) copy-start(bf16[256,3072]{1,0:T(8,128)(2,1)} %param.17) | copy-start | bytes 4718596
  7.7 1.2 %collective-permute-start.1 = (f32[2,256]{1,0:T(2,128)S(1)}, f32[2,256]{1,0:T(2,128)S(1)}, u32[]{:S(2)}, u32[]{:S(2)}) collective-permute-start(f32[2,256]{1,0:T(2,128)S(1)} %fusion.52), channel_id=1, source_target_pairs={{0,4},{4,0},{8,12},{12,8},{1,5},{5,1},{9,13},{13,9},{2,6},{6,2},{1... | collective-permute-start | bytes 6152 | tf_op jit(solution)/shard_map/ppermute | solution.py:230
  11.4 5.4 %copy-start.4 = (bf16[160,3072]{1,0:T(8,128)(2,1)}, bf16[160,3072]{1,0:T(8,128)(2,1)S(1)}, u32[]{:S(2)}) copy-start(bf16[160,3072]{1,0:T(8,128)(2,1)S(1)} %fusion.7.refs_3_.refs_4_) | copy-start | bytes 2949124
  11.4 4.2 %copy-start.14 = (bf16[256,768]{1,0:T(8,128)(2,1)S(1)}, bf16[256,768]{1,0:T(8,128)(2,1)}, u32[]{:S(2)}) copy-start(bf16[256,768]{1,0:T(8,128)(2,1)} %fusion.25) | copy-start | bytes 1179652
  11.4 10.3 %collective-permute-start.3 = (bf16[160,3072]{1,0:T(8,128)(2,1)S(1)}, bf16[160,3072]{1,0:T(8,128)(2,1)S(1)}, u32[]{:S(2)}, u32[]{:S(2)}) collective-permute-start(bf16[160,3072]{1,0:T(8,128)(2,1)S(1)} %fusion.7.refs_3_.refs_4_), channel_id=1, source_target_pairs={{0,4},{4,0},{8,12},{12,8},{1,5},{5,1},{9,13},{13,9},{2,6},{6,2},{1... | collective-permute-start | bytes 2949128 | tf_op jit(solution)/shard_map/ppermute | solution.py:296
  13.4 8.2 %collective-permute-start.4 = (bf16[96,3072]{1,0:T(8,128)(2,1)}, bf16[96,3072]{1,0:T(8,128)(2,1)}, u32[]{:S(2)}, u32[]{:S(2)}) collective-permute-start(bf16[96,3072]{1,0:T(8,128)(2,1)} %fusion.16.refs_4_.refs_5_), channel_id=1, source_target_pairs={{0,4},{4,0},{8,12},{12,8},{1,5},{5,1},{9,13},{13,9},{2,6},{6,2},{1... | collective-permute-start | bytes 1769480 | tf_op jit(solution)/shard_map/ppermute | solution.py:296
  13.7 40.9 %collective-permute-start.6 = (bf16[160,3072]{1,0:T(8,128)(2,1)S(1)}, bf16[160,3072]{1,0:T(8,128)(2,1)S(1)}, u32[]{:S(2)}, u32[]{:S(2)}) collective-permute-start(bf16[160,3072]{1,0:T(8,128)(2,1)S(1)} %fusion.7.refs_3_.refs_4_), channel_id=1, source_target_pairs={{0,8},{8,0},{4,12},{12,4},{1,9},{9,1},{5,13},{13,5},{2,10},{10,2},... | collective-permute-start | bytes 2949128 | tf_op jit(solution)/shard_map/ppermute | solution.py:297
  16.8 47.1 %all-to-all-start = ((bf16[4,256,768]{2,1,0:T(8,128)(2,1)}), bf16[4,256,768]{2,1,0:T(8,128)(2,1)}, u32[]{:S(2)}, u32[]{:S(2)}) async-start(bf16[4,256,768]{2,1,0:T(8,128)(2,1)} %broadcast_in_dim.2), calls=%async_computation | async-start | bytes 3145728 | tf_op jit(solution)/shard_map/all_to_all | solution.py:283
  21.7 0.9 copy-start.7
  35.4 2.1 %collective-permute-start.9 = (bf16[128,2304]{1,0:T(8,128)(2,1)S(1)}, bf16[128,2304]{1,0:T(8,128)(2,1)S(1)}, u32[]{:S(2)}, u32[]{:S(2)}) collective-permute-start(bf16[128,2304]{1,0:T(8,128)(2,1)S(1)} %get-tuple-element.62), channel_id=1, source_target_pairs={{0,4},{4,0},{8,12},{12,8},{1,5},{5,1},{9,13},{13,9},{2,6},{6,2},{1... | collective-permute-start | bytes 1769480 | tf_op jit(solution)/shard_map/ppermute | solution.py:314
  35.4 2.8 %collective-permute-start.8 = (bf16[128,2304]{1,0:T(8,128)(2,1)S(1)}, bf16[128,2304]{1,0:T(8,128)(2,1)S(1)}, u32[]{:S(2)}, u32[]{:S(2)}) collective-permute-start(bf16[128,2304]{1,0:T(8,128)(2,1)S(1)} %get-tuple-element.63), channel_id=1, source_target_pairs={{0,4},{4,0},{8,12},{12,8},{1,5},{5,1},{9,13},{13,9},{2,6},{6,2},{1... | collective-permute-start | bytes 1769480 | tf_op jit(solution)/shard_map/ppermute | solution.py:314
  37.4 0.8 copy-start.10
  38.3 0.8 copy-start.11
  54.6 7.5 %copy-start = (bf16[160,3072]{1,0:T(8,128)(2,1)}, bf16[160,3072]{1,0:T(8,128)(2,1)S(1)}, u32[]{:S(2)}) copy-start(bf16[160,3072]{1,0:T(8,128)(2,1)S(1)} %collective-permute-done.6.refs_1_.refs_8_) | copy-start | bytes 2949124
  54.6 2.6 %collective-permute-start.10 = (bf16[160,3072]{1,0:T(8,128)(2,1)S(1)}, bf16[160,3072]{1,0:T(8,128)(2,1)S(1)}, u32[]{:S(2)}, u32[]{:S(2)}) collective-permute-start(bf16[160,3072]{1,0:T(8,128)(2,1)S(1)} %collective-permute-done.6.refs_1_.refs_8_), channel_id=1, source_target_pairs={{0,4},{4,0},{8,12},{12,8},{1,5},{5,1},{9,13},{13,9},{2,6},{6,2},{1... | collective-permute-start | bytes 2949128 | tf_op jit(solution)/shard_map/ppermute | solution.py:332
  54.6 17.5 %collective-permute-start.13 = (bf16[96,3072]{1,0:T(8,128)(2,1)}, bf16[96,3072]{1,0:T(8,128)(2,1)S(1)}, u32[]{:S(2)}, u32[]{:S(2)}) collective-permute-start(bf16[96,3072]{1,0:T(8,128)(2,1)} %fusion.16.refs_4_.refs_5_), channel_id=1, source_target_pairs={{0,8},{8,0},{4,12},{12,4},{1,9},{9,1},{5,13},{13,5},{2,10},{10,2},... | collective-permute-start | bytes 1769480 | tf_op jit(solution)/shard_map/ppermute | solution.py:297
  54.9 17.2 %collective-permute-start.5 = (bf16[256,768]{1,0:T(8,128)(2,1)}, bf16[256,768]{1,0:T(8,128)(2,1)S(1)}, u32[]{:S(2)}, u32[]{:S(2)}) collective-permute-start(bf16[256,768]{1,0:T(8,128)(2,1)} %get-tuple-element.31), channel_id=1, source_target_pairs={{0,1},{1,0},{2,3},{3,2},{4,5},{5,4},{6,7},{7,6},{8,9},{9,8},{10,11... | collective-permute-start | bytes 1179656 | tf_op jit(solution)/shard_map/ppermute | solution.py:310
  57.2 5.0 %copy-start.1 = (bf16[160,3072]{1,0:T(8,128)(2,1)}, bf16[160,3072]{1,0:T(8,128)(2,1)S(1)}, u32[]{:S(2)}) copy-start(bf16[160,3072]{1,0:T(8,128)(2,1)S(1)} %collective-permute-done.10.refs_2_.refs_10_) | copy-start | bytes 2949124
  62.2 10.3 %collective-permute-start.11 = (bf16[160,768]{1,0:T(8,128)(2,1)S(1)}, bf16[160,768]{1,0:T(8,128)(2,1)S(1)}, u32[]{:S(2)}, u32[]{:S(2)}) collective-permute-start(bf16[160,768]{1,0:T(8,128)(2,1)S(1)} %get-tuple-element.38), channel_id=1, source_target_pairs={{0,1},{1,0},{2,3},{3,2},{4,5},{5,4},{6,7},{7,6},{8,9},{9,8},{10,11... | collective-permute-start | bytes 737288 | tf_op jit(solution)/shard_map/ppermute | solution.py:349
  72.1 7.5 %copy-start.2 = (bf16[96,3072]{1,0:T(8,128)(2,1)}, bf16[96,3072]{1,0:T(8,128)(2,1)S(1)}, u32[]{:S(2)}) copy-start(bf16[96,3072]{1,0:T(8,128)(2,1)S(1)} %collective-permute-done.13.refs_1_.refs_9_) | copy-start | bytes 1769476
  72.4 2.6 %collective-permute-start.14 = (bf16[96,3072]{1,0:T(8,128)(2,1)S(1)}, bf16[96,3072]{1,0:T(8,128)(2,1)S(1)}, u32[]{:S(2)}, u32[]{:S(2)}) collective-permute-start(bf16[96,3072]{1,0:T(8,128)(2,1)S(1)} %collective-permute-done.13.refs_1_.refs_9_), channel_id=1, source_target_pairs={{0,4},{4,0},{8,12},{12,8},{1,5},{5,1},{9,13},{13,9},{2,6},{6,2},{1... | collective-permute-start | bytes 1769480 | tf_op jit(solution)/shard_map/ppermute | solution.py:332
  72.6 15.2 %collective-permute-start.12 = (bf16[112,768]{1,0:T(8,128)(2,1)S(1)}, bf16[112,768]{1,0:T(8,128)(2,1)S(1)}, u32[]{:S(2)}, u32[]{:S(2)}) collective-permute-start(bf16[112,768]{1,0:T(8,128)(2,1)S(1)} %slice.86), channel_id=1, source_target_pairs={{0,2},{2,0},{1,3},{3,1},{4,6},{6,4},{5,7},{7,5},{8,10},{10,8},{9,1... | collective-permute-start | bytes 516104 | tf_op jit(solution)/shard_map/ppermute | solution.py:367
  75.1 4.6 %copy-start.3 = (bf16[96,3072]{1,0:T(8,128)(2,1)}, bf16[96,3072]{1,0:T(8,128)(2,1)S(1)}, u32[]{:S(2)}) copy-start(bf16[96,3072]{1,0:T(8,128)(2,1)S(1)} %collective-permute-done.14.refs_2_.refs_11_) | copy-start | bytes 1769476
  79.6 9.1 %collective-permute-start.15 = (bf16[96,768]{1,0:T(8,128)(2,1)S(1)}, bf16[96,768]{1,0:T(8,128)(2,1)S(1)}, u32[]{:S(2)}, u32[]{:S(2)}) collective-permute-start(bf16[96,768]{1,0:T(8,128)(2,1)S(1)} %get-tuple-element.45), channel_id=1, source_target_pairs={{0,1},{1,0},{2,3},{3,2},{4,5},{5,4},{6,7},{7,6},{8,9},{9,8},{10,11... | collective-permute-start | bytes 442376 | tf_op jit(solution)/shard_map/ppermute | solution.py:349
  80.9 6.9 %collective-permute-start.16 = (bf16[48,768]{1,0:T(8,128)(2,1)S(1)}, bf16[48,768]{1,0:T(8,128)(2,1)S(1)}, u32[]{:S(2)}, u32[]{:S(2)}) collective-permute-start(bf16[48,768]{1,0:T(8,128)(2,1)S(1)} %slice.87), channel_id=1, source_target_pairs={{0,2},{2,0},{1,3},{3,1},{4,6},{6,4},{5,7},{7,5},{8,10},{10,8},{9,1... | collective-permute-start | bytes 221192 | tf_op jit(solution)/shard_map/ppermute | solution.py:367
  88.9 9.9 %collective-permute-start.17 = (bf16[96,768]{1,0:T(8,128)(2,1)S(1)}, bf16[96,768]{1,0:T(8,128)(2,1)S(1)}, u32[]{:S(2)}, u32[]{:S(2)}) collective-permute-start(bf16[96,768]{1,0:T(8,128)(2,1)S(1)} %select_convert_fusion.1.refs_13_), channel_id=1, source_target_pairs={{0,2},{2,0},{1,3},{3,1},{4,6},{6,4},{5,7},{7,5},{8,10},{10,8},{9,1... | collective-permute-start | bytes 442376 | tf_op jit(solution)/shard_map/ppermute | solution.py:367
  97.4 1.5 %copy-start.6 = (f32[256,1536]{1,0:T(8,128)S(1)}, f32[256,1536]{1,0:T(8,128)}, u32[]{:S(2)}) copy-start(f32[256,1536]{1,0:T(8,128)} %copy-done.5) | copy-start | bytes 4718596
  97.4 1.5 %copy-start.9 = (bf16[256,768]{1,0:T(8,128)(2,1)S(1)}, bf16[256,768]{1,0:T(8,128)(2,1)}, u32[]{:S(2)}) copy-start(bf16[256,768]{1,0:T(8,128)(2,1)} %param.10) | copy-start | bytes 1179652
  99.4 3.6 %collective-permute-start.19 = (f32[2,256]{1,0:T(2,128)S(1)}, f32[2,256]{1,0:T(2,128)S(1)}, u32[]{:S(2)}, u32[]{:S(2)}) collective-permute-start(f32[2,256]{1,0:T(2,128)S(1)} %pad_maximum_fusion.1), channel_id=1, source_target_pairs={{0,8},{8,0},{4,12},{12,4},{1,9},{9,1},{5,13},{13,5},{2,10},{10,2},... | collective-permute-start | bytes 6152 | tf_op jit(solution)/shard_map/ppermute | solution.py:237
  100.8 3.0 %collective-permute-start.20 = (f32[2,256]{1,0:T(2,128)S(1)}, f32[2,256]{1,0:T(2,128)S(1)}, u32[]{:S(2)}, u32[]{:S(2)}) collective-permute-start(f32[2,256]{1,0:T(2,128)S(1)} %pad_maximum_fusion.1), channel_id=1, source_target_pairs={{0,12},{12,0},{4,8},{8,4},{1,13},{13,1},{5,9},{9,5},{2,14},{14,2},... | collective-permute-start | bytes 6152 | tf_op jit(solution)/shard_map/ppermute | solution.py:238
  100.8 3.0 %collective-permute-start.18 = (f32[2,256]{1,0:T(2,128)S(1)}, f32[2,256]{1,0:T(2,128)S(1)}, u32[]{:S(2)}, u32[]{:S(2)}) collective-permute-start(f32[2,256]{1,0:T(2,128)S(1)} %pad_maximum_fusion.1), channel_id=1, source_target_pairs={{0,4},{4,0},{8,12},{12,8},{1,5},{5,1},{9,13},{13,9},{2,6},{6,2},{1... | collective-permute-start | bytes 6152 | tf_op jit(solution)/shard_map/ppermute | solution.py:236
